TPU v7x, 32 devices: a whole 2x2x4 slice. The times are simulated.
32 devices in a mesh: groups: 2 (over x), node: 4 (over y, core), local: 4 (over z).
Axes of the slice: x: 2, y: 2, z: 4, core: 2. Of those that a mesh axis runs over, the one named last changes fastest.
Arguments:
- out_grad: bfloat16 [1024, 3584], P(('groups', 'node', 'local')), parts along dimension 0, may hold values from -0.29882812 to 0.29882812
- lengths: int32 [32], P('groups'), parts along dimension 0, may hold values from 1 to 64, 512 in all
- gate_weights: bfloat16 [1024, 8], P(('groups', 'node', 'local')), parts along dimension 0, may hold values from 0.049804688 to 1
- expert_ids: int32 [1024, 8], P(('groups', 'node', 'local')), parts along dimension 0, may hold values from 0 to 7, as said below
- hidden_routed: bfloat16 [8, 992, 2048], P('node', 'groups', 'local'), parts along dimension 1, may hold values from -6 to 6
- down_routed: bfloat16 [8, 2048, 3584], P('node', 'local'), may hold values from -0.125 to 0.125
- hidden_shared: bfloat16 [1024, 2048], P(('groups', 'node'), 'local'), parts along dimension 0, may hold values from -6 to 6
- down_shared: bfloat16 [2048, 3584], P('local'), may hold values from -0.125 to 0.125
Outputs:
- d_hidden_routed: bfloat16 [8, 992, 2048], P('node', 'groups', 'local'), parts along dimension 1
- d_down_routed: bfloat16 [16, 2048, 3584], P(('groups', 'node'), 'local'), parts along dimension 0
- d_gate: float32 [1024, 8], P(('groups', 'node', 'local')), parts along dimension 0
- d_hidden_shared: bfloat16 [1024, 2048], P(('groups', 'node'), 'local'), parts along dimension 0
- d_down_shared: bfloat16 [4096, 3584], P(('groups', 'local'), 'node'), parts along dimension 0
There are 2 independent parts, one for each index of `groups`. A program takes and returns all parts, laid end to end along the dimension named above; an argument that names none is the same for every part. Nothing has to cross between parts.
Inputs may be any that keep to these rules, and one draw needn't show every extreme that they name: `expert_ids`: each token names 8 different experts; expert e belongs to node group floor(e / 2), and one token's experts lie in at most 4 node groups.
All inputs are finite; a program needn't handle non-finite values.
Results may differ from a plain program's by a relative error of at most 0.012.
Values may be sent and summed in bfloat16 or wider, within the bound.
No kernel may reach another device: no remote copies, remote signals or barrier semaphores. Data moves between devices by JAX's collectives and lax.ppermute only.
A program may use at most 128 MiB of HBM per device.

v0:
```python
import jax
import jax.numpy as jnp
from jax import lax
from jax.sharding import PartitionSpec as P

MEAN_LENGTH = 32.0


def token_weights(lengths, first, count):
    end_marks = jnp.cumsum(lengths)
    starts = end_marks - lengths
    places = first + jnp.arange(count, dtype=jnp.int32)
    inside = (places[:, None] >= starts[None, :]) & (places[:, None] < end_marks[None, :])
    own_length = jnp.sum(jnp.where(inside, lengths[None, :], 0), axis=1)
    return MEAN_LENGTH / own_length.astype(jnp.float32)


def body(
    out_grad,
    lengths,
    gate_weights,
    expert_ids,
    hidden_routed,
    down_routed,
    hidden_shared,
    down_shared,
):
    node_count = lax.axis_size("node")
    local_count = lax.axis_size("local")
    device_count = node_count * local_count
    token_count = out_grad.shape[0]
    feature_count = out_grad.shape[1]
    experts_here = down_routed.shape[0]
    slot_total = hidden_routed.shape[1]
    capacity = slot_total // device_count
    expert_total = experts_here * node_count
    position = lax.axis_index(("node", "local"))
    weight = token_weights(lengths, position * token_count, token_count)
    grad_rows = (out_grad.astype(jnp.float32) * weight[:, None]).astype(jnp.bfloat16)
    hit_count = jnp.sum(
        (expert_ids[:, :, None] == jnp.arange(expert_total, dtype=jnp.int32)[None, None, :]).astype(
            jnp.int32
        ),
        axis=1,
    )
    before = jnp.cumsum(hit_count, axis=0) - hit_count
    rank_value = jnp.take_along_axis(before, expert_ids, axis=1)
    slots = jnp.where(rank_value < capacity, rank_value, -1)
    live_mask = slots >= 0
    target = (
        expert_ids % experts_here * (node_count * capacity)
        + expert_ids // experts_here * capacity
        + slots
    )
    target = jnp.where(live_mask, target, -1)
    cell_numbers = jnp.arange(experts_here * node_count * capacity, dtype=jnp.int32)
    matches = target[None, :, :] == cell_numbers[:, None, None]
    placing = jnp.any(matches, axis=2).astype(jnp.bfloat16)
    send_rows = jnp.dot(placing, grad_rows, preferred_element_type=jnp.float32).astype(jnp.bfloat16)
    send_rows = send_rows.reshape(experts_here, node_count, capacity, feature_count)
    send_gates = jnp.sum(
        jnp.where(matches, gate_weights.astype(jnp.float32)[None, :, :], 0.0), axis=(1, 2)
    )
    send_gates = send_gates.astype(jnp.bfloat16).reshape(experts_here, node_count, capacity)
    wide_rows = jnp.broadcast_to(
        send_rows[:, :, None], (experts_here, node_count, local_count, capacity, feature_count)
    )
    wide_rows = wide_rows.reshape(experts_here, device_count, capacity, feature_count)
    wide_gates = jnp.broadcast_to(
        send_gates[:, :, None], (experts_here, node_count, local_count, capacity)
    )
    wide_gates = wide_gates.reshape(experts_here, device_count, capacity)
    got_rows, got_gates = (
        lax.all_to_all(wide_rows, ("node", "local"), split_axis=1, concat_axis=1, tiled=True),
        lax.all_to_all(wide_gates, ("node", "local"), split_axis=1, concat_axis=1, tiled=True),
    )
    slot_rows = got_rows.reshape(experts_here, slot_total, feature_count)
    slot_gates = got_gates.reshape(experts_here, slot_total)
    back_grad = jnp.einsum(
        "esd,efd->esf", slot_rows, down_routed, preferred_element_type=jnp.float32
    )
    scaled = slot_rows * slot_gates[:, :, None]
    grad_down = jnp.einsum(
        "esf,esd->efd", hidden_routed, scaled, preferred_element_type=jnp.float32
    )
    d_hidden_routed = (slot_gates.astype(jnp.float32)[:, :, None] * back_grad).astype(jnp.bfloat16)
    d_down_routed = grad_down.astype(jnp.bfloat16)
    slot_grad = jnp.sum(hidden_routed.astype(jnp.float32) * back_grad, axis=2)
    grad_split = slot_grad.reshape(experts_here, node_count, local_count, capacity)
    summed = lax.psum(grad_split, "local")
    own_share = lax.dynamic_index_in_dim(summed, lax.axis_index("local"), 2, keepdims=False)
    returned = lax.all_to_all(own_share, "node", split_axis=1, concat_axis=1, tiled=True)
    flat_grad = returned.reshape(-1)
    d_gate = jnp.sum(jnp.where(matches, flat_grad[:, None, None], 0.0), axis=0)
    shard_piece = lax.all_gather(grad_rows, "local", axis=0, tiled=True)
    part_back = lax.dot_general(
        shard_piece, down_shared, (((1,), (1,)), ((), ())), preferred_element_type=jnp.float32
    )
    grad_now = lax.dot_general(
        hidden_shared, shard_piece, (((0,), (0,)), ((), ())), preferred_element_type=jnp.float32
    )
    d_hidden_shared = part_back.astype(jnp.bfloat16)
    column_count = feature_count // node_count
    whole_sum = lax.psum(grad_now.astype(jnp.bfloat16), "node").astype(jnp.float32)
    own_columns = lax.dynamic_slice_in_dim(
        whole_sum, lax.axis_index("node") * column_count, column_count, 1
    )
    d_down_shared = own_columns.astype(jnp.bfloat16)
    return (d_hidden_routed, d_down_routed, d_gate, d_hidden_shared, d_down_shared)


def solution(mesh):
    placed = (
        P(("groups", "node", "local"), None),
        P("groups"),
        P(("groups", "node", "local"), None),
        P(("groups", "node", "local"), None),
        P("node", "groups", "local"),
        P("node", "local", None),
        P(("groups", "node"), "local"),
        P("local", None),
    )
    return jax.shard_map(
        body,
        mesh=mesh,
        in_specs=placed,
        out_specs=(
            P("node", "groups", "local"),
            P(("groups", "node"), "local", None),
            P(("groups", "node", "local"), None),
            P(("groups", "node"), "local"),
            P(("groups", "local"), "node"),
        ),
        check_vma=False,
    )
```

profile of v0, /device:TPU:0, one launch (start us, length us, event | category | flops | bytes accessed | tf_op | source)
XLA Modules:
  0.0 312.7 jit_solution(4696342127378677703)
XLA Ops:
  7.2 0.0 copy-start
  7.2 0.8 copy.76
  8.0 0.7 convert_reduce_fusion
  8.7 0.1 copy.79
  8.8 0.1 reduce_window_sum.18
  8.8 0.1 reshape.92
  8.9 0.0 copy-start.3
  8.9 0.0 copy-start.1
  8.9 1.9 gather_fusion
  10.9 0.1 reshape.95
  11.0 0.2 fusion.9
  11.2 0.0 copy-done.3
  11.2 0.1 copy.87
  11.3 0.1 reduce
  11.5 0.1 select_reduce_fusion.2
  11.6 0.0 copy-done.1
  11.6 0.1 multiply_convert_fusion.1
  11.7 1.9 convolution_convert_fusion.2
  13.6 2.0 broadcast_in_dim.76
  15.6 1.9 copy.88
  17.5 4.9 %broadcast_in_dim.77 = bf16[2,4,4,31,3584]{4,0,3,2,1:T(2,128)(2,1)} broadcast(bf16[2,4,31,3584]{3,0,2,1:T(2,128)(2,1)S(1)} %copy.88), dimensions={0,1,3,4} | broadcast | bytes 8888320 | tf_op jit(solution)/shard_map/broadcast_in_dim | solution.py:65
  22.3 7.4 %all-to-all-start.1 = ((bf16[2,16,31,3584]{3,0,2,1:T(2,128)(2,1)}), bf16[2,16,31,3584]{3,0,2,1:T(2,128)(2,1)}, u32[]{:S(2)}, u32[]{:S(2)}) async-start(bf16[2,16,31,3584]{3,0,2,1:T(2,128)(2,1)} %bitcast.21), calls=%async_computation.1 | async-start | bytes 14221312 | tf_op jit(solution)/shard_map/all_to_all | solution.py:74
  29.8 0.0 all-reduce.2.cloned.1.call-start
  29.8 170.9 %all_gather.3 = bf16[128,3584]{1,0:T(8,128)(2,1)S(1)} all-gather(bf16[32,3584]{1,0:T(8,128)(2,1)S(1)} %multiply_convert_fusion.1), channel_id=1, replica_groups=mesh['groups'=2,'node'=4,'local'=4] {'local'}, dimensions={0}, use_global_device_ids=true | all-gather | bytes 1146880 | tf_op jit(solution)/shard_map/all_gather | solution.py:95
  200.8 0.0 copy-done
  200.8 3.0 fusion.7
  203.7 0.0 all-reduce.2.cloned.1.call-update
  203.8 0.0 all-to-all-done.1
  203.8 0.0 copy-start.2
  203.8 9.3 %multiply_reduce_fusion = (f32[2,496]{1,0:T(2,128)S(1)}, f32[2,496,512]{2,1,0:T(8,128)S(1)}) fusion(bf16[2,496,512]{2,1,0:T(8,128)(2,1)} %param.12, bf16[2,512,3584]{2,1,0:T(8,128)(2,1)} %param.13, bf16[2,496,3584]{2,0,1:T(2,128)(2,1)} %bitcast.4), kind=kOutput, calls=%fused_computation.11 | convolution fusion | flops 3642178560 | bytes 17502080 | tf_op jit(solution)/shard_map/esd,efd->esf/dot_general | solution.py:79
  213.1 0.1 reshape.91
  213.2 18.5 %psum.14 = f32[2,4,4,31]{3,2,1,0:T(4,128)S(1)} all-reduce(f32[2,4,4,31]{3,2,1,0:T(4,128)S(1)} %reshape.91), channel_id=1, replica_groups=mesh['groups'=2,'node'=4,'local'=4] {'local'}, use_global_device_ids=true, to_apply=%region_7.8 | all-reduce | flops 992 | bytes 7936 | tf_op jit(solution)/shard_map/psum | solution.py:90
  231.7 0.6 copy.90
  232.3 3.2 %all-to-all-start.2 = ((f32[2,4,31]{2,0,1:T(2,128)}), f32[2,4,31]{2,0,1:T(2,128)S(1)}, u32[]{:S(2)}, u32[]{:S(2)}) async-start(f32[2,4,31]{2,0,1:T(2,128)} %copy.90), calls=%async_computation.2 | async-start | bytes 8192 | tf_op jit(solution)/shard_map/all_to_all | solution.py:92
  235.6 4.0 %convolution_convert_fusion.3 = bf16[128,512]{1,0:T(8,128)(2,1)} fusion(bf16[128,3584]{1,0:T(8,128)(2,1)S(1)} %all_gather.3, bf16[512,3584]{1,0:T(8,128)(2,1)} %param.15), kind=kOutput, calls=%fused_computation.14 | convolution fusion | flops 469827584 | bytes 4718592 | tf_op jit(solution)/shard_map/dot_general | solution.py:96
  239.6 0.0 copy-done.2
  239.6 0.1 copy.84
  239.7 0.0 all-to-all-done.2
  239.7 0.1 broadcast_in_dim.78
  239.8 0.2 select_reduce_fusion
  240.0 0.1 convert_element_type.70
  240.1 0.6 broadcast_in_dim.73
  240.7 3.7 %all-to-all-start = ((bf16[2,16,31]{2,0,1:T(2,128)(2,1)}), bf16[2,16,31]{2,0,1:T(2,128)(2,1)S(1)}, u32[]{:S(2)}, u32[]{:S(2)}) async-start(bf16[2,16,31]{2,0,1:T(2,128)(2,1)} %bitcast.1), calls=%async_computation | async-start | bytes 16384 | tf_op jit(solution)/shard_map/all_to_all | solution.py:75
  244.4 36.4 %all-reduce.2.cloned.1.call-done = bf16[512,3584]{0,1:T(8,128)(2,1)} async-done(((bf16[512,3584]{0,1:T(8,128)(2,1)}), bf16[512,3584]{0,1:T(8,128)(2,1)}) %all-reduce.2.cloned.1.call-update) | async-done | bytes 3670032 | tf_op jit(solution)/shard_map/psum | solution.py:104
  280.8 1.2 convert_convert_fusion
  282.0 1.3 copy.94
  283.3 0.7 copy.93
  284.0 0.0 all-to-all-done
  284.0 0.1 reshape.86
  284.1 10.7 %fusion.1 = bf16[2,512,3584]{1,2,0:T(8,128)(2,1)} fusion(bf16[2,496,512]{2,1,0:T(8,128)(2,1)} %param.12, bf16[2,496,3584]{2,0,1:T(2,128)(2,1)} %bitcast.4, bf16[2,496]{1,0:T(2,128)(2,1)S(1)} %reshape.86), kind=kOutput, calls=%fused_computation.3 | convolution fusion | flops 3647881216 | bytes 15468480 | tf_op jit(solution)/shard_map/esf,esd->efd/dot_general | solution.py:83
  294.8 9.9 %copy.92 = bf16[2,512,3584]{2,1,0:T(8,128)(2,1)} copy(bf16[2,512,3584]{1,2,0:T(8,128)(2,1)} %fusion.1) | data formatting | bytes 14680064
  304.7 1.2 multiply_convert_fusion
  (12 shorter events, 0.1 us)
Async XLA Ops:
  7.2 193.6 %copy-start = (bf16[128,512]{1,0:T(8,128)(2,1)S(1)}, bf16[128,512]{1,0:T(8,128)(2,1)}, u32[]{:S(2)}) copy-start(bf16[128,512]{1,0:T(8,128)(2,1)} %param.14) | copy-start | bytes 393220
  8.9 2.3 copy-start.3
  8.9 2.6 copy-start.1
  22.3 181.4 %all-to-all-start.1 = ((bf16[2,16,31,3584]{3,0,2,1:T(2,128)(2,1)}), bf16[2,16,31,3584]{3,0,2,1:T(2,128)(2,1)}, u32[]{:S(2)}, u32[]{:S(2)}) async-start(bf16[2,16,31,3584]{3,0,2,1:T(2,128)(2,1)} %bitcast.21), calls=%async_computation.1 | async-start | bytes 14221312 | tf_op jit(solution)/shard_map/all_to_all | solution.py:74
  29.8 251.0 %all-reduce.2.cloned.1.call-start = ((), (), s32[]{:S(2)}) async-start(), calls=%async_computation.3 | async-start | bytes 7340032 | tf_op jit(solution)/shard_map/psum | solution.py:104
  203.8 35.9 %copy-start.2 = (bf16[32,8]{0,1:T(8,128)(2,1)S(1)}, bf16[32,8]{0,1:T(8,128)(2,1)}, u32[]{:S(2)}) copy-start(bf16[32,8]{0,1:T(8,128)(2,1)} %param.10) | copy-start | bytes 1540
  232.3 7.4 %all-to-all-start.2 = ((f32[2,4,31]{2,0,1:T(2,128)}), f32[2,4,31]{2,0,1:T(2,128)S(1)}, u32[]{:S(2)}, u32[]{:S(2)}) async-start(f32[2,4,31]{2,0,1:T(2,128)} %copy.90), calls=%async_computation.2 | async-start | bytes 8192 | tf_op jit(solution)/shard_map/all_to_all | solution.py:92
  240.7 43.2 %all-to-all-start = ((bf16[2,16,31]{2,0,1:T(2,128)(2,1)}), bf16[2,16,31]{2,0,1:T(2,128)(2,1)S(1)}, u32[]{:S(2)}, u32[]{:S(2)}) async-start(bf16[2,16,31]{2,0,1:T(2,128)(2,1)} %bitcast.1), calls=%async_computation | async-start | bytes 16384 | tf_op jit(solution)/shard_map/all_to_all | solution.py:75
Sparse Core Ops, SparseCore 0:
  203.9 76.8 all-reduce.1
where the time goes:
time: 313 us
  blocking collectives  189 us (60%)
  waiting for transfers between devices  36.4 us (12%)
  matrix products  28.9 us (9%)
  local copies, waits for them, and re-layouts  25.4 us (8%)
  starting transfers between devices  14.4 us (5%)
  between operations  14.2 us (5%)
  other arithmetic  3.95 us (1%)
    all_gather x1, blocking collectives, body(): shard_piece = lax.all_gather(grad_rows, 'local', axis=0, tiled=True)  171 us
    psum x1, waiting for transfers between devices, body(): lax.psum(grad_now.astype(jnp.bfloat16), 'node').astype(jnp.float32)  36.4 us
    psum x1, blocking collectives, body(): summed = lax.psum(grad_split, 'local')  18.5 us
    unnamed x12, local copies, waits for them, and re-layouts  12.7 us
    dot_general x1, matrix products, body(): jnp.einsum('esf,esd->efd', hidden_routed, scaled, preferred_element_type=...  10.7 us
    dot_general x1, matrix products, body(): jnp.einsum('esd,efd->esf', slot_rows, down_routed, preferred_element_type...  9.32 us
    broadcast_in_dim x3, local copies, waits for them, and re-layouts, body(): jnp.broadcast_to(send_rows[:, :, None], (experts_here, node_count, local_...  8.77 us
    all_to_all x1, starting transfers between devices, body(): lax.all_to_all(wide_rows, ('node', 'local'), split_axis=1, concat_axis=1,...  7.43 us
  transfers between devices with their start and end apart: 4, of which 1 were waited for; matrix products, arithmetic and copies ran while one was open for 7% of the time, Pallas kernels for 0%

commit v1 on v0

v1 whole, which is shorter than its diff:
```python
import jax
import jax.numpy as jnp
from jax import lax
from jax.sharding import PartitionSpec as P

MEAN_LENGTH = 32.0
AXES = ("node", "local")
F32 = jnp.float32
BF16 = jnp.bfloat16


def dot(a, b, ca, cb):
    return lax.dot_general(a, b, (((ca,), (cb,)), ((), ())), preferred_element_type=F32)


def ring_places(node_count, local_count):
    chips = []
    for y in range(node_count // 2):
        row = range(local_count) if y % 2 == 0 else range(local_count - 1, -1, -1)
        chips += [(y, z) for z in row]
    return chips


def gather_ring(block, node_count, local_count, split):
    chips = ring_places(node_count, local_count)
    total = len(chips)

    def flat(chip, core):
        return (chip[0] * 2 + core) * local_count + chip[1]

    def shift(step):
        return [
            (flat(chips[r], c), flat(chips[(r + step) % total], c))
            for r in range(total)
            for c in (0, 1)
        ]

    swap = [(flat(chip, c), flat(chip, 1 - c)) for chip in chips for c in (0, 1)]
    up, down = shift(1), shift(-1)
    held = [(0, block)]
    forth = back = block
    for step in range(1, (total - 1) // 2 + 1):
        forth = lax.ppermute(forth, AXES, up)
        back = lax.ppermute(back, AXES, down)
        held += [(-step, forth), (step, back)]
    left = lax.ppermute(forth[:, :split], AXES, up)
    right = lax.ppermute(back[:, split:], AXES, down)
    held.append((total // 2, jnp.concatenate([left, right], axis=1)))
    node, local = lax.axis_index("node"), lax.axis_index("local")
    y, core = node // 2, node % 2
    mine = y * local_count + jnp.where(y % 2 == 0, local, local_count - 1 - local)
    blocks, offsets, cores = [], [], []
    for offset, piece in held:
        blocks += [piece, lax.ppermute(piece, AXES, swap)]
        offsets += [offset, offset]
        cores += [0, 1]
    at = (mine + jnp.array(offsets, jnp.int32) + total) % total
    at_y = at // local_count
    at_z = jnp.where(at_y % 2 == 0, at % local_count, local_count - 1 - at % local_count)
    order = (at_y * 2 + (core + jnp.array(cores, jnp.int32)) % 2) * local_count + at_z
    return blocks, order


def gather_nodes(block):
    node_count = lax.axis_size("node")
    if node_count != 4:
        return lax.all_gather(block, "node", axis=0)
    node = lax.axis_index("node")
    core_swap = [(n, n ^ 1) for n in range(4)]
    chip_swap = [(n, n ^ 2) for n in range(4)]
    across = lax.ppermute(block, "node", chip_swap)
    found = [block, lax.ppermute(block, "node", core_swap), across, lax.ppermute(across, "node", core_swap)]
    stacked = jnp.stack(found)
    return stacked[jnp.arange(4) ^ node]


def body(
    out_grad,
    lengths,
    gate_weights,
    expert_ids,
    hidden_routed,
    down_routed,
    hidden_shared,
    down_shared,
):
    node_count = lax.axis_size("node")
    local_count = lax.axis_size("local")
    device_count = node_count * local_count
    here, features = out_grad.shape
    choices = expert_ids.shape[1]
    experts, slot_total, units = hidden_routed.shape
    capacity = slot_total // device_count
    node, local = lax.axis_index("node"), lax.axis_index("local")

    pad = jnp.zeros((here, 128 - 2 * choices), BF16)
    packed = jnp.concatenate([out_grad, gate_weights, expert_ids.astype(BF16), pad], axis=1)
    if device_count <= 16:
        split = features // 2 // 128 * 128
        blocks, order = gather_ring(packed, node_count, local_count, split)
        rows = jnp.concatenate(blocks, axis=0)
    else:
        rows = lax.all_gather(packed, AXES, axis=0, tiled=True)
        order = jnp.arange(device_count, dtype=jnp.int32)
    token_total = device_count * here
    counted = jnp.arange(device_count, dtype=jnp.int32)
    place = jnp.sum(jnp.where(order[None, :] == counted[:, None], counted[None, :], 0), axis=1)

    ends = jnp.cumsum(lengths)
    places = (order[:, None] * here + jnp.arange(here, dtype=jnp.int32)[None, :]).reshape(-1)
    inside = (places[:, None] >= (ends - lengths)[None, :]) & (places[:, None] < ends[None, :])
    weight = MEAN_LENGTH / jnp.sum(jnp.where(inside, lengths[None, :], 0), axis=1).astype(F32)

    x = rows[:, :features]
    gates = rows[:, features : features + choices].astype(F32)
    ids = rows[:, features + choices : features + 2 * choices].astype(jnp.int32)
    first = node * experts
    d_hidden, d_down, sums = [], [], []
    for e in range(experts):
        named = ids == first + e
        hit = jnp.any(named, axis=1)
        gate = jnp.sum(jnp.where(named, gates, 0.0), axis=1)
        hits = hit.astype(jnp.int32).reshape(device_count, here)
        rank = (jnp.cumsum(hits, axis=1) - hits).reshape(-1)
        cell = jnp.repeat(order, here) * capacity + rank
        cell = jnp.where(hit & (rank < capacity), cell, -1)
        placing = jnp.arange(slot_total, dtype=jnp.int32)[:, None] == cell[None, :]
        placing = placing.astype(BF16)
        hidden = dot(hidden_routed[e], placing, 0, 0)
        back = dot(down_routed[e], x, 1, 1) * weight[None, :]
        sums.append(jnp.sum(hidden * back, axis=0))
        gated = placing * gate.astype(BF16)[None, :]
        d_hidden.append(dot(gated, back.astype(BF16), 1, 1).astype(BF16))
        scaled = (hidden * (gate * weight)[None, :]).astype(BF16)
        d_down.append(dot(scaled, x, 1, 0).astype(BF16))
    d_hidden_routed = jnp.stack(d_hidden)
    d_down_routed = jnp.stack(d_down)

    slot_grad = jnp.stack(sums).reshape(experts, device_count, here)[:, place]
    slot_grad = slot_grad.reshape(experts, node_count, local_count, here)

    def turn(count, step):
        return [(i, (i + step) % count) for i in range(count)]

    def own(a):
        return lax.dynamic_index_in_dim(a, local, 2, keepdims=False)

    total = own(slot_grad)
    for step in range(1, local_count):
        total = total + own(lax.ppermute(slot_grad, "local", turn(local_count, step)))
    d_gate = jnp.zeros(expert_ids.shape, F32)
    for step in range(node_count):
        got = total if step == 0 else lax.ppermute(total, "node", turn(node_count, step))
        got = lax.dynamic_index_in_dim(got, node, 1, keepdims=False)
        start = (node + node_count - step) % node_count * experts
        for e in range(experts):
            d_gate = d_gate + jnp.where(expert_ids == start + e, got[e][:, None], 0.0)

    blocked = x.reshape(device_count, here, features)
    near = lax.dynamic_slice_in_dim(place, node * local_count, local_count, 0)
    near_weight = weight.reshape(device_count, here)[near].reshape(-1)
    shared_back = dot(blocked[near].reshape(-1, features), down_shared, 1, 1)
    d_hidden_shared = (shared_back * near_weight[:, None]).astype(BF16)
    columns = features // node_count
    mine = lax.dynamic_slice_in_dim(x, node * columns, columns, 1)
    shared = gather_nodes(hidden_shared).reshape(device_count, here, -1)[order]
    shared = (shared.reshape(token_total, -1).astype(F32) * weight[:, None]).astype(BF16)
    d_down_shared = dot(shared, mine, 0, 0).astype(BF16)
    return (d_hidden_routed, d_down_routed, d_gate, d_hidden_shared, d_down_shared)


def solution(mesh):
    placed = (
        P(("groups", "node", "local"), None),
        P("groups"),
        P(("groups", "node", "local"), None),
        P(("groups", "node", "local"), None),
        P("node", "groups", "local"),
        P("node", "local", None),
        P(("groups", "node"), "local"),
        P("local", None),
    )
    return jax.shard_map(
        body,
        mesh=mesh,
        in_specs=placed,
        out_specs=(
            P("node", "groups", "local"),
            P(("groups", "node"), "local", None),
            P(("groups", "node", "local"), None),
            P(("groups", "node"), "local"),
            P(("groups", "local"), "node"),
        ),
        check_vma=False,
    )
```

time: 313 us -> 96.6 us (0.31)
  blocking collectives: 189 us -> 0 us
  waiting for transfers between devices: 36.4 us -> 8.57 us
  between operations: 14.2 us -> 0.96 us
  other arithmetic: 3.95 us -> 14 us
  starting transfers between devices: 14.4 us -> 19.1 us
    all_gather x1 -> x0, blocking collectives: 171 us -> none  [body(): shard_piece = lax.all_gather(grad_rows, 'local', axis=0, tiled=True)]
    psum x1 -> x0, waiting for transfers between devices: 36.4 us -> none  [body(): lax.psum(grad_now.astype(jnp.bfloat16), 'node').astype(jnp.float32)]
    ppermute x0 -> x25, starting transfers between devices: none -> 19.1 us  [the longest x3 5.41 us: gather_ring(): forth = lax.ppermute(forth, AXES, up)]
    psum x1 -> x0, blocking collectives: 18.5 us -> none  [body(): summed = lax.psum(grad_split, 'local')]
    all_to_all x3 -> x0, starting transfers between devices: 14.3 us -> none  [the longest x1 7.43 us: body(): lax.all_to_all(wide_rows, ('node', 'local'), split_axis=1, concat_axis=1,...]
    broadcast_in_dim x5 -> x6, local copies, waits for them, and re-layouts: 9.47 us -> 0.1 us  [the longest x1 0.07 us: body(): cell = jnp.repeat(order, here) * capacity + rank]
    ppermute x0 -> x25, waiting for transfers between devices: none -> 8.57 us  [the longest x3 3.72 us: gather_ring(): back = lax.ppermute(back, AXES, down)]
    another operation x3 -> x8, other arithmetic: 0.21 us -> 6.25 us  [the longest x1 3.68 us: body(): d_down_routed = jnp.stack(d_down)]
  transfers between devices with their start and end apart: 4 -> 25, of which waited for: 1 -> 8; matrix products, arithmetic and copies ran while one was open for 7% -> 48% of each run, Pallas kernels for 0% -> 0%
where the time goes in v1:
time: 96.6 us; the launch traced here: 96 us
  matrix products  28.5 us (30%)
  local copies, waits for them, and re-layouts  24.9 us (26%)
  starting transfers between devices  19.1 us (20%)
  other arithmetic  14 us (14%)
  waiting for transfers between devices  8.57 us (9%)
    dot_general x10, matrix products, dot(): lax.dot_general(a, b, (((ca,), (cb,)), ((), ())), preferred_element_type=...  28.5 us
    unnamed x31, local copies, waits for them, and re-layouts  12 us
    ppermute x3, starting transfers between devices, gather_ring(): forth = lax.ppermute(forth, AXES, up)  5.41 us
    ppermute x3, starting transfers between devices, body(): lax.ppermute(slot_grad, 'local', turn(local_count, step))  4.66 us
    slice x1, local copies, waits for them, and re-layouts, body(): x = rows[:, :features]  4.07 us
    ppermute x3, waiting for transfers between devices, gather_ring(): back = lax.ppermute(back, AXES, down)  3.72 us
    another operation x1, other arithmetic, body(): d_down_routed = jnp.stack(d_down)  3.68 us
    ppermute x1, starting transfers between devices, gather_nodes(): across = lax.ppermute(block, 'node', chip_swap)  3.03 us
  transfers between devices with their start and end apart: 25, of which 8 were waited for; matrix products, arithmetic and copies ran while one was open for 48% of the time, Pallas kernels for 0%

profile of v1, /device:TPU:0, one launch (start us, length us, event | category | flops | bytes accessed | tf_op | source)
XLA Modules:
  0.0 96.0 jit_solution(11800561284174341666)
XLA Ops:
  0.6 3.0 %collective-permute-start.23 = (bf16[128,512]{1,0:T(8,128)(2,1)}, bf16[128,512]{1,0:T(8,128)(2,1)S(1)}, u32[]{:S(2)}, u32[]{:S(2)}) collective-permute-start(bf16[128,512]{1,0:T(8,128)(2,1)} %param.16), channel_id=1, source_target_pairs={{0,8},{4,12},{8,0},{12,4},{1,9},{5,13},{9,1},{13,5},{2,10},{6,14},... | collective-permute-start | bytes 393224 | tf_op jit(solution)/shard_map/ppermute | solution.py:71
  3.7 0.7 convert_element_type.115
  4.4 0.8 copy.23
  5.2 1.0 %concatenate.10 = bf16[32,3712]{1,0:T(8,128)(2,1)S(1)} concatenate(bf16[32,3584]{1,0:T(8,128)(2,1)} %param.10, bf16[32,8]{1,0:T(8,128)(2,1)S(1)} %copy.23, bf16[32,8]{1,0:T(8,128)(2,1)S(1)} %copy.24, bf16[32,112]{1,0:T(8,128)(2,1)S(1)} %broadcast_in_dim.139), dimensions={1} | concatenate | bytes 475136 | tf_op jit(solution)/shard_map/concatenate | solution.py:97
  6.4 1.9 %collective-permute-start.1 = (bf16[32,3712]{1,0:T(8,128)(2,1)S(1)}, bf16[32,3712]{1,0:T(8,128)(2,1)S(1)}, u32[]{:S(2)}, u32[]{:S(2)}) collective-permute-start(bf16[32,3712]{1,0:T(8,128)(2,1)S(1)} %concatenate.10), channel_id=1, source_target_pairs={{0,1},{4,5},{1,2},{5,6},{2,3},{6,7},{3,11},{7,15},{11,10},{15,14},... | collective-permute-start | bytes 712712 | tf_op jit(solution)/shard_map/ppermute | solution.py:43
  8.3 0.7 compare_select_fusion
  9.2 0.7 constant_dynamic-update-slice_fusion.15
  10.3 0.7 copy.25
  11.2 0.7 sub.47
  11.9 0.7 select_reduce_fusion
  12.6 0.6 collective-permute-start.24
  13.2 1.3 %collective-permute-done.3 = bf16[32,3712]{1,0:T(8,128)(2,1)S(1)} collective-permute-done((bf16[32,3712]{1,0:T(8,128)(2,1)S(1)}, bf16[32,3712]{1,0:T(8,128)(2,1)S(1)}, u32[]{:S(2)}, u32[]{:S(2)}) %collective-permute-start.3) | collective-permute-done | bytes 237600 | tf_op jit(solution)/shard_map/ppermute | solution.py:44
  14.8 1.8 %collective-permute-start.5 = (bf16[32,3712]{1,0:T(8,128)(2,1)S(1)}, bf16[32,3712]{1,0:T(8,128)(2,1)S(1)}, u32[]{:S(2)}, u32[]{:S(2)}) collective-permute-start(bf16[32,3712]{1,0:T(8,128)(2,1)S(1)} %collective-permute-done.1), channel_id=1, source_target_pairs={{0,1},{4,5},{1,2},{5,6},{2,3},{6,7},{3,11},{7,15},{11,10},{15,14},... | collective-permute-start | bytes 712712 | tf_op jit(solution)/shard_map/ppermute | solution.py:43
  16.6 0.7 constant_dynamic-update-slice_fusion.14
  17.3 0.7 constant_dynamic-update-slice_fusion.13
  18.2 1.0 %pad_maximum_fusion.2 = bf16[4,128,512]{2,1,0:T(8,128)(2,1)S(1)} fusion(bf16[1,128,512]{2,1,0:T(8,128)(2,1)S(1)} %bitcast.72, bf16[1,128,512]{2,1,0:T(8,128)(2,1)S(1)} %bitcast.70, bf16[1,128,512]{2,1,0:T(8,128)(2,1)S(1)} %bitcast.71, bf16[1,128,512]{2,1,0:T(8,128)(2,1)} %bitcast.69), kind=kLoop, calls=%fused_computation.38 | loop fusion | flops 786432 | bytes 1048576 | tf_op jit(solution)/shard_map/stack | solution.py:73
  19.2 0.6 gather_fusion.3
  19.7 0.6 gather_fusion.4
  20.8 1.1 %collective-permute-done.7 = bf16[32,3712]{1,0:T(8,128)(2,1)S(1)} collective-permute-done((bf16[32,3712]{1,0:T(8,128)(2,1)S(1)}, bf16[32,3712]{1,0:T(8,128)(2,1)S(1)}, u32[]{:S(2)}, u32[]{:S(2)}) %collective-permute-start.7) | collective-permute-done | bytes 237600 | tf_op jit(solution)/shard_map/ppermute | solution.py:44
  22.3 0.7 collective-permute-done.5
  23.0 1.7 %collective-permute-start.9 = (bf16[32,3712]{1,0:T(8,128)(2,1)S(1)}, bf16[32,3712]{1,0:T(8,128)(2,1)S(1)}, u32[]{:S(2)}, u32[]{:S(2)}) collective-permute-start(bf16[32,3712]{1,0:T(8,128)(2,1)S(1)} %collective-permute-done.5), channel_id=1, source_target_pairs={{0,1},{4,5},{1,2},{5,6},{2,3},{6,7},{3,11},{7,15},{11,10},{15,14},... | collective-permute-start | bytes 712712 | tf_op jit(solution)/shard_map/ppermute | solution.py:43
  24.7 0.7 constant_dynamic-update-slice_fusion.12
  25.4 0.7 constant_dynamic-update-slice_fusion.11
  26.1 0.7 constant_dynamic-update-slice_fusion.10
  26.9 0.7 constant_dynamic-update-slice_fusion.9
  27.6 1.4 %collective-permute-done.11 = bf16[32,3712]{1,0:T(8,128)(2,1)S(1)} collective-permute-done((bf16[32,3712]{1,0:T(8,128)(2,1)S(1)}, bf16[32,3712]{1,0:T(8,128)(2,1)S(1)}, u32[]{:S(2)}, u32[]{:S(2)}) %collective-permute-start.11) | collective-permute-done | bytes 237600 | tf_op jit(solution)/shard_map/ppermute | solution.py:44
  29.3 1.2 %collective-permute-done.9 = bf16[32,3712]{1,0:T(8,128)(2,1)S(1)} collective-permute-done((bf16[32,3712]{1,0:T(8,128)(2,1)S(1)}, bf16[32,3712]{1,0:T(8,128)(2,1)S(1)}, u32[]{:S(2)}, u32[]{:S(2)}) %collective-permute-start.9) | collective-permute-done | bytes 237600 | tf_op jit(solution)/shard_map/ppermute | solution.py:43
  30.5 1.7 %collective-permute-start.13 = (bf16[32,1792]{1,0:T(8,128)(2,1)S(1)}, bf16[32,1792]{1,0:T(8,128)(2,1)S(1)}, u32[]{:S(2)}, u32[]{:S(2)}) collective-permute-start(bf16[32,1792]{1,0:T(8,128)(2,1)S(1)} %slice.88), channel_id=1, source_target_pairs={{0,1},{4,5},{1,2},{5,6},{2,3},{6,7},{3,11},{7,15},{11,10},{15,14},... | collective-permute-start | bytes 344072 | tf_op jit(solution)/shard_map/ppermute | solution.py:46
  32.7 0.7 constant_dynamic-update-slice_fusion.8
  33.4 0.7 constant_dynamic-update-slice_fusion.7
  34.1 0.7 constant_dynamic-update-slice_fusion.6
  34.8 0.7 constant_dynamic-update-slice_fusion.5
  35.7 0.7 constant_dynamic-update-slice_fusion.4
  36.4 0.7 constant_dynamic-update-slice_fusion.3
  37.1 0.7 constant_dynamic-update-slice_fusion.2
  37.8 0.7 constant_dynamic-update-slice_fusion.1
  38.4 0.7 constant_dynamic-update-slice_fusion.16
  39.1 0.7 constant_dynamic-update-slice_fusion
  39.8 1.2 %fusion.43 = (pred[512]{0:T(512)(128)(4,1)S(1)}, pred[512]{0:T(512)(128)(4,1)S(1)}) fusion(s32[]{:T(128)S(6)} %mul.137, bf16[512,3712]{1,0:T(8,128)(2,1)} %constant_dynamic-update-slice_fusion, s32[]{:T(128)S(6)} %add.228), kind=kLoop, calls=%fused_computation.86 | loop fusion | flops 19456 | bytes 9224 | tf_op jit(solution)/shard_map/reduce_or | solution.py:121
  41.0 1.3 %fusion.37 = (f32[512]{0:T(512)S(1)}, f32[512]{0:T(512)S(1)}) fusion(bf16[512,3712]{1,0:T(8,128)(2,1)} %constant_dynamic-update-slice_fusion, s32[]{:T(128)S(6)} %mul.137, s32[]{:T(128)S(6)} %add.228), kind=kLoop, calls=%fused_computation.57 | loop fusion | flops 31744 | bytes 20488 | tf_op jit(solution)/shard_map/reduce_sum | solution.py:122
  42.3 0.6 fusion.65
  43.0 5.4 %fusion.11 = f32[512,512]{0,1:T(8,128)S(1)} fusion(bf16[2,512,3584]{2,1,0:T(8,128)(2,1)} %param.15, f32[512]{0:T(512)S(1)} %get-tuple-element.22, bf16[512,3712]{1,0:T(8,128)(2,1)} %constant_dynamic-update-slice_fusion), kind=kOutput, calls=%fused_computation.18 | convolution fusion | flops 1879310336 | bytes 8390656 | tf_op jit(solution)/shard_map/dot_general | solution.py:13
  48.4 4.1 %fusion.8 = f32[512,512]{0,1:T(8,128)S(1)} fusion(bf16[2,512,3584]{2,1,0:T(8,128)(2,1)} %param.15, f32[512]{0:T(512)S(1)} %get-tuple-element.22, bf16[512,3712]{1,0:T(8,128)(2,1)S(1)} %copy-done), kind=kOutput, calls=%fused_computation.17 | convolution fusion | flops 1879310336 | bytes 8390656 | tf_op jit(solution)/shard_map/dot_general | solution.py:13
  53.2 2.6 %multiply_reduce_fusion = (f32[512]{0:T(512)S(1)}, f32[512,512]{0,1:T(8,128)}) fusion(f32[512,512]{0,1:T(8,128)S(1)} %fusion.11, bf16[2,496,512]{2,1,0:T(8,128)(2,1)} %param.14, s32[512]{0:T(512)S(1)} %get-tuple-element.25), kind=kOutput, calls=%fused_computation.26 | convolution fusion | flops 260824576 | bytes 2609152 | tf_op jit(solution)/shard_map/dot_general | solution.py:13
  55.9 2.6 %multiply_reduce_fusion.1 = (f32[512]{0:T(512)S(1)}, f32[512,512]{0,1:T(8,128)}) fusion(f32[512,512]{0,1:T(8,128)S(1)} %fusion.8, bf16[2,496,512]{2,1,0:T(8,128)(2,1)} %param.14, s32[512]{0:T(512)S(1)} %get-tuple-element.24), kind=kOutput, calls=%fused_computation.27 | convolution fusion | flops 260824576 | bytes 2609152 | tf_op jit(solution)/shard_map/dot_general | solution.py:13
  58.6 0.6 gather_fusion
  59.2 3.6 %collective-permute-start.18 = (f32[2,4,4,32]{3,2,1,0:T(4,128)S(1)}, f32[2,4,4,32]{3,2,1,0:T(4,128)}, u32[]{:S(2)}, u32[]{:S(2)}) collective-permute-start(f32[2,4,4,32]{3,2,1,0:T(4,128)S(1)} %bitcast.74), channel_id=1, source_target_pairs={{0,3},{1,0},{2,1},{3,2},{4,7},{5,4},{6,5},{7,6},{8,11},{9,8},{10,9... | collective-permute-start | bytes 12296 | tf_op jit(solution)/shard_map/ppermute | solution.py:150
  62.8 1.0 %collective-permute-start.16 = (f32[2,4,4,32]{3,2,1,0:T(4,128)S(1)}, f32[2,4,4,32]{3,2,1,0:T(4,128)}, u32[]{:S(2)}, u32[]{:S(2)}) collective-permute-start(f32[2,4,4,32]{3,2,1,0:T(4,128)S(1)} %bitcast.76), channel_id=1, source_target_pairs={{0,1},{1,2},{2,3},{3,0},{4,5},{5,6},{6,7},{7,4},{8,9},{9,10},{10,1... | collective-permute-start | bytes 12296 | tf_op jit(solution)/shard_map/ppermute | solution.py:150
  63.8 4.1 %slice.92 = bf16[512,3584]{1,0:T(8,128)(2,1)} slice(bf16[512,3712]{1,0:T(8,128)(2,1)} %constant_dynamic-update-slice_fusion), slice={[0:512], [0:3584]} | slice | bytes 7340032 | tf_op jit(solution)/shard_map/slice | solution.py:114
  67.9 0.6 gather_fusion.2
  68.5 1.3 %fusion.15 = bf16[1,496,512]{2,1,0:T(8,128)(2,1)} fusion(f32[512,512]{0,1:T(8,128)S(1)} %fusion.11, s32[512]{0:T(512)S(1)} %get-tuple-element.25, bf16[512]{0:T(512)(128)(2,1)S(1)} %get-tuple-element.21), kind=kOutput, calls=%fused_computation.22 | convolution fusion | flops 261070848 | bytes 1559552 | tf_op jit(solution)/shard_map/dot_general | solution.py:13
  69.8 1.1 %fusion.14 = bf16[1,496,512]{2,1,0:T(8,128)(2,1)S(1)} fusion(f32[512,512]{0,1:T(8,128)S(1)} %fusion.8, s32[512]{0:T(512)S(1)} %get-tuple-element.24, bf16[512]{0:T(512)(128)(2,1)} %get-tuple-element.23), kind=kOutput, calls=%fused_computation.21 | convolution fusion | flops 261070848 | bytes 1559552 | tf_op jit(solution)/shard_map/dot_general | solution.py:13
  70.9 2.6 %gather_fusion.1 = bf16[4,32,3584]{2,1,0:T(8,128)(2,1)S(1)} fusion(bf16[16,32,3584]{2,1,0:T(8,128)(2,1)} %bitcast.66, s32[1024]{0:T(1024)S(1)} %get-tuple-element.33), kind=kCustom, calls=%fused_computation.1 | custom fusion | bytes 1835024 | tf_op jit(solution)/shard_map/gather | solution.py:162
  73.6 4.6 %fusion.1 = bf16[1,512,3584]{2,1,0:T(8,128)(2,1)S(1)} fusion(f32[512,512]{0,1:T(8,128)} %get-tuple-element.29, f32[512]{0:T(512)} %get-tuple-element.20, bf16[512,3712]{1,0:T(8,128)(2,1)} %constant_dynamic-update-slice_fusion), kind=kOutput, calls=%fused_computation.9 | convolution fusion | flops 1881407488 | bytes 8390656 | tf_op jit(solution)/shard_map/dot_general | solution.py:13
  78.3 2.1 %fusion = bf16[1,512,3584]{2,1,0:T(8,128)(2,1)S(1)} fusion(f32[512,512]{0,1:T(8,128)S(1)} %copy-done.3, f32[512]{0:T(512)S(1)} %copy-done.6, bf16[512,3712]{1,0:T(8,128)(2,1)S(1)} %copy-done.1), kind=kOutput, calls=%fused_computation.8 | convolution fusion | flops 1881407488 | bytes 8390656 | tf_op jit(solution)/shard_map/dot_general | solution.py:13
  80.4 2.8 %convolution_convert_fusion.2 = bf16[512,896]{1,0:T(8,128)(2,1)} fusion(bf16[512,3584]{1,0:T(8,128)(2,1)} %slice.92, s32[]{:T(128)S(6)} %select_n.199, f32[512,512]{0,1:T(8,128)S(1)} %copy.27, f32[512]{0:T(512)S(1)} %get-tuple-element.22), kind=kOutput, calls=%fused_computation.16 | convolution fusion | flops 470745088 | bytes 2885636 | tf_op jit(solution)/shard_map/dot_general | solution.py:13
  83.2 3.7 %pad_maximum_fusion = bf16[2,512,3584]{2,1,0:T(8,128)(2,1)} fusion(bf16[1,512,3584]{2,1,0:T(8,128)(2,1)S(1)} %fusion.1, bf16[1,512,3584]{2,1,0:T(8,128)(2,1)S(1)} %fusion), kind=kLoop, calls=%fused_computation.5 | loop fusion | flops 3670016 | bytes 14680064 | tf_op jit(solution)/shard_map/stack | solution.py:137
  86.9 2.0 %fusion.16 = bf16[128,512]{1,0:T(8,128)(2,1)} fusion(bf16[128,3584]{1,0:T(8,128)(2,1)S(1)} %bitcast.67, bf16[512,3584]{1,0:T(8,128)(2,1)S(1)} %copy-done.2, f32[128]{0:T(128)S(1)} %mul.164), kind=kOutput, calls=%fused_computation.24 | convolution fusion | flops 469893120 | bytes 4719104 | tf_op jit(solution)/shard_map/dot_general | solution.py:13
  88.8 1.0 %pad_maximum_fusion.1 = bf16[2,496,512]{2,1,0:T(8,128)(2,1)} fusion(bf16[1,496,512]{2,1,0:T(8,128)(2,1)S(1)} %copy-done.4, bf16[1,496,512]{2,1,0:T(8,128)(2,1)S(1)} %fusion.14), kind=kLoop, calls=%fused_computation.30 | loop fusion | flops 507904 | bytes 2031616 | tf_op jit(solution)/shard_map/stack | solution.py:136
  89.9 0.8 dynamic-slice_add_fusion
  90.7 0.8 collective-permute-start.21
  91.5 0.8 collective-permute-start.20
  92.8 2.3 %collective-permute-done.20 = f32[2,4,32]{2,1,0:T(4,128)S(1)} collective-permute-done((f32[2,4,32]{2,1,0:T(4,128)S(1)}, f32[2,4,32]{2,1,0:T(4,128)S(1)}, u32[]{:S(2)}, u32[]{:S(2)}) %collective-permute-start.20) | collective-permute-done | bytes 1056 | tf_op jit(solution)/shard_map/ppermute | solution.py:153
  95.3 0.6 select_add_fusion
  (88 shorter events, 5.1 us)
Async XLA Ops:
  0.6 12.0 %collective-permute-start.23 = (bf16[128,512]{1,0:T(8,128)(2,1)}, bf16[128,512]{1,0:T(8,128)(2,1)S(1)}, u32[]{:S(2)}, u32[]{:S(2)}) collective-permute-start(bf16[128,512]{1,0:T(8,128)(2,1)} %param.16), channel_id=1, source_target_pairs={{0,8},{4,12},{8,0},{12,4},{1,9},{5,13},{9,1},{13,5},{2,10},{6,14},... | collective-permute-start | bytes 393224 | tf_op jit(solution)/shard_map/ppermute | solution.py:71
  3.7 14.3 %collective-permute-start.22 = (bf16[128,512]{1,0:T(8,128)(2,1)}, bf16[128,512]{1,0:T(8,128)(2,1)S(1)}, u32[]{:S(2)}, u32[]{:S(2)}) collective-permute-start(bf16[128,512]{1,0:T(8,128)(2,1)} %param.16), channel_id=1, source_target_pairs={{0,4},{4,0},{8,12},{12,8},{1,5},{5,1},{9,13},{13,9},{2,6},{6,2},{1... | collective-permute-start | bytes 393224 | tf_op jit(solution)/shard_map/ppermute | solution.py:72
  6.3 8.2 %collective-permute-start.3 = (bf16[32,3712]{1,0:T(8,128)(2,1)S(1)}, bf16[32,3712]{1,0:T(8,128)(2,1)S(1)}, u32[]{:S(2)}, u32[]{:S(2)}) collective-permute-start(bf16[32,3712]{1,0:T(8,128)(2,1)S(1)} %concatenate.10), channel_id=1, source_target_pairs={{0,8},{4,12},{1,0},{5,4},{2,1},{6,5},{3,2},{7,6},{11,3},{15,7},{10... | collective-permute-start | bytes 712712 | tf_op jit(solution)/shard_map/ppermute | solution.py:44
  6.4 8.4 %collective-permute-start.1 = (bf16[32,3712]{1,0:T(8,128)(2,1)S(1)}, bf16[32,3712]{1,0:T(8,128)(2,1)S(1)}, u32[]{:S(2)}, u32[]{:S(2)}) collective-permute-start(bf16[32,3712]{1,0:T(8,128)(2,1)S(1)} %concatenate.10), channel_id=1, source_target_pairs={{0,1},{4,5},{1,2},{5,6},{2,3},{6,7},{3,11},{7,15},{11,10},{15,14},... | collective-permute-start | bytes 712712 | tf_op jit(solution)/shard_map/ppermute | solution.py:43
  8.3 6.5 %collective-permute-start = (bf16[32,3712]{1,0:T(8,128)(2,1)S(1)}, bf16[32,3712]{1,0:T(8,128)(2,1)S(1)}, u32[]{:S(2)}, u32[]{:S(2)}) collective-permute-start(bf16[32,3712]{1,0:T(8,128)(2,1)S(1)} %concatenate.10), channel_id=1, source_target_pairs={{0,4},{4,0},{1,5},{5,1},{2,6},{6,2},{3,7},{7,3},{11,15},{15,11},{1... | collective-permute-start | bytes 712712 | tf_op jit(solution)/shard_map/ppermute | solution.py:54
  12.6 5.6 %collective-permute-start.24 = (bf16[128,512]{1,0:T(8,128)(2,1)S(1)}, bf16[128,512]{1,0:T(8,128)(2,1)S(1)}, u32[]{:S(2)}, u32[]{:S(2)}) collective-permute-start(bf16[128,512]{1,0:T(8,128)(2,1)S(1)} %collective-permute-done.23), channel_id=1, source_target_pairs={{0,4},{4,0},{8,12},{12,8},{1,5},{5,1},{9,13},{13,9},{2,6},{6,2},{1... | collective-permute-start | bytes 393224 | tf_op jit(solution)/shard_map/ppermute | solution.py:72
  14.5 7.4 %collective-permute-start.7 = (bf16[32,3712]{1,0:T(8,128)(2,1)S(1)}, bf16[32,3712]{1,0:T(8,128)(2,1)S(1)}, u32[]{:S(2)}, u32[]{:S(2)}) collective-permute-start(bf16[32,3712]{1,0:T(8,128)(2,1)S(1)} %collective-permute-done.3), channel_id=1, source_target_pairs={{0,8},{4,12},{1,0},{5,4},{2,1},{6,5},{3,2},{7,6},{11,3},{15,7},{10... | collective-permute-start | bytes 712712 | tf_op jit(solution)/shard_map/ppermute | solution.py:44
  14.8 11.4 %collective-permute-start.4 = (bf16[32,3712]{1,0:T(8,128)(2,1)S(1)}, bf16[32,3712]{1,0:T(8,128)(2,1)S(1)}, u32[]{:S(2)}, u32[]{:S(2)}) collective-permute-start(bf16[32,3712]{1,0:T(8,128)(2,1)S(1)} %collective-permute-done.3), channel_id=1, source_target_pairs={{0,4},{4,0},{1,5},{5,1},{2,6},{6,2},{3,7},{7,3},{11,15},{15,11},{1... | collective-permute-start | bytes 712712 | tf_op jit(solution)/shard_map/ppermute | solution.py:54
  14.8 8.2 %collective-permute-start.5 = (bf16[32,3712]{1,0:T(8,128)(2,1)S(1)}, bf16[32,3712]{1,0:T(8,128)(2,1)S(1)}, u32[]{:S(2)}, u32[]{:S(2)}) collective-permute-start(bf16[32,3712]{1,0:T(8,128)(2,1)S(1)} %collective-permute-done.1), channel_id=1, source_target_pairs={{0,1},{4,5},{1,2},{5,6},{2,3},{6,7},{3,11},{7,15},{11,10},{15,14},... | collective-permute-start | bytes 712712 | tf_op jit(solution)/shard_map/ppermute | solution.py:43
  18.0 6.7 %collective-permute-start.2 = (bf16[32,3712]{1,0:T(8,128)(2,1)S(1)}, bf16[32,3712]{1,0:T(8,128)(2,1)S(1)}, u32[]{:S(2)}, u32[]{:S(2)}) collective-permute-start(bf16[32,3712]{1,0:T(8,128)(2,1)S(1)} %collective-permute-done.1), channel_id=1, source_target_pairs={{0,4},{4,0},{1,5},{5,1},{2,6},{6,2},{3,7},{7,3},{11,15},{15,11},{1... | collective-permute-start | bytes 712712 | tf_op jit(solution)/shard_map/ppermute | solution.py:54
  21.9 7.0 %collective-permute-start.11 = (bf16[32,3712]{1,0:T(8,128)(2,1)S(1)}, bf16[32,3712]{1,0:T(8,128)(2,1)S(1)}, u32[]{:S(2)}, u32[]{:S(2)}) collective-permute-start(bf16[32,3712]{1,0:T(8,128)(2,1)S(1)} %collective-permute-done.7), channel_id=1, source_target_pairs={{0,8},{4,12},{1,0},{5,4},{2,1},{6,5},{3,2},{7,6},{11,3},{15,7},{10... | collective-permute-start | bytes 712712 | tf_op jit(solution)/shard_map/ppermute | solution.py:44
  22.3 11.8 %collective-permute-start.8 = (bf16[32,3712]{1,0:T(8,128)(2,1)S(1)}, bf16[32,3712]{1,0:T(8,128)(2,1)S(1)}, u32[]{:S(2)}, u32[]{:S(2)}) collective-permute-start(bf16[32,3712]{1,0:T(8,128)(2,1)S(1)} %collective-permute-done.7), channel_id=1, source_target_pairs={{0,4},{4,0},{1,5},{5,1},{2,6},{6,2},{3,7},{7,3},{11,15},{15,11},{1... | collective-permute-start | bytes 712712 | tf_op jit(solution)/shard_map/ppermute | solution.py:54
  23.0 7.5 %collective-permute-start.9 = (bf16[32,3712]{1,0:T(8,128)(2,1)S(1)}, bf16[32,3712]{1,0:T(8,128)(2,1)S(1)}, u32[]{:S(2)}, u32[]{:S(2)}) collective-permute-start(bf16[32,3712]{1,0:T(8,128)(2,1)S(1)} %collective-permute-done.5), channel_id=1, source_target_pairs={{0,1},{4,5},{1,2},{5,6},{2,3},{6,7},{3,11},{7,15},{11,10},{15,14},... | collective-permute-start | bytes 712712 | tf_op jit(solution)/shard_map/ppermute | solution.py:43
  24.7 7.5 %collective-permute-start.6 = (bf16[32,3712]{1,0:T(8,128)(2,1)S(1)}, bf16[32,3712]{1,0:T(8,128)(2,1)S(1)}, u32[]{:S(2)}, u32[]{:S(2)}) collective-permute-start(bf16[32,3712]{1,0:T(8,128)(2,1)S(1)} %collective-permute-done.5), channel_id=1, source_target_pairs={{0,4},{4,0},{1,5},{5,1},{2,6},{6,2},{3,7},{7,3},{11,15},{15,11},{1... | collective-permute-start | bytes 712712 | tf_op jit(solution)/shard_map/ppermute | solution.py:54
  28.9 6.6 %collective-permute-start.14 = (bf16[32,1920]{1,0:T(8,128)(2,1)S(1)}, bf16[32,1920]{1,0:T(8,128)(2,1)S(1)}, u32[]{:S(2)}, u32[]{:S(2)}) collective-permute-start(bf16[32,1920]{1,0:T(8,128)(2,1)S(1)} %slice.89), channel_id=1, source_target_pairs={{0,8},{4,12},{1,0},{5,4},{2,1},{6,5},{3,2},{7,6},{11,3},{15,7},{10... | collective-permute-start | bytes 368648 | tf_op jit(solution)/shard_map/ppermute | solution.py:47
  30.5 5.0 %collective-permute-start.13 = (bf16[32,1792]{1,0:T(8,128)(2,1)S(1)}, bf16[32,1792]{1,0:T(8,128)(2,1)S(1)}, u32[]{:S(2)}, u32[]{:S(2)}) collective-permute-start(bf16[32,1792]{1,0:T(8,128)(2,1)S(1)} %slice.88), channel_id=1, source_target_pairs={{0,1},{4,5},{1,2},{5,6},{2,3},{6,7},{3,11},{7,15},{11,10},{15,14},... | collective-permute-start | bytes 344072 | tf_op jit(solution)/shard_map/ppermute | solution.py:46
  32.2 4.9 %collective-permute-start.12 = (bf16[32,3712]{1,0:T(8,128)(2,1)S(1)}, bf16[32,3712]{1,0:T(8,128)(2,1)S(1)}, u32[]{:S(2)}, u32[]{:S(2)}) collective-permute-start(bf16[32,3712]{1,0:T(8,128)(2,1)S(1)} %collective-permute-done.11), channel_id=1, source_target_pairs={{0,4},{4,0},{1,5},{5,1},{2,6},{6,2},{3,7},{7,3},{11,15},{15,11},{1... | collective-permute-start | bytes 712712 | tf_op jit(solution)/shard_map/ppermute | solution.py:54
  32.2 3.5 %collective-permute-start.10 = (bf16[32,3712]{1,0:T(8,128)(2,1)S(1)}, bf16[32,3712]{1,0:T(8,128)(2,1)S(1)}, u32[]{:S(2)}, u32[]{:S(2)}) collective-permute-start(bf16[32,3712]{1,0:T(8,128)(2,1)S(1)} %collective-permute-done.9), channel_id=1, source_target_pairs={{0,4},{4,0},{1,5},{5,1},{2,6},{6,2},{3,7},{7,3},{11,15},{15,11},{1... | collective-permute-start | bytes 712712 | tf_op jit(solution)/shard_map/ppermute | solution.py:54
  35.6 3.5 %collective-permute-start.15 = (bf16[32,3712]{1,0:T(8,128)(2,1)S(1)}, bf16[32,3712]{1,0:T(8,128)(2,1)S(1)}, u32[]{:S(2)}, u32[]{:S(2)}) collective-permute-start(bf16[32,3712]{1,0:T(8,128)(2,1)S(1)} %pad_maximum_fusion.3), channel_id=1, source_target_pairs={{0,4},{4,0},{1,5},{5,1},{2,6},{6,2},{3,7},{7,3},{11,15},{15,11},{1... | collective-permute-start | bytes 712712 | tf_op jit(solution)/shard_map/ppermute | solution.py:54
  43.0 5.4 %copy-start = (bf16[512,3712]{1,0:T(8,128)(2,1)S(1)}, bf16[512,3712]{1,0:T(8,128)(2,1)}, u32[]{:S(2)}) copy-start(bf16[512,3712]{1,0:T(8,128)(2,1)} %constant_dynamic-update-slice_fusion) | copy-start | bytes 11403268
  59.2 30.7 %collective-permute-start.18 = (f32[2,4,4,32]{3,2,1,0:T(4,128)S(1)}, f32[2,4,4,32]{3,2,1,0:T(4,128)}, u32[]{:S(2)}, u32[]{:S(2)}) collective-permute-start(f32[2,4,4,32]{3,2,1,0:T(4,128)S(1)} %bitcast.74), channel_id=1, source_target_pairs={{0,3},{1,0},{2,1},{3,2},{4,7},{5,4},{6,5},{7,6},{8,11},{9,8},{10,9... | collective-permute-start | bytes 12296 | tf_op jit(solution)/shard_map/ppermute | solution.py:150
  62.8 27.1 %collective-permute-start.17 = (f32[2,4,4,32]{3,2,1,0:T(4,128)S(1)}, f32[2,4,4,32]{3,2,1,0:T(4,128)}, u32[]{:S(2)}, u32[]{:S(2)}) collective-permute-start(f32[2,4,4,32]{3,2,1,0:T(4,128)S(1)} %bitcast.75), channel_id=1, source_target_pairs={{0,2},{1,3},{2,0},{3,1},{4,6},{5,7},{6,4},{7,5},{8,10},{9,11},{10,... | collective-permute-start | bytes 12296 | tf_op jit(solution)/shard_map/ppermute | solution.py:150
  62.8 27.1 %collective-permute-start.16 = (f32[2,4,4,32]{3,2,1,0:T(4,128)S(1)}, f32[2,4,4,32]{3,2,1,0:T(4,128)}, u32[]{:S(2)}, u32[]{:S(2)}) collective-permute-start(f32[2,4,4,32]{3,2,1,0:T(4,128)S(1)} %bitcast.76), channel_id=1, source_target_pairs={{0,1},{1,2},{2,3},{3,0},{4,5},{5,6},{6,7},{7,4},{8,9},{9,10},{10,1... | collective-permute-start | bytes 12296 | tf_op jit(solution)/shard_map/ppermute | solution.py:150
  73.6 4.6 %copy-start.1 = (bf16[512,3712]{1,0:T(8,128)(2,1)S(1)}, bf16[512,3712]{1,0:T(8,128)(2,1)}, u32[]{:S(2)}) copy-start(bf16[512,3712]{1,0:T(8,128)(2,1)} %constant_dynamic-update-slice_fusion) | copy-start | bytes 11403268
  73.6 4.6 %copy-start.3 = (f32[512,512]{0,1:T(8,128)S(1)}, f32[512,512]{0,1:T(8,128)}, u32[]{:S(2)}) copy-start(f32[512,512]{0,1:T(8,128)} %get-tuple-element.31) | copy-start | bytes 3145732
  73.6 4.6 %copy-start.6 = (f32[512]{0:T(512)S(1)}, f32[512]{0:T(512)}, u32[]{:S(2)}) copy-start(f32[512]{0:T(512)} %get-tuple-element.19) | copy-start | bytes 6148
  83.2 3.7 %copy-start.2 = (bf16[512,3584]{1,0:T(8,128)(2,1)S(1)}, bf16[512,3584]{1,0:T(8,128)(2,1)}, u32[]{:S(2)}) copy-start(bf16[512,3584]{1,0:T(8,128)(2,1)} %param.17) | copy-start | bytes 11010052
  86.9 2.0 %copy-start.4 = (bf16[1,496,512]{2,1,0:T(8,128)(2,1)S(1)}, bf16[1,496,512]{2,1,0:T(8,128)(2,1)}, u32[]{:S(2)}) copy-start(bf16[1,496,512]{2,1,0:T(8,128)(2,1)} %fusion.15) | copy-start | bytes 1523716
  86.9 8.5 %copy-start.5 = (s32[32,8]{0,1:T(8,128)S(1)}, s32[32,8]{0,1:T(8,128)}, u32[]{:S(2)}) copy-start(s32[32,8]{0,1:T(8,128)} %param.13) | copy-start | bytes 3076
  90.7 2.1 %collective-permute-start.21 = (f32[2,4,32]{2,1,0:T(4,128)S(1)}, f32[2,4,32]{2,1,0:T(4,128)S(1)}, u32[]{:S(2)}, u32[]{:S(2)}) collective-permute-start(f32[2,4,32]{2,1,0:T(4,128)S(1)} %bitcast.78), channel_id=1, source_target_pairs={{0,12},{4,0},{8,4},{12,8},{1,13},{5,1},{9,5},{13,9},{2,14},{6,2},{... | collective-permute-start | bytes 3080 | tf_op jit(solution)/shard_map/ppermute | solution.py:153
  91.5 3.6 %collective-permute-start.20 = (f32[2,4,32]{2,1,0:T(4,128)S(1)}, f32[2,4,32]{2,1,0:T(4,128)S(1)}, u32[]{:S(2)}, u32[]{:S(2)}) collective-permute-start(f32[2,4,32]{2,1,0:T(4,128)S(1)} %bitcast.79), channel_id=1, source_target_pairs={{0,8},{4,12},{8,0},{12,4},{1,9},{5,13},{9,1},{13,5},{2,10},{6,14},... | collective-permute-start | bytes 3080 | tf_op jit(solution)/shard_map/ppermute | solution.py:153
  92.3 3.0 %collective-permute-start.19 = (f32[2,4,32]{2,1,0:T(4,128)S(1)}, f32[2,4,32]{2,1,0:T(4,128)S(1)}, u32[]{:S(2)}, u32[]{:S(2)}) collective-permute-start(f32[2,4,32]{2,1,0:T(4,128)S(1)} %bitcast.80), channel_id=1, source_target_pairs={{0,4},{4,8},{8,12},{12,0},{1,5},{5,9},{9,13},{13,1},{2,6},{6,10},{... | collective-permute-start | bytes 3080 | tf_op jit(solution)/shard_map/ppermute | solution.py:153

commit v2 on v1

v2 whole, which is shorter than its diff:
```python
import jax
import jax.numpy as jnp
from jax import lax
from jax.experimental import pallas as pl
from jax.experimental.pallas import tpu as pltpu
from jax.sharding import PartitionSpec as P

MEAN_LENGTH = 32.0
AXES = ("node", "local")
F32 = jnp.float32
BF16 = jnp.bfloat16


def dot(a, b, ca, cb):
    return lax.dot_general(a, b, (((ca,), (cb,)), ((), ())), preferred_element_type=F32)


def ring_places(node_count, local_count):
    chips = []
    for y in range(node_count // 2):
        row = range(local_count) if y % 2 == 0 else range(local_count - 1, -1, -1)
        chips += [(y, z) for z in row]
    return chips


def ring_offsets(total):
    offsets = [0]
    for step in range(1, (total - 1) // 2 + 1):
        offsets += [-step, step]
    return offsets + [total // 2]


def gather_ring(rows, tags, node_count, local_count, split):
    chips = ring_places(node_count, local_count)
    total = len(chips)

    def flat(chip, core):
        return (chip[0] * 2 + core) * local_count + chip[1]

    def shift(step):
        return [
            (flat(chips[r], c), flat(chips[(r + (step if c == 0 else -step)) % total], c))
            for r in range(total)
            for c in (0, 1)
        ]

    swap = [(flat(chip, c), flat(chip, 1 - c)) for chip in chips for c in (0, 1)]
    one, two = shift(1), shift(-1)

    def send(a, perm):
        return lax.ppermute(a, AXES, perm)

    def joined(a, b):
        return jnp.concatenate([a, b], axis=1)

    core = lax.axis_index("node") % 2
    first, second = send(rows, one), send(rows, two)
    tag_first, tag_second = send(tags, one), send(tags, two)
    blocks = [joined(rows, tags), joined(send(rows, swap), send(tags, swap))]
    first, second = joined(first, tag_first), joined(second, tag_second)
    for step in range(1, (total - 1) // 2 + 1):
        if step > 1:
            first, second = send(first, one), send(second, two)
        blocks += [first, send(first, swap), second, send(second, swap)]
    first, second = send(first[:, :split], one), send(second[:, split:], two)
    last = joined(first, second)
    blocks += [last, send(last, swap)]
    return blocks


def block_numbers(node, local, node_count, local_count):
    total = node_count // 2 * local_count
    y, core = node // 2, node % 2
    sign = 1 - 2 * core
    mine = y * local_count + jnp.where(y % 2 == 0, local, local_count - 1 - local)
    steps = [(0, 0), (0, 1)]
    for s in range(1, (total - 1) // 2 + 1):
        steps += [(-s, 0), (s, 1), (s, 0), (-s, 1)]
    steps += [(total // 2, 0), (total // 2, 1)]
    numbers = []
    for offset, other in steps:
        at = (mine + sign * offset + total) % total
        at_y, at_z = at // local_count, at % local_count
        at_z = jnp.where(at_y % 2 == 0, at_z, local_count - 1 - at_z)
        at_core = core + other - 2 * core * other
        numbers.append((at_y * 2 + at_core) * local_count + at_z)
    return numbers


def lengths_at(lens_ref, tokens):
    found = jnp.zeros(tokens.shape, jnp.int32)
    end = 0
    for r in range(lens_ref.shape[0]):
        found = jnp.where(tokens >= end, lens_ref[r], found)
        end = end + lens_ref[r]
    return found.astype(F32)


def rows_kernel(counts, first_block, choices, capacity, lens_ref, where_ref, *refs):
    count = counts[2]
    blocks, refs = refs[:count], refs[count:]
    if first_block:
        before_ref, refs = refs[0], refs[1:]
    hidden_ref, down_ref, x_ref, scaled_ref, grad_ref, info_ref, sums_ref, hidden_scr = refs
    experts, slot_total, units = hidden_ref.shape
    here = blocks[0].shape[0]
    features = x_ref.shape[1]
    tokens = count * here
    node, local = where_ref[0], where_ref[1]
    numbers = block_numbers(node, local, counts[0], counts[1])[first_block : first_block + count]
    for b in range(count):
        x_ref[b * here : (b + 1) * here, :] = blocks[b][:, :features]
    tags = jnp.concatenate([ref[:, features:] for ref in blocks], axis=0).astype(F32).T
    gates, ids = tags[:choices], tags[choices : 2 * choices]
    token = lax.broadcasted_iota(jnp.int32, (1, tokens), 1)
    number = jnp.zeros((1, tokens), jnp.int32)
    for b in range(count):
        number = jnp.where(token // here == b, numbers[b], number)
    weight = MEAN_LENGTH / lengths_at(lens_ref, number * here + token % here)
    earlier = lax.broadcasted_iota(jnp.int32, (tokens, tokens), 0)
    later = lax.broadcasted_iota(jnp.int32, (tokens, tokens), 1)
    earlier = ((earlier < later) & (earlier // here == later // here)).astype(F32).astype(BF16)
    named = [ids == (node * experts + e).astype(F32) for e in range(experts)]
    hits = [jnp.sum(n.astype(F32), axis=0, keepdims=True) for n in named]
    gate = [jnp.sum(jnp.where(n, gates, 0.0), axis=0, keepdims=True) for n in named]
    row = lax.broadcasted_iota(jnp.int32, (8, tokens), 0)
    stacked = jnp.zeros((8, tokens), F32)
    for e in range(experts):
        stacked = jnp.where(row == e, hits[e], stacked)
    ranks = dot(stacked.astype(BF16), earlier, 1, 0)
    slot = lax.broadcasted_iota(jnp.int32, (slot_total, tokens), 0).astype(F32)
    info = jnp.zeros((8, tokens), F32)
    for e in range(experts):
        rank = ranks[e : e + 1]
        live = (hits[e] > 0.5) & (rank < capacity - 0.5)
        cell = jnp.where(live, number.astype(F32) * capacity + rank, -1.0)
        info = jnp.where(row == e, cell, info)
        info = jnp.where(row == experts + e, gate[e], info)
        placing = (slot == cell).astype(F32).astype(BF16)
        hidden = dot(hidden_ref[e], placing, 0, 0)
        hidden_scr[e] = hidden.astype(BF16)
        scaled_ref[e] = (hidden * (gate[e] * weight)).astype(BF16)
    info_ref[...] = info
    step = 256 if units % 256 == 0 else units
    sums = jnp.zeros((8, tokens), F32)
    for e in range(experts):

        def part(i, total, e=e):
            at = pl.ds(pl.multiple_of(i * step, step), step)
            back = dot(down_ref[e, at, :], x_ref[...], 1, 1) * weight
            grad_ref[e, at, :] = back.astype(BF16)
            return total + jnp.sum(back * hidden_scr[e, at, :].astype(F32), axis=0, keepdims=True)

        total = lax.fori_loop(0, units // step, part, jnp.zeros((1, tokens), F32))
        sums = jnp.where(row == e, total, sums)
    if first_block:
        sums_ref[...] = before_ref[...]
    else:
        sums_ref[...] = jnp.zeros(sums_ref.shape, F32)
    for b in range(count):
        sums_ref[numbers[b]] = sums[:experts, b * here : (b + 1) * here]


VMEM = pl.BlockSpec(memory_space=pltpu.VMEM)
SMEM = pl.BlockSpec(memory_space=pltpu.SMEM)


def rows_call(counts, first_block, choices, capacity, lengths, where, blocks, before, hidden, down):
    count = len(blocks)
    here = blocks[0].shape[0]
    experts, _, units = hidden.shape
    features = down.shape[2]
    tokens = count * here
    device_count = counts[0] * counts[1]
    given = [lengths, where, *blocks] + ([before] if first_block else []) + [hidden, down]
    return pl.pallas_call(
        lambda *refs: rows_kernel((*counts, count), first_block, choices, capacity, *refs),
        out_shape=(
            jax.ShapeDtypeStruct((tokens, features), BF16),
            jax.ShapeDtypeStruct((experts, units, tokens), BF16),
            jax.ShapeDtypeStruct((experts, units, tokens), BF16),
            jax.ShapeDtypeStruct((8, tokens), F32),
            jax.ShapeDtypeStruct((device_count, experts, here), F32),
        ),
        in_specs=[SMEM, SMEM] + [VMEM] * (len(given) - 2),
        out_specs=[VMEM] * 5,
        scratch_shapes=[pltpu.VMEM((experts, units, tokens), BF16)],
        compiler_params=pltpu.CompilerParams(vmem_limit_bytes=16 * 2**20),
        cost_estimate=pl.CostEstimate(
            flops=2 * tokens * experts * units * features,
            bytes_accessed=2 * experts * units * features,
            transcendentals=0,
        ),
        name="rows_first" if not first_block else "rows_second",
    )(*given)


def weights_kernel(
    counts,
    tile,
    lens_ref,
    where_ref,
    x_a,
    x_b,
    scaled_a,
    scaled_b,
    grad_a,
    grad_b,
    info_a,
    info_b,
    shared_0,
    shared_1,
    shared_2,
    shared_3,
    down_ref,
    d_down_ref,
    d_hidden_ref,
    d_hidden_shared_ref,
    d_down_shared_ref,
    shared_scr,
    ordered_scr,
    near_scr,
):
    experts = scaled_a.shape[0]
    tokens, features = x_a.shape
    slot_total = d_hidden_ref.shape[1]
    node_tokens = shared_0.shape[0]
    node_count, local_count = counts
    here = node_tokens // local_count
    node, local = where_ref[0], where_ref[1]
    i = pl.program_id(0)
    at = pl.ds(pl.multiple_of(i * tile, tile), tile)
    for e in range(experts):
        total = dot(scaled_a[e], x_a[:, at], 1, 0) + dot(scaled_b[e], x_b[:, at], 1, 0)
        d_down_ref[e] = total.astype(BF16)

    for e in range(experts):

        @pl.when(i == 1 + e)
        def _(e=e):
            slot = lax.broadcasted_iota(jnp.int32, (slot_total, tokens), 0).astype(F32)
            total = jnp.zeros((slot_total, grad_a.shape[1]), F32)
            for info, grad in ((info_a, grad_a), (info_b, grad_b)):
                gate = info[experts + e : experts + e + 1, :]
                gated = jnp.where(slot == info[e : e + 1, :], gate, 0.0).astype(BF16)
                total = total + dot(gated, grad[e], 1, 1)
            d_hidden_ref[e] = total.astype(BF16)

    @pl.when(i == 1 + experts)
    def _():
        numbers = block_numbers(node, local, node_count, local_count)
        half = len(numbers) // 2
        for b, number in enumerate(numbers):
            x = x_a if b < half else x_b
            rows = x.at[(b % half) * here : (b % half + 1) * here, :]

            @pl.when(number // local_count == node)
            def _(rows=rows, number=number):
                to = pl.ds(pl.multiple_of(number % local_count * here, here), here)
                near_scr[to, :] = rows[...]

        spread = lax.broadcasted_iota(jnp.int32, (node_tokens, 128), 0)
        weight = MEAN_LENGTH / lengths_at(lens_ref, node * node_tokens + spread)[:, :1]
        back = dot(near_scr[...], down_ref[...], 1, 1)
        d_hidden_shared_ref[...] = (back * weight).astype(BF16)

    @pl.when(i == 2 + experts)
    def _():
        spread = lax.broadcasted_iota(jnp.int32, (node_tokens, 128), 0)
        for step, shared in enumerate((shared_0, shared_1, shared_2, shared_3)):
            n = node + step - 2 * (node & step)
            weight = MEAN_LENGTH / lengths_at(lens_ref, n * node_tokens + spread)[:, :1]
            to = pl.ds(pl.multiple_of(n * node_tokens, node_tokens), node_tokens)
            shared_scr[to, :] = (shared[...].astype(F32) * weight).astype(BF16)
        numbers = block_numbers(node, local, node_count, local_count)
        for b, number in enumerate(numbers):
            rows = pl.ds(pl.multiple_of(number * here, here), here)
            ordered_scr[b * here : (b + 1) * here, :] = shared_scr[rows, :]
        width = d_down_shared_ref.shape[1]
        columns = pl.ds(pl.multiple_of(node * width, width), width)
        total = dot(ordered_scr[:tokens, :], x_a[:, columns], 0, 0)
        total = total + dot(ordered_scr[tokens:, :], x_b[:, columns], 0, 0)
        d_down_shared_ref[...] = total.astype(BF16)


def weights_call(counts, slot_total, lengths, where, first, second, shared, down_shared):
    x_a, scaled_a, grad_a, info_a, _ = first
    x_b, scaled_b, grad_b, info_b, _ = second
    experts, units, tokens = scaled_a.shape
    features = x_a.shape[1]
    node_tokens, shared_units = shared[0].shape
    tile = 512 if features % 512 == 0 else 128
    width = features // counts[0]
    whole = lambda *shape: pl.BlockSpec(shape, lambda i: (0,) * len(shape))
    return pl.pallas_call(
        lambda *refs: weights_kernel(counts, tile, *refs),
        grid=(features // tile,),
        out_shape=(
            jax.ShapeDtypeStruct((experts, units, features), BF16),
            jax.ShapeDtypeStruct((experts, slot_total, units), BF16),
            jax.ShapeDtypeStruct((node_tokens, shared_units), BF16),
            jax.ShapeDtypeStruct((shared_units, width), BF16),
        ),
        in_specs=[SMEM, SMEM] + [VMEM] * 13,
        out_specs=(
            pl.BlockSpec((experts, units, tile), lambda i: (0, 0, i)),
            whole(experts, slot_total, units),
            whole(node_tokens, shared_units),
            whole(shared_units, width),
        ),
        scratch_shapes=[
            pltpu.VMEM((4 * node_tokens, shared_units), BF16),
            pltpu.VMEM((4 * node_tokens, shared_units), BF16),
            pltpu.VMEM((node_tokens, features), BF16),
        ],
        compiler_params=pltpu.CompilerParams(vmem_limit_bytes=20 * 2**20),
        cost_estimate=pl.CostEstimate(
            flops=4 * tokens * experts * units * features,
            bytes_accessed=2 * experts * units * features,
            transcendentals=0,
        ),
        name="weights",
    )(lengths, where, x_a, x_b, scaled_a, scaled_b, grad_a, grad_b, info_a, info_b, *shared, down_shared)


def swapped_nodes(block):
    core_swap = [(n, n ^ 1) for n in range(4)]
    chip_swap = [(n, n ^ 2) for n in range(4)]
    across = lax.ppermute(block, "node", chip_swap)
    return [block, lax.ppermute(block, "node", core_swap), across, lax.ppermute(across, "node", core_swap)]


def return_gates(slot_grad, expert_ids, experts):
    node_count, local_count = lax.axis_size("node"), lax.axis_size("local")
    node, local = lax.axis_index("node"), lax.axis_index("local")
    here = expert_ids.shape[0]
    slot_grad = slot_grad.reshape(node_count, local_count, experts, here)

    def turn(count, step):
        return [(i, (i + step) % count) for i in range(count)]

    def own(a):
        return lax.dynamic_index_in_dim(a, local, 1, keepdims=False)

    total = own(slot_grad)
    for step in range(1, local_count):
        total = total + own(lax.ppermute(slot_grad, "local", turn(local_count, step)))
    d_gate = jnp.zeros(expert_ids.shape, F32)
    for step in range(node_count):
        got = total if step == 0 else lax.ppermute(total, "node", turn(node_count, step))
        got = lax.dynamic_index_in_dim(got, node, 0, keepdims=False)
        start = (node + node_count - step) % node_count * experts
        for e in range(experts):
            d_gate = d_gate + jnp.where(expert_ids == start + e, got[e][:, None], 0.0)
    return d_gate


def wide_body(
    out_grad,
    lengths,
    gate_weights,
    expert_ids,
    hidden_routed,
    down_routed,
    hidden_shared,
    down_shared,
):
    node_count = lax.axis_size("node")
    local_count = lax.axis_size("local")
    device_count = node_count * local_count
    here, features = out_grad.shape
    choices = expert_ids.shape[1]
    experts, slot_total, units = hidden_routed.shape
    capacity = slot_total // device_count
    node = lax.axis_index("node")
    pad = jnp.zeros((here, 128 - 2 * choices), BF16)
    packed = jnp.concatenate([out_grad, gate_weights, expert_ids.astype(BF16), pad], axis=1)
    rows = lax.all_gather(packed, AXES, axis=0, tiled=True)
    token_total = device_count * here
    ends = jnp.cumsum(lengths)
    places = jnp.arange(token_total, dtype=jnp.int32)
    inside = (places[:, None] >= (ends - lengths)[None, :]) & (places[:, None] < ends[None, :])
    weight = MEAN_LENGTH / jnp.sum(jnp.where(inside, lengths[None, :], 0), axis=1).astype(F32)
    x = rows[:, :features]
    gates = rows[:, features : features + choices].astype(F32)
    ids = rows[:, features + choices : features + 2 * choices].astype(jnp.int32)
    d_hidden, d_down, sums = [], [], []
    for e in range(experts):
        named = ids == node * experts + e
        hit = jnp.any(named, axis=1)
        gate = jnp.sum(jnp.where(named, gates, 0.0), axis=1)
        hits = hit.astype(jnp.int32).reshape(device_count, here)
        rank = (jnp.cumsum(hits, axis=1) - hits).reshape(-1)
        cell = places // here * capacity + rank
        cell = jnp.where(hit & (rank < capacity), cell, -1)
        placing = jnp.arange(slot_total, dtype=jnp.int32)[:, None] == cell[None, :]
        placing = placing.astype(BF16)
        hidden = dot(hidden_routed[e], placing, 0, 0)
        back = dot(down_routed[e], x, 1, 1) * weight[None, :]
        sums.append(jnp.sum(hidden * back, axis=0))
        gated = placing * gate.astype(BF16)[None, :]
        d_hidden.append(dot(gated, back.astype(BF16), 1, 1).astype(BF16))
        scaled = (hidden * (gate * weight)[None, :]).astype(BF16)
        d_down.append(dot(scaled, x, 1, 0).astype(BF16))
    slot_grad = jnp.stack(sums).reshape(experts, device_count, here)
    d_gate = return_gates(jnp.swapaxes(slot_grad, 0, 1), expert_ids, experts)
    near_total = local_count * here
    near = lax.dynamic_slice_in_dim(x, node * near_total, near_total, 0)
    near_weight = lax.dynamic_slice_in_dim(weight, node * near_total, near_total, 0)
    shared_back = dot(near, down_shared, 1, 1)
    d_hidden_shared = (shared_back * near_weight[:, None]).astype(BF16)
    columns = features // node_count
    mine = lax.dynamic_slice_in_dim(x, node * columns, columns, 1)
    shared = lax.all_gather(hidden_shared, "node", axis=0, tiled=True)
    shared = (shared.astype(F32) * weight[:, None]).astype(BF16)
    d_down_shared = dot(shared, mine, 0, 0).astype(BF16)
    return (jnp.stack(d_hidden), jnp.stack(d_down), d_gate, d_hidden_shared, d_down_shared)


def body(
    out_grad,
    lengths,
    gate_weights,
    expert_ids,
    hidden_routed,
    down_routed,
    hidden_shared,
    down_shared,
):
    counts = lax.axis_size("node"), lax.axis_size("local")
    device_count = counts[0] * counts[1]
    here, features = out_grad.shape
    choices = expert_ids.shape[1]
    experts, slot_total, units = hidden_routed.shape
    capacity = slot_total // device_count
    where = jnp.stack([lax.axis_index("node"), lax.axis_index("local")]).astype(jnp.int32)
    pad = jnp.zeros((here, 128 - 2 * choices), BF16)
    tags = jnp.concatenate([gate_weights, expert_ids.astype(BF16), pad], axis=1)
    blocks = gather_ring(out_grad, tags, *counts, features // 2 // 128 * 128)
    half = len(blocks) // 2
    shared = swapped_nodes(hidden_shared)
    first = rows_call(
        counts, 0, choices, capacity, lengths, where, blocks[:half], None, hidden_routed, down_routed
    )
    second = rows_call(
        counts, half, choices, capacity, lengths, where, blocks[half:], first[4], hidden_routed, down_routed
    )
    d_gate = return_gates(second[4], expert_ids, experts)
    d_down_routed, d_hidden_routed, d_hidden_shared, d_down_shared = weights_call(
        counts, slot_total, lengths, where, first, second, shared, down_shared
    )
    return (d_hidden_routed, d_down_routed, d_gate, d_hidden_shared, d_down_shared)


def solution(mesh):
    placed = (
        P(("groups", "node", "local"), None),
        P("groups"),
        P(("groups", "node", "local"), None),
        P(("groups", "node", "local"), None),
        P("node", "groups", "local"),
        P("node", "local", None),
        P(("groups", "node"), "local"),
        P("local", None),
    )
    small = mesh.shape["node"] == 4 and mesh.shape["local"] == 4
    return jax.shard_map(
        body if small else wide_body,
        mesh=mesh,
        in_specs=placed,
        out_specs=(
            P("node", "groups", "local"),
            P(("groups", "node"), "local", None),
            P(("groups", "node", "local"), None),
            P(("groups", "node"), "local"),
            P(("groups", "local"), "node"),
        ),
        check_vma=False,
    )
```

time: 96.6 us -> 74 us (0.77)
  matrix products: 28.5 us -> 0 us
  Pallas kernels: 0 us -> 19.8 us
  local copies, waits for them, and re-layouts: 24.9 us -> 6.46 us
  other arithmetic: 14 us -> 0.81 us
  waiting for transfers between devices: 8.57 us -> 21 us
  starting transfers between devices: 19.1 us -> 24.8 us
    dot_general x10 -> x0, matrix products: 28.5 us -> none  [dot(): lax.dot_general(a, b, (((ca,), (cb,)), ((), ())), preferred_element_type=...]
    pallas_call x0 -> x3, Pallas kernels: none -> 19.8 us  [the longest x1 11.6 us: weights_call(): pl.pallas_call(lambda *refs: weights_kernel(counts, tile, *refs), grid=(f...]
    ppermute x25 -> x28, waiting for transfers between devices: 8.57 us -> 21 us  [the longest x19 18 us: send(): return lax.ppermute(a, AXES, perm)]
    unnamed x31 -> x21, local copies, waits for them, and re-layouts: 12 us -> 5.34 us
    another operation x8 -> x1, other arithmetic: 6.25 us -> 0.08 us  [body(): jnp.stack([lax.axis_index('node'), lax.axis_index('local')])]
    ppermute x25 -> x28, starting transfers between devices: 19.1 us -> 24.8 us  [the longest x19 15.3 us: send(): return lax.ppermute(a, AXES, perm)]
    gather x6 -> x0, local copies, waits for them, and re-layouts: 4.96 us -> none  [the longest x1 2.64 us: body(): shared_back = dot(blocked[near].reshape(-1, features), down_shared, 1, 1)]
    slice x3 -> x2, local copies, waits for them, and re-layouts: 4.08 us -> 0.02 us  [gather_ring(): first, second = (send(first[:, :split], one), send(second[:, split:], two))]
  transfers between devices with their start and end apart: 25 -> 28, of which waited for: 8 -> 13; matrix products, arithmetic and copies ran while one was open for 48% -> 4% of each run, Pallas kernels for 0% -> 27%
where the time goes in v2:
time: 74 us; the launch traced here: 73.8 us
  starting transfers between devices  24.8 us (34%)
  waiting for transfers between devices  21 us (28%)
  Pallas kernels  19.8 us (27%)
  local copies, waits for them, and re-layouts  6.46 us (9%)
  between operations  0.88 us (1%)
  other arithmetic  0.81 us (1%)
    ppermute x19, waiting for transfers between devices, send(): return lax.ppermute(a, AXES, perm)  18 us
    ppermute x19, starting transfers between devices, send(): return lax.ppermute(a, AXES, perm)  15.3 us
    pallas_call x1, Pallas kernels, weights_call(): pl.pallas_call(lambda *refs: weights_kernel(counts, tile, *refs), grid=(f...  11.6 us
    pallas_call x2, Pallas kernels, rows_call(): pl.pallas_call(lambda *refs: rows_kernel((*counts, count), first_block, c...  8.18 us
    ppermute x3, starting transfers between devices, return_gates(): lax.ppermute(slot_grad, 'local', turn(local_count, step))  7.26 us
    unnamed x21, local copies, waits for them, and re-layouts  5.34 us
    ppermute x3, waiting for transfers between devices, return_gates(): lax.ppermute(total, 'node', turn(node_count, step))  3 us
  transfers between devices with their start and end apart: 28, of which 13 were waited for; matrix products, arithmetic and copies ran while one was open for 4% of the time, Pallas kernels for 27%

profile of v2, /device:TPU:0, one launch (start us, length us, event | category | flops | bytes accessed | tf_op | source)
XLA Modules:
  0.0 73.8 jit_solution(5991899656454543823)
XLA Ops:
  0.6 3.1 %collective-permute-start.2 = (bf16[32,3584]{1,0:T(8,128)(2,1)}, bf16[32,3584]{1,0:T(8,128)(2,1)S(1)}, u32[]{:S(2)}, u32[]{:S(2)}) collective-permute-start(bf16[32,3584]{1,0:T(8,128)(2,1)} %param.8), channel_id=1, source_target_pairs={{0,1},{4,12},{1,2},{5,4},{2,3},{6,5},{3,11},{7,6},{11,10},{15,7},{... | collective-permute-start | bytes 688136 | tf_op jit(solution)/shard_map/ppermute | solution.py:51
  3.7 0.8 %copy.14 = bf16[32,8]{1,0:T(8,128)(2,1)S(1)} copy(bf16[32,8]{0,1:T(8,128)(2,1)} %param.10) | data formatting | bytes 1024 | tf_op args[2]
  4.5 0.8 %copy.13 = s32[32,8]{1,0:T(8,128)S(1)} copy(s32[32,8]{0,1:T(8,128)} %param.11) | data formatting | bytes 2048 | tf_op args[3]
  5.3 0.1 pad_maximum_fusion.1
  5.3 0.0 collective-permute-start.6
  5.4 2.0 %collective-permute-start.3 = (bf16[32,128]{1,0:T(8,128)(2,1)S(1)}, bf16[32,128]{1,0:T(8,128)(2,1)S(1)}, u32[]{:S(2)}, u32[]{:S(2)}) collective-permute-start(bf16[32,128]{1,0:T(8,128)(2,1)S(1)} %pad_maximum_fusion.1), channel_id=1, source_target_pairs={{0,1},{4,12},{1,2},{5,4},{2,3},{6,5},{3,11},{7,6},{11,10},{15,7},{... | collective-permute-start | bytes 24584 | tf_op jit(solution)/shard_map/ppermute | solution.py:51
  7.4 0.1 collective-permute-start.5
  7.4 0.7 collective-permute-done.2
  8.1 0.9 %collective-permute-done.3 = bf16[32,128]{1,0:T(8,128)(2,1)S(1)} collective-permute-done((bf16[32,128]{1,0:T(8,128)(2,1)S(1)}, bf16[32,128]{1,0:T(8,128)(2,1)S(1)}, u32[]{:S(2)}, u32[]{:S(2)}) %collective-permute-start.3) | collective-permute-done | bytes 8224 | tf_op jit(solution)/shard_map/ppermute | solution.py:51
  9.1 2.1 %collective-permute-start.8 = (bf16[32,3712]{1,0:T(8,128)(2,1)S(1)}, bf16[32,3712]{1,0:T(8,128)(2,1)S(1)}, u32[]{:S(2)}, u32[]{:S(2)}) collective-permute-start(bf16[32,3712]{1,0:T(8,128)(2,1)S(1)} %constant_dynamic-update-slice_fusion.refs_4_), channel_id=1, source_target_pairs={{0,1},{4,12},{1,2},{5,4},{2,3},{6,5},{3,11},{7,6},{11,10},{15,7},{... | collective-permute-start | bytes 712712 | tf_op jit(solution)/shard_map/ppermute | solution.py:51
  11.2 4.2 %collective-permute-done.5 = bf16[32,3584]{1,0:T(8,128)(2,1)S(1)} collective-permute-done((bf16[32,3584]{1,0:T(8,128)(2,1)}, bf16[32,3584]{1,0:T(8,128)(2,1)S(1)}, u32[]{:S(2)}, u32[]{:S(2)}) %collective-permute-start.5) | collective-permute-done | bytes 229408 | tf_op jit(solution)/shard_map/ppermute | solution.py:51
  15.4 0.0 collective-permute-done.6
  15.4 0.1 collective-permute-start.10
  15.5 1.6 %collective-permute-done.8.refs_8_ = bf16[32,3712]{1,0:T(8,128)(2,1)S(1)} collective-permute-done((bf16[32,3712]{1,0:T(8,128)(2,1)S(1)}, bf16[32,3712]{1,0:T(8,128)(2,1)S(1)}, u32[]{:S(2)}, u32[]{:S(2)}) %collective-permute-start.8) | collective-permute-done | bytes 237600 | tf_op jit(solution)/shard_map/ppermute | solution.py:51
  17.1 2.5 %collective-permute-start.12 = (bf16[32,3712]{1,0:T(8,128)(2,1)S(1)}, bf16[32,3712]{1,0:T(8,128)(2,1)S(1)}, u32[]{:S(2)}, u32[]{:S(2)}) collective-permute-start(bf16[32,3712]{1,0:T(8,128)(2,1)S(1)} %collective-permute-done.8.refs_8_), channel_id=1, source_target_pairs={{0,1},{4,12},{1,2},{5,4},{2,3},{6,5},{3,11},{7,6},{11,10},{15,7},{... | collective-permute-start | bytes 712712 | tf_op jit(solution)/shard_map/ppermute | solution.py:51
  19.5 3.2 %collective-permute-done.10.refs_2_ = bf16[32,3712]{1,0:T(8,128)(2,1)S(1)} collective-permute-done((bf16[32,3712]{1,0:T(8,128)(2,1)S(1)}, bf16[32,3712]{1,0:T(8,128)(2,1)S(1)}, u32[]{:S(2)}, u32[]{:S(2)}) %collective-permute-start.10) | collective-permute-done | bytes 237600 | tf_op jit(solution)/shard_map/ppermute | solution.py:51
  22.7 1.3 %collective-permute-start.14 = (bf16[32,3712]{1,0:T(8,128)(2,1)S(1)}, bf16[32,3712]{1,0:T(8,128)(2,1)S(1)}, u32[]{:S(2)}, u32[]{:S(2)}) collective-permute-start(bf16[32,3712]{1,0:T(8,128)(2,1)S(1)} %collective-permute-done.10.refs_2_), channel_id=1, source_target_pairs={{0,8},{4,5},{1,0},{5,6},{2,1},{6,7},{3,2},{7,15},{11,3},{15,14},{1... | collective-permute-start | bytes 712712 | tf_op jit(solution)/shard_map/ppermute | solution.py:51
  24.0 0.0 collective-permute-start.1
  24.0 0.5 collective-permute-start
  24.5 1.2 %collective-permute-done.12.refs_4_ = bf16[32,3712]{1,0:T(8,128)(2,1)S(1)} collective-permute-done((bf16[32,3712]{1,0:T(8,128)(2,1)S(1)}, bf16[32,3712]{1,0:T(8,128)(2,1)S(1)}, u32[]{:S(2)}, u32[]{:S(2)}) %collective-permute-start.12) | collective-permute-done | bytes 237600 | tf_op jit(solution)/shard_map/ppermute | solution.py:51
  25.7 1.7 %collective-permute-start.16 = (bf16[32,1792]{1,0:T(8,128)(2,1)S(1)}, bf16[32,1792]{1,0:T(8,128)(2,1)S(1)}, u32[]{:S(2)}, u32[]{:S(2)}) collective-permute-start(bf16[32,1792]{1,0:T(8,128)(2,1)S(1)} %slice.48), channel_id=1, source_target_pairs={{0,1},{4,12},{1,2},{5,4},{2,3},{6,5},{3,11},{7,6},{11,10},{15,7},{... | collective-permute-start | bytes 344072 | tf_op jit(solution)/shard_map/ppermute | solution.py:51
  27.4 1.0 %concatenate.19.refs_2_ = bf16[32,3712]{1,0:T(8,128)(2,1)S(1)} concatenate(bf16[32,3584]{1,0:T(8,128)(2,1)} %param.8, bf16[32,8]{1,0:T(8,128)(2,1)S(1)} %copy.14, bf16[32,8]{1,0:T(8,128)(2,1)S(1)} %convert_element_type.3, bf16[32,112]{1,0:T(8,128)(2,1)S(1)} %broadcast_in_dim.73), dimensions={1} | concatenate | bytes 475136 | tf_op jit(solution)/shard_map/concatenate | solution.py:54
  28.5 0.1 pad_add_fusion.refs_1_
  28.6 0.0 collective-permute-start.4
  28.6 1.5 %collective-permute-done.14.refs_6_ = bf16[32,3712]{1,0:T(8,128)(2,1)S(1)} collective-permute-done((bf16[32,3712]{1,0:T(8,128)(2,1)S(1)}, bf16[32,3712]{1,0:T(8,128)(2,1)S(1)}, u32[]{:S(2)}, u32[]{:S(2)}) %collective-permute-start.14) | collective-permute-done | bytes 237600 | tf_op jit(solution)/shard_map/ppermute | solution.py:51
  30.1 0.0 collective-permute-start.7
  30.1 0.5 collective-permute-done.16
  30.5 0.8 %collective-permute-start.17 = (bf16[32,1920]{1,0:T(8,128)(2,1)S(1)}, bf16[32,1920]{1,0:T(8,128)(2,1)S(1)}, u32[]{:S(2)}, u32[]{:S(2)}) collective-permute-start(bf16[32,1920]{1,0:T(8,128)(2,1)S(1)} %slice.49), channel_id=1, source_target_pairs={{0,8},{4,5},{1,0},{5,6},{2,1},{6,7},{3,2},{7,15},{11,3},{15,14},{1... | collective-permute-start | bytes 368648 | tf_op jit(solution)/shard_map/ppermute | solution.py:51
  31.3 4.1 %collective-permute-done.17 = bf16[32,1920]{1,0:T(8,128)(2,1)S(1)} collective-permute-done((bf16[32,1920]{1,0:T(8,128)(2,1)S(1)}, bf16[32,1920]{1,0:T(8,128)(2,1)S(1)}, u32[]{:S(2)}, u32[]{:S(2)}) %collective-permute-start.17) | collective-permute-done | bytes 122912 | tf_op jit(solution)/shard_map/ppermute | solution.py:51
  35.4 0.0 collective-permute-start.9
  35.4 0.0 collective-permute-done.1
  35.4 0.6 collective-permute-start.11
  36.0 0.0 collective-permute-done
  36.0 0.1 collective-permute-start.13
  36.1 0.0 collective-permute-done.4.refs_5_
  36.1 0.4 collective-permute-start.15
  36.5 0.1 collective-permute-start.18
  36.6 0.3 collective-permute-done.9.refs_9_
  36.9 0.8 %collective-permute-start.20 = (bf16[128,512]{1,0:T(8,128)(2,1)}, bf16[128,512]{1,0:T(8,128)(2,1)S(1)}, u32[]{:S(2)}, u32[]{:S(2)}) collective-permute-start(bf16[128,512]{1,0:T(8,128)(2,1)} %refs_10_.3), channel_id=1, source_target_pairs={{0,8},{4,12},{8,0},{12,4},{1,9},{5,13},{9,1},{13,5},{2,10},{6,14},... | collective-permute-start | bytes 393224 | tf_op jit(solution)/shard_map/ppermute | solution.py:329
  37.7 3.1 %copy-done = bf16[2,512,3584]{2,1,0:T(8,128)(2,1)S(1)} copy-done((bf16[2,512,3584]{2,1,0:T(8,128)(2,1)S(1)}, bf16[2,512,3584]{2,1,0:T(8,128)(2,1)}, u32[]{:S(2)}) %copy-start) | copy-done | bytes 7340056
  40.8 0.7 copy-done.3
  41.4 4.1 %rows_first.1 = (bf16[256,3584]{1,0:T(8,128)(2,1)S(1)}, bf16[2,512,256]{2,1,0:T(8,128)(2,1)S(1)}, bf16[2,512,256]{2,1,0:T(8,128)(2,1)S(1)}, f32[8,256]{1,0:T(8,128)S(1)}, f32[16,2,32]{2,1,0:T(2,128)S(1)}) custom-call(s32[16]{0:T(128)S(1)} %copy-done.3, s32[2]{0:T(128)S(1)} %pad_add_fusion.refs_1_, bf16[32,3712]{1,0:T(8,128)(2,1)S(1)} %concatenate.19.refs_2_, ...), custom_call_target="tpu_custom_call" | custom-call | flops 1879048192 | bytes 7340032 | tf_op jit(solution)/shard_map/rows_first/pallas_call | solution.py:176
  45.5 0.0 collective-permute-done.20.refs_12_
  45.5 0.1 collective-permute-start.19
  45.6 0.0 collective-permute-done.11.refs_3_
  45.6 0.5 collective-permute-start.21
  46.1 0.0 copy-start.4
  46.1 0.0 copy-start.5
  46.1 4.1 %rows_second.1 = (bf16[256,3584]{1,0:T(8,128)(2,1)S(1)}, bf16[2,512,256]{2,1,0:T(8,128)(2,1)S(1)}, bf16[2,512,256]{2,1,0:T(8,128)(2,1)S(1)}, f32[8,256]{1,0:T(8,128)S(1)}, f32[16,2,32]{2,1,0:T(2,128)S(1)}) custom-call(s32[16]{0:T(128)S(1)} %copy-done.3, s32[2]{0:T(128)S(1)} %pad_add_fusion.refs_1_, bf16[32,3712]{1,0:T(8,128)(2,1)S(1)} %collective-permute-done.10.refs_2_, ...), custom_call_target="tpu_custom_call" | custom-call | flops 1879048192 | bytes 7340032 | tf_op jit(solution)/shard_map/rows_second/pallas_call | solution.py:176
  50.2 3.4 %collective-permute-start.23 = (f32[4,4,2,32]{3,2,0,1:T(2,128)S(1)}, f32[4,4,2,32]{3,2,0,1:T(2,128)S(1)}, u32[]{:S(2)}, u32[]{:S(2)}) collective-permute-start(f32[4,4,2,32]{3,2,0,1:T(2,128)S(1)} %copy.16), channel_id=1, source_target_pairs={{0,2},{1,3},{2,0},{3,1},{4,6},{5,7},{6,4},{7,5},{8,10},{9,11},{10,... | collective-permute-start | bytes 12296 | tf_op jit(solution)/shard_map/ppermute | solution.py:347
  53.7 1.6 %collective-permute-start.22 = (f32[4,4,2,32]{3,2,0,1:T(2,128)S(1)}, f32[4,4,2,32]{3,2,0,1:T(2,128)S(1)}, u32[]{:S(2)}, u32[]{:S(2)}) collective-permute-start(f32[4,4,2,32]{3,2,0,1:T(2,128)S(1)} %copy.16), channel_id=1, source_target_pairs={{0,1},{1,2},{2,3},{3,0},{4,5},{5,6},{6,7},{7,4},{8,9},{9,10},{10,1... | collective-permute-start | bytes 12296 | tf_op jit(solution)/shard_map/ppermute | solution.py:347
  55.3 2.2 %collective-permute-start.24 = (f32[4,4,2,32]{3,2,0,1:T(2,128)S(1)}, f32[4,4,2,32]{3,2,0,1:T(2,128)S(1)}, u32[]{:S(2)}, u32[]{:S(2)}) collective-permute-start(f32[4,4,2,32]{3,2,0,1:T(2,128)S(1)} %copy.16), channel_id=1, source_target_pairs={{0,3},{1,0},{2,1},{3,2},{4,7},{5,4},{6,5},{7,6},{8,11},{9,8},{10,9... | collective-permute-start | bytes 12296 | tf_op jit(solution)/shard_map/ppermute | solution.py:347
  57.5 0.0 collective-permute-done.19.refs_11_
  57.5 0.0 copy-start.7
  57.5 11.6 %weights.1 = (bf16[2,512,3584]{2,1,0:T(8,128)(2,1)}, bf16[2,496,512]{2,1,0:T(8,128)(2,1)}, bf16[128,512]{1,0:T(8,128)(2,1)}, bf16[512,896]{1,0:T(8,128)(2,1)}) custom-call(s32[16]{0:T(128)S(1)} %copy-done.4, s32[2]{0:T(128)S(1)} %pad_add_fusion.refs_1_, bf16[256,3584]{1,0:T(8,128)(2,1)S(1)} %get-tuple-element.19.refs_2_, ...), custom_call_target="tpu_custom_call" | custom-call | flops 3758096384 | bytes 7340032 | tf_op jit(solution)/shard_map/weights/pallas_call | solution.py:295
  69.1 0.0 collective-permute-done.23
  69.1 0.0 collective-permute-done.24
  69.2 0.1 collective-permute-start.27
  69.2 0.9 %collective-permute-start.26 = (f32[4,2,32]{2,1,0:T(2,128)S(1)}, f32[4,2,32]{2,1,0:T(2,128)S(1)}, u32[]{:S(2)}, u32[]{:S(2)}) collective-permute-start(f32[4,2,32]{2,1,0:T(2,128)S(1)} %bitcast.25), channel_id=1, source_target_pairs={{0,8},{4,12},{8,0},{12,4},{1,9},{5,13},{9,1},{13,5},{2,10},{6,14},... | collective-permute-start | bytes 3080 | tf_op jit(solution)/shard_map/ppermute | solution.py:350
  70.1 0.0 collective-permute-start.25
  70.1 0.4 collective-permute-done.27
  70.6 2.3 %collective-permute-done.26 = f32[4,2,32]{2,1,0:T(2,128)S(1)} collective-permute-done((f32[4,2,32]{2,1,0:T(2,128)S(1)}, f32[4,2,32]{2,1,0:T(2,128)S(1)}, u32[]{:S(2)}, u32[]{:S(2)}) %collective-permute-start.26) | collective-permute-done | bytes 1056 | tf_op jit(solution)/shard_map/ppermute | solution.py:350
  72.9 0.2 collective-permute-done.25
  73.1 0.6 select_add_fusion
  (38 shorter events, 0.2 us)
Async XLA Ops:
  0.6 37.0 %copy-start.2 = (bf16[2,496,512]{2,1,0:T(8,128)(2,1)S(1)}, bf16[2,496,512]{2,1,0:T(8,128)(2,1)}, u32[]{:S(2)}) copy-start(bf16[2,496,512]{2,1,0:T(8,128)(2,1)} %refs_11_.3) | copy-start | bytes 3047428
  0.6 7.5 %collective-permute-start.2 = (bf16[32,3584]{1,0:T(8,128)(2,1)}, bf16[32,3584]{1,0:T(8,128)(2,1)S(1)}, u32[]{:S(2)}, u32[]{:S(2)}) collective-permute-start(bf16[32,3584]{1,0:T(8,128)(2,1)} %param.8), channel_id=1, source_target_pairs={{0,1},{4,12},{1,2},{5,4},{2,3},{6,5},{3,11},{7,6},{11,10},{15,7},{... | collective-permute-start | bytes 688136 | tf_op jit(solution)/shard_map/ppermute | solution.py:51
  5.3 10.1 %collective-permute-start.6 = (bf16[32,128]{1,0:T(8,128)(2,1)S(1)}, bf16[32,128]{1,0:T(8,128)(2,1)S(1)}, u32[]{:S(2)}, u32[]{:S(2)}) collective-permute-start(bf16[32,128]{1,0:T(8,128)(2,1)S(1)} %pad_maximum_fusion.1), channel_id=1, source_target_pairs={{0,8},{4,5},{1,0},{5,6},{2,1},{6,7},{3,2},{7,15},{11,3},{15,14},{1... | collective-permute-start | bytes 24584 | tf_op jit(solution)/shard_map/ppermute | solution.py:51
  5.4 3.7 %collective-permute-start.3 = (bf16[32,128]{1,0:T(8,128)(2,1)S(1)}, bf16[32,128]{1,0:T(8,128)(2,1)S(1)}, u32[]{:S(2)}, u32[]{:S(2)}) collective-permute-start(bf16[32,128]{1,0:T(8,128)(2,1)S(1)} %pad_maximum_fusion.1), channel_id=1, source_target_pairs={{0,1},{4,12},{1,2},{5,4},{2,3},{6,5},{3,11},{7,6},{11,10},{15,7},{... | collective-permute-start | bytes 24584 | tf_op jit(solution)/shard_map/ppermute | solution.py:51
  7.4 8.0 %collective-permute-start.5 = (bf16[32,3584]{1,0:T(8,128)(2,1)}, bf16[32,3584]{1,0:T(8,128)(2,1)S(1)}, u32[]{:S(2)}, u32[]{:S(2)}) collective-permute-start(bf16[32,3584]{1,0:T(8,128)(2,1)} %param.8), channel_id=1, source_target_pairs={{0,8},{4,5},{1,0},{5,6},{2,1},{6,7},{3,2},{7,15},{11,3},{15,14},{1... | collective-permute-start | bytes 688136 | tf_op jit(solution)/shard_map/ppermute | solution.py:51
  9.1 8.0 %collective-permute-start.8 = (bf16[32,3712]{1,0:T(8,128)(2,1)S(1)}, bf16[32,3712]{1,0:T(8,128)(2,1)S(1)}, u32[]{:S(2)}, u32[]{:S(2)}) collective-permute-start(bf16[32,3712]{1,0:T(8,128)(2,1)S(1)} %constant_dynamic-update-slice_fusion.refs_4_), channel_id=1, source_target_pairs={{0,1},{4,12},{1,2},{5,4},{2,3},{6,5},{3,11},{7,6},{11,10},{15,7},{... | collective-permute-start | bytes 712712 | tf_op jit(solution)/shard_map/ppermute | solution.py:51
  15.4 7.3 %collective-permute-start.10 = (bf16[32,3712]{1,0:T(8,128)(2,1)S(1)}, bf16[32,3712]{1,0:T(8,128)(2,1)S(1)}, u32[]{:S(2)}, u32[]{:S(2)}) collective-permute-start(bf16[32,3712]{1,0:T(8,128)(2,1)S(1)} %constant_dynamic-update-slice_fusion.2.refs_6_), channel_id=1, source_target_pairs={{0,8},{4,5},{1,0},{5,6},{2,1},{6,7},{3,2},{7,15},{11,3},{15,14},{1... | collective-permute-start | bytes 712712 | tf_op jit(solution)/shard_map/ppermute | solution.py:51
  17.1 8.6 %collective-permute-start.12 = (bf16[32,3712]{1,0:T(8,128)(2,1)S(1)}, bf16[32,3712]{1,0:T(8,128)(2,1)S(1)}, u32[]{:S(2)}, u32[]{:S(2)}) collective-permute-start(bf16[32,3712]{1,0:T(8,128)(2,1)S(1)} %collective-permute-done.8.refs_8_), channel_id=1, source_target_pairs={{0,1},{4,12},{1,2},{5,4},{2,3},{6,5},{3,11},{7,6},{11,10},{15,7},{... | collective-permute-start | bytes 712712 | tf_op jit(solution)/shard_map/ppermute | solution.py:51
  22.7 7.3 %collective-permute-start.14 = (bf16[32,3712]{1,0:T(8,128)(2,1)S(1)}, bf16[32,3712]{1,0:T(8,128)(2,1)S(1)}, u32[]{:S(2)}, u32[]{:S(2)}) collective-permute-start(bf16[32,3712]{1,0:T(8,128)(2,1)S(1)} %collective-permute-done.10.refs_2_), channel_id=1, source_target_pairs={{0,8},{4,5},{1,0},{5,6},{2,1},{6,7},{3,2},{7,15},{11,3},{15,14},{1... | collective-permute-start | bytes 712712 | tf_op jit(solution)/shard_map/ppermute | solution.py:51
  24.0 11.4 %collective-permute-start.1 = (bf16[32,128]{1,0:T(8,128)(2,1)S(1)}, bf16[32,128]{1,0:T(8,128)(2,1)S(1)}, u32[]{:S(2)}, u32[]{:S(2)}) collective-permute-start(bf16[32,128]{1,0:T(8,128)(2,1)S(1)} %pad_maximum_fusion.1), channel_id=1, source_target_pairs={{0,4},{4,0},{1,5},{5,1},{2,6},{6,2},{3,7},{7,3},{11,15},{15,11},{1... | collective-permute-start | bytes 24584 | tf_op jit(solution)/shard_map/ppermute | solution.py:51
  24.0 12.0 %collective-permute-start = (bf16[32,3584]{1,0:T(8,128)(2,1)}, bf16[32,3584]{1,0:T(8,128)(2,1)S(1)}, u32[]{:S(2)}, u32[]{:S(2)}) collective-permute-start(bf16[32,3584]{1,0:T(8,128)(2,1)} %param.8), channel_id=1, source_target_pairs={{0,4},{4,0},{1,5},{5,1},{2,6},{6,2},{3,7},{7,3},{11,15},{15,11},{1... | collective-permute-start | bytes 688136 | tf_op jit(solution)/shard_map/ppermute | solution.py:51
  25.7 4.8 %collective-permute-start.16 = (bf16[32,1792]{1,0:T(8,128)(2,1)S(1)}, bf16[32,1792]{1,0:T(8,128)(2,1)S(1)}, u32[]{:S(2)}, u32[]{:S(2)}) collective-permute-start(bf16[32,1792]{1,0:T(8,128)(2,1)S(1)} %slice.48), channel_id=1, source_target_pairs={{0,1},{4,12},{1,2},{5,4},{2,3},{6,5},{3,11},{7,6},{11,10},{15,7},{... | collective-permute-start | bytes 344072 | tf_op jit(solution)/shard_map/ppermute | solution.py:51
  28.6 7.5 %collective-permute-start.4 = (bf16[32,3712]{1,0:T(8,128)(2,1)S(1)}, bf16[32,3712]{1,0:T(8,128)(2,1)S(1)}, u32[]{:S(2)}, u32[]{:S(2)}) collective-permute-start(bf16[32,3712]{1,0:T(8,128)(2,1)S(1)} %constant_dynamic-update-slice_fusion.refs_4_), channel_id=1, source_target_pairs={{0,4},{4,0},{1,5},{5,1},{2,6},{6,2},{3,7},{7,3},{11,15},{15,11},{1... | collective-permute-start | bytes 712712 | tf_op jit(solution)/shard_map/ppermute | solution.py:51
  30.1 6.5 %collective-permute-start.7 = (bf16[32,3712]{1,0:T(8,128)(2,1)S(1)}, bf16[32,3712]{1,0:T(8,128)(2,1)S(1)}, u32[]{:S(2)}, u32[]{:S(2)}) collective-permute-start(bf16[32,3712]{1,0:T(8,128)(2,1)S(1)} %constant_dynamic-update-slice_fusion.2.refs_6_), channel_id=1, source_target_pairs={{0,4},{4,0},{1,5},{5,1},{2,6},{6,2},{3,7},{7,3},{11,15},{15,11},{1... | collective-permute-start | bytes 712712 | tf_op jit(solution)/shard_map/ppermute | solution.py:51
  30.5 4.9 %collective-permute-start.17 = (bf16[32,1920]{1,0:T(8,128)(2,1)S(1)}, bf16[32,1920]{1,0:T(8,128)(2,1)S(1)}, u32[]{:S(2)}, u32[]{:S(2)}) collective-permute-start(bf16[32,1920]{1,0:T(8,128)(2,1)S(1)} %slice.49), channel_id=1, source_target_pairs={{0,8},{4,5},{1,0},{5,6},{2,1},{6,7},{3,2},{7,15},{11,3},{15,14},{1... | collective-permute-start | bytes 368648 | tf_op jit(solution)/shard_map/ppermute | solution.py:51
  35.4 1.5 %collective-permute-start.9 = (bf16[32,3712]{1,0:T(8,128)(2,1)S(1)}, bf16[32,3712]{1,0:T(8,128)(2,1)S(1)}, u32[]{:S(2)}, u32[]{:S(2)}) collective-permute-start(bf16[32,3712]{1,0:T(8,128)(2,1)S(1)} %collective-permute-done.8.refs_8_), channel_id=1, source_target_pairs={{0,4},{4,0},{1,5},{5,1},{2,6},{6,2},{3,7},{7,3},{11,15},{15,11},{1... | collective-permute-start | bytes 712712 | tf_op jit(solution)/shard_map/ppermute | solution.py:51
  35.4 10.2 %collective-permute-start.11 = (bf16[32,3712]{1,0:T(8,128)(2,1)S(1)}, bf16[32,3712]{1,0:T(8,128)(2,1)S(1)}, u32[]{:S(2)}, u32[]{:S(2)}) collective-permute-start(bf16[32,3712]{1,0:T(8,128)(2,1)S(1)} %collective-permute-done.10.refs_2_), channel_id=1, source_target_pairs={{0,4},{4,0},{1,5},{5,1},{2,6},{6,2},{3,7},{7,3},{11,15},{15,11},{1... | collective-permute-start | bytes 712712 | tf_op jit(solution)/shard_map/ppermute | solution.py:51
  36.0 10.1 %collective-permute-start.13 = (bf16[32,3712]{1,0:T(8,128)(2,1)S(1)}, bf16[32,3712]{1,0:T(8,128)(2,1)S(1)}, u32[]{:S(2)}, u32[]{:S(2)}) collective-permute-start(bf16[32,3712]{1,0:T(8,128)(2,1)S(1)} %collective-permute-done.12.refs_4_), channel_id=1, source_target_pairs={{0,4},{4,0},{1,5},{5,1},{2,6},{6,2},{3,7},{7,3},{11,15},{15,11},{1... | collective-permute-start | bytes 712712 | tf_op jit(solution)/shard_map/ppermute | solution.py:51
  36.1 10.0 %collective-permute-start.15 = (bf16[32,3712]{1,0:T(8,128)(2,1)S(1)}, bf16[32,3712]{1,0:T(8,128)(2,1)S(1)}, u32[]{:S(2)}, u32[]{:S(2)}) collective-permute-start(bf16[32,3712]{1,0:T(8,128)(2,1)S(1)} %collective-permute-done.14.refs_6_), channel_id=1, source_target_pairs={{0,4},{4,0},{1,5},{5,1},{2,6},{6,2},{3,7},{7,3},{11,15},{15,11},{1... | collective-permute-start | bytes 712712 | tf_op jit(solution)/shard_map/ppermute | solution.py:51
  36.5 9.6 %collective-permute-start.18 = (bf16[32,3712]{1,0:T(8,128)(2,1)S(1)}, bf16[32,3712]{1,0:T(8,128)(2,1)S(1)}, u32[]{:S(2)}, u32[]{:S(2)}) collective-permute-start(bf16[32,3712]{1,0:T(8,128)(2,1)S(1)} %constant_dynamic-update-slice_fusion.4.refs_8_), channel_id=1, source_target_pairs={{0,4},{4,0},{1,5},{5,1},{2,6},{6,2},{3,7},{7,3},{11,15},{15,11},{1... | collective-permute-start | bytes 712712 | tf_op jit(solution)/shard_map/ppermute | solution.py:51
  36.6 8.9 %copy-start.6 = (bf16[128,512]{1,0:T(8,128)(2,1)S(1)}, bf16[128,512]{1,0:T(8,128)(2,1)}, u32[]{:S(2)}) copy-start(bf16[128,512]{1,0:T(8,128)(2,1)} %refs_10_.3) | copy-start | bytes 393220
  36.9 8.6 %collective-permute-start.20 = (bf16[128,512]{1,0:T(8,128)(2,1)}, bf16[128,512]{1,0:T(8,128)(2,1)S(1)}, u32[]{:S(2)}, u32[]{:S(2)}) collective-permute-start(bf16[128,512]{1,0:T(8,128)(2,1)} %refs_10_.3), channel_id=1, source_target_pairs={{0,8},{4,12},{8,0},{12,4},{1,9},{5,13},{9,1},{13,5},{2,10},{6,14},... | collective-permute-start | bytes 393224 | tf_op jit(solution)/shard_map/ppermute | solution.py:329
  37.7 3.1 %copy-start = (bf16[2,512,3584]{2,1,0:T(8,128)(2,1)S(1)}, bf16[2,512,3584]{2,1,0:T(8,128)(2,1)}, u32[]{:S(2)}) copy-start(bf16[2,512,3584]{2,1,0:T(8,128)(2,1)} %refs_12_.1) | copy-start | bytes 22020100
  40.8 0.7 copy-start.3
  41.4 4.7 %copy-start.1 = (bf16[2,512,3584]{2,1,0:T(8,128)(2,1)S(1)}, bf16[2,512,3584]{2,1,0:T(8,128)(2,1)}, u32[]{:S(2)}) copy-start(bf16[2,512,3584]{2,1,0:T(8,128)(2,1)} %refs_12_.1) | copy-start | bytes 22020100
  45.5 12.0 %collective-permute-start.19 = (bf16[128,512]{1,0:T(8,128)(2,1)S(1)}, bf16[128,512]{1,0:T(8,128)(2,1)S(1)}, u32[]{:S(2)}, u32[]{:S(2)}) collective-permute-start(bf16[128,512]{1,0:T(8,128)(2,1)S(1)} %copy-done.6), channel_id=1, source_target_pairs={{0,4},{4,0},{8,12},{12,8},{1,5},{5,1},{9,13},{13,9},{2,6},{6,2},{1... | collective-permute-start | bytes 393224 | tf_op jit(solution)/shard_map/ppermute | solution.py:330
  45.6 11.9 %collective-permute-start.21 = (bf16[128,512]{1,0:T(8,128)(2,1)S(1)}, bf16[128,512]{1,0:T(8,128)(2,1)S(1)}, u32[]{:S(2)}, u32[]{:S(2)}) collective-permute-start(bf16[128,512]{1,0:T(8,128)(2,1)S(1)} %collective-permute-done.20.refs_12_), channel_id=1, source_target_pairs={{0,4},{4,0},{8,12},{12,8},{1,5},{5,1},{9,13},{13,9},{2,6},{6,2},{1... | collective-permute-start | bytes 393224 | tf_op jit(solution)/shard_map/ppermute | solution.py:330
  46.1 11.4 %copy-start.4 = (s32[16]{0:T(128)S(1)}, s32[16]{0:T(128)}, u32[]{:S(2)}) copy-start(s32[16]{0:T(128)} %refs_0_.5) | copy-start | bytes 196
  46.1 11.4 %copy-start.5 = (bf16[512,3584]{1,0:T(8,128)(2,1)S(1)}, bf16[512,3584]{1,0:T(8,128)(2,1)}, u32[]{:S(2)}) copy-start(bf16[512,3584]{1,0:T(8,128)(2,1)} %refs_14_.1) | copy-start | bytes 11010052
  50.2 18.9 %collective-permute-start.23 = (f32[4,4,2,32]{3,2,0,1:T(2,128)S(1)}, f32[4,4,2,32]{3,2,0,1:T(2,128)S(1)}, u32[]{:S(2)}, u32[]{:S(2)}) collective-permute-start(f32[4,4,2,32]{3,2,0,1:T(2,128)S(1)} %copy.16), channel_id=1, source_target_pairs={{0,2},{1,3},{2,0},{3,1},{4,6},{5,7},{6,4},{7,5},{8,10},{9,11},{10,... | collective-permute-start | bytes 12296 | tf_op jit(solution)/shard_map/ppermute | solution.py:347
  53.7 15.4 %collective-permute-start.22 = (f32[4,4,2,32]{3,2,0,1:T(2,128)S(1)}, f32[4,4,2,32]{3,2,0,1:T(2,128)S(1)}, u32[]{:S(2)}, u32[]{:S(2)}) collective-permute-start(f32[4,4,2,32]{3,2,0,1:T(2,128)S(1)} %copy.16), channel_id=1, source_target_pairs={{0,1},{1,2},{2,3},{3,0},{4,5},{5,6},{6,7},{7,4},{8,9},{9,10},{10,1... | collective-permute-start | bytes 12296 | tf_op jit(solution)/shard_map/ppermute | solution.py:347
  55.3 13.8 %collective-permute-start.24 = (f32[4,4,2,32]{3,2,0,1:T(2,128)S(1)}, f32[4,4,2,32]{3,2,0,1:T(2,128)S(1)}, u32[]{:S(2)}, u32[]{:S(2)}) collective-permute-start(f32[4,4,2,32]{3,2,0,1:T(2,128)S(1)} %copy.16), channel_id=1, source_target_pairs={{0,3},{1,0},{2,1},{3,2},{4,7},{5,4},{6,5},{7,6},{8,11},{9,8},{10,9... | collective-permute-start | bytes 12296 | tf_op jit(solution)/shard_map/ppermute | solution.py:347
  57.5 15.6 %copy-start.7 = (s32[32,8]{0,1:T(8,128)S(1)}, s32[32,8]{0,1:T(8,128)}, u32[]{:S(2)}) copy-start(s32[32,8]{0,1:T(8,128)} %param.11) | copy-start | bytes 3076
  69.2 1.4 %collective-permute-start.27 = (f32[4,2,32]{2,1,0:T(2,128)S(1)}, f32[4,2,32]{2,1,0:T(2,128)S(1)}, u32[]{:S(2)}, u32[]{:S(2)}) collective-permute-start(f32[4,2,32]{2,1,0:T(2,128)S(1)} %bitcast.24), channel_id=1, source_target_pairs={{0,12},{4,0},{8,4},{12,8},{1,13},{5,1},{9,5},{13,9},{2,14},{6,2},{... | collective-permute-start | bytes 3080 | tf_op jit(solution)/shard_map/ppermute | solution.py:350
  69.2 3.7 %collective-permute-start.26 = (f32[4,2,32]{2,1,0:T(2,128)S(1)}, f32[4,2,32]{2,1,0:T(2,128)S(1)}, u32[]{:S(2)}, u32[]{:S(2)}) collective-permute-start(f32[4,2,32]{2,1,0:T(2,128)S(1)} %bitcast.25), channel_id=1, source_target_pairs={{0,8},{4,12},{8,0},{12,4},{1,9},{5,13},{9,1},{13,5},{2,10},{6,14},... | collective-permute-start | bytes 3080 | tf_op jit(solution)/shard_map/ppermute | solution.py:350
  70.1 3.0 %collective-permute-start.25 = (f32[4,2,32]{2,1,0:T(2,128)S(1)}, f32[4,2,32]{2,1,0:T(2,128)S(1)}, u32[]{:S(2)}, u32[]{:S(2)}) collective-permute-start(f32[4,2,32]{2,1,0:T(2,128)S(1)} %bitcast.26), channel_id=1, source_target_pairs={{0,4},{4,8},{8,12},{12,0},{1,5},{5,9},{9,13},{13,1},{2,6},{6,10},{... | collective-permute-start | bytes 3080 | tf_op jit(solution)/shard_map/ppermute | solution.py:350

commit v3 on v1

v3 whole, which is shorter than its diff:
```python
import jax
import jax.numpy as jnp
from jax import lax
from jax.experimental import pallas as pl
from jax.experimental.pallas import tpu as pltpu
from jax.sharding import PartitionSpec as P

MEAN_LENGTH = 32.0
AXES = ("node", "local")
F32 = jnp.float32
BF16 = jnp.bfloat16


def dot(a, b, ca, cb):
    return lax.dot_general(a, b, (((ca,), (cb,)), ((), ())), preferred_element_type=F32)


def ring_places(node_count, local_count):
    chips = []
    for y in range(node_count // 2):
        row = range(local_count) if y % 2 == 0 else range(local_count - 1, -1, -1)
        chips += [(y, z) for z in row]
    return chips


def ring_shift(node_count, local_count, step):
    chips = ring_places(node_count, local_count)
    pairs = []
    for r, chip in enumerate(chips):
        to = chips[(r + step) % len(chips)]
        for core in (0, 1):
            pairs.append(
                ((chip[0] * 2 + core) * local_count + chip[1], (to[0] * 2 + core) * local_count + to[1])
            )
    return pairs


def block_numbers(node, local, node_count, local_count):
    total = node_count // 2 * local_count
    y, core = node // 2, node % 2
    mine = y * local_count + jnp.where(y % 2 == 0, local, local_count - 1 - local)
    offsets = [0]
    for step in range(1, (total - 1) // 2 + 1):
        offsets += [-step, step]
    offsets.append(total // 2)
    numbers = []
    for offset in offsets:
        at = (mine + offset + total) % total
        at_y, at_z = at // local_count, at % local_count
        at_z = jnp.where(at_y % 2 == 0, at_z, local_count - 1 - at_z)
        for at_core in (core, 1 - core):
            numbers.append((at_y * 2 + at_core) * local_count + at_z)
    return numbers


def lengths_at(lens_ref, tokens):
    found = jnp.zeros(tokens.shape, jnp.int32)
    end = 0
    for r in range(lens_ref.shape[0]):
        found = jnp.where(tokens >= end, lens_ref[r], found)
        end = end + lens_ref[r]
    return found.astype(F32)


VMEM = pl.BlockSpec(memory_space=pltpu.VMEM)
SMEM = pl.BlockSpec(memory_space=pltpu.SMEM)
ANY = pl.BlockSpec(memory_space=pl.ANY)
MIB = 2**20
WEIGHTS_FLOPS = 20 * 10**9
HALF_FLOPS = 6 * 10**9
SHARED_FLOPS = 3 * 10**9
PACK_MIB = 50
LAST_MIB = 40
ROWS_BYTES = 66 * MIB
LITTLE = pl.CostEstimate(flops=10**6, bytes_accessed=10**4, transcendentals=0)


def numbers_at(numbers, tokens, here):
    token = lax.broadcasted_iota(jnp.int32, (1, tokens), 1)
    found = jnp.zeros((1, tokens), jnp.int32)
    for b, number in enumerate(numbers):
        found = jnp.where(token >= b * here, number, found)
    return found


def pack_call(out_grad, gates, ids):
    here, features = out_grad.shape
    choices = gates.shape[0]

    def kernel(rows_ref, gates_ref, ids_ref, out_ref, gates_scr, ids_scr, sems):
        pairs = ((gates_ref, gates_scr), (ids_ref, ids_scr), (rows_ref, out_ref.at[:, :features]))
        copies = [pltpu.make_async_copy(a, b, sems.at[n]) for n, (a, b) in enumerate(pairs)]
        for copy in copies:
            copy.start()
        for copy in copies[:2]:
            copy.wait()
        pad = jnp.zeros((128 - 2 * choices, here), F32)
        tags = jnp.concatenate([gates_scr[...].astype(F32), ids_scr[...].astype(F32), pad], axis=0)
        out_ref[:, features:] = tags.T.astype(BF16)
        copies[2].wait()

    return pl.pallas_call(
        kernel,
        out_shape=jax.ShapeDtypeStruct((here, features + 128), BF16),
        in_specs=[ANY] * 3,
        out_specs=VMEM,
        scratch_shapes=[
            pltpu.VMEM(gates.shape, gates.dtype),
            pltpu.VMEM(ids.shape, ids.dtype),
            pltpu.SemaphoreType.DMA((3,)),
        ],
        compiler_params=pltpu.CompilerParams(vmem_limit_bytes=PACK_MIB * MIB),
        cost_estimate=LITTLE,
        name="pack",
    )(out_grad, gates, ids)


def weights_call(counts, lengths, where, shared):
    node_tokens, _ = shared.shape
    here = node_tokens // counts[1]
    tokens = counts[0] * node_tokens

    def kernel(lens_ref, where_ref, shared_ref, weight_ref, out_ref):
        node, local = where_ref[0], where_ref[1]
        number = numbers_at(block_numbers(node, local, *counts), tokens, here)
        token = lax.broadcasted_iota(jnp.int32, (1, tokens), 1)
        row = lax.broadcasted_iota(jnp.int32, (8, tokens), 0)
        weight = MEAN_LENGTH / lengths_at(lens_ref, number * here + token % here)
        near = MEAN_LENGTH / lengths_at(lens_ref, node * node_tokens + token % node_tokens)
        weight_ref[...] = jnp.where(row == 0, weight, near)
        spread = lax.broadcasted_iota(jnp.int32, (node_tokens, 128), 0)
        column = MEAN_LENGTH / lengths_at(lens_ref, node * node_tokens + spread)[:, :1]
        out_ref[...] = (shared_ref[...].astype(F32) * column).astype(BF16)

    return pl.pallas_call(
        kernel,
        out_shape=(jax.ShapeDtypeStruct((8, tokens), F32), jax.ShapeDtypeStruct(shared.shape, BF16)),
        in_specs=[SMEM, SMEM, VMEM],
        out_specs=[VMEM] * 2,
        compiler_params=pltpu.CompilerParams(vmem_limit_bytes=4 * MIB),
        cost_estimate=pl.CostEstimate(flops=WEIGHTS_FLOPS, bytes_accessed=10**6, transcendentals=0),
        name="weights",
    )(lengths, where, shared)


def place(node, numbers, capacity, blocks, weight, hidden_ref, features, choices):
    here = blocks[0].shape[0]
    tokens = here * len(blocks)
    experts, slot_total, _ = hidden_ref.shape
    tags = jnp.concatenate([block[:, features:] for block in blocks], axis=0).astype(F32).T
    gates, ids = tags[:choices], tags[choices : 2 * choices]
    number = numbers_at(numbers, tokens, here).astype(F32)
    token = lax.broadcasted_iota(jnp.int32, (1, tokens), 1)
    first = token - token % here
    down = lax.broadcasted_iota(jnp.int32, (tokens, 1), 0)
    earlier = ((down < token) & (down >= first)).astype(F32).astype(BF16)
    named = [ids == (node * experts + e).astype(F32) for e in range(experts)]
    hits = [jnp.sum(n.astype(F32), axis=0, keepdims=True) for n in named]
    gate = [jnp.sum(jnp.where(n, gates, 0.0), axis=0, keepdims=True) for n in named]
    row = lax.broadcasted_iota(jnp.int32, (8, tokens), 0)
    stacked = jnp.zeros((8, tokens), F32)
    for e in range(experts):
        stacked = jnp.where(row == e, hits[e], stacked)
    ranks = dot(stacked.astype(BF16), earlier, 1, 0)
    slot = lax.broadcasted_iota(jnp.int32, (slot_total, 1), 0).astype(F32)
    info = jnp.zeros((8, tokens), F32)
    placed, scaled = [], []
    for e in range(experts):
        rank = ranks[e : e + 1]
        live = (hits[e] > 0.5) & (rank < capacity - 0.5)
        cell = jnp.where(live, number * capacity + rank, -1.0)
        info = jnp.where(row == e, cell, info)
        info = jnp.where(row == experts + e, gate[e], info)
        placing = (slot == cell).astype(F32).astype(BF16)
        hidden = dot(hidden_ref[e], placing, 0, 0)
        placed.append(hidden.astype(BF16))
        scaled.append((hidden * (gate[e] * weight)).astype(BF16))
    return info, placed, scaled


def half_call(counts, capacity, choices, start, where, weights, blocks, down, hidden, rows, sums):
    experts, units, features = down.shape
    count, here = len(blocks), blocks[0].shape[0]
    tokens = here * count
    device_count = counts[0] * counts[1]
    first = start * here
    step = 256 if units % 256 == 0 else units
    more = [] if rows is None else [rows, sums]

    def kernel(where_ref, *refs):
        blocks, (weights_ref, down_ref, hidden_ref), refs = refs[:count], refs[count : count + 3], refs[count + 3 :]
        before, refs = refs[: len(more)], refs[len(more) :]
        rows_ref, grad_ref, scaled_ref, info_ref, sums_ref, x_scr, grad_scr, scaled_scr, placed_scr, sems = refs
        copies = []

        def write(scr, ref):
            copies.append(pltpu.make_async_copy(scr, ref, sems.at[len(copies)]))
            copies[-1].start()

        node, local = where_ref[0], where_ref[1]
        numbers = block_numbers(node, local, *counts)[start : start + count]
        for b, block in enumerate(blocks):
            x_scr[b * here : (b + 1) * here, :] = block[:, :features]
        write(x_scr, rows_ref.at[pl.ds(first, tokens)])
        weight = weights_ref[:1, first : first + tokens]
        info, placed, scaled = place(node, numbers, capacity, blocks, weight, hidden_ref, features, choices)
        info_ref[...] = info
        for e in range(experts):
            scaled_scr[e] = scaled[e]
            placed_scr[e] = placed[e]
        write(scaled_scr, scaled_ref)
        row = lax.broadcasted_iota(jnp.int32, (8, tokens), 0)
        total = jnp.zeros((8, tokens), F32)
        for e in range(experts):
            for i in range(0, units, step):
                at = slice(i, i + step)
                back = dot(down_ref[e, at, :], x_scr[...], 1, 1) * weight
                grad_scr[e, at, :] = back.astype(BF16)
                found = jnp.sum(back * placed_scr[e, at, :].astype(F32), axis=0, keepdims=True)
                total = total + jnp.where(row == e, found, 0.0)
            write(grad_scr.at[e], grad_ref.at[e])
        if more:
            sums_ref[...] = before[1][...]
        else:
            sums_ref[...] = jnp.zeros(sums_ref.shape, F32)
        for b, number in enumerate(numbers):
            sums_ref[number] = total[:experts, b * here : (b + 1) * here]
        for copy in copies:
            copy.wait()

    return pl.pallas_call(
        kernel,
        out_shape=(
            jax.ShapeDtypeStruct((-(-ROWS_BYTES // (2 * features)), features), BF16),
            jax.ShapeDtypeStruct((experts, units, tokens), BF16),
            jax.ShapeDtypeStruct((experts, units, tokens), BF16),
            jax.ShapeDtypeStruct((8, tokens), F32),
            jax.ShapeDtypeStruct((device_count, experts, here), F32),
        ),
        in_specs=[SMEM] + [VMEM] * (count + 3) + [ANY, VMEM][: len(more)],
        out_specs=[ANY, ANY, ANY, VMEM, VMEM],
        input_output_aliases={count + 4: 0} if more else {},
        scratch_shapes=[
            pltpu.VMEM((tokens, features), BF16),
            pltpu.VMEM((experts, units, tokens), BF16),
            pltpu.VMEM((experts, units, tokens), BF16),
            pltpu.VMEM((experts, units, tokens), BF16),
            pltpu.SemaphoreType.DMA((2 + experts,)),
        ],
        compiler_params=pltpu.CompilerParams(vmem_limit_bytes=12 * MIB),
        cost_estimate=pl.CostEstimate(flops=HALF_FLOPS, bytes_accessed=10**6, transcendentals=0),
        name="half_second" if more else "half_first",
    )(where, *blocks, weights, down, hidden, *more)


def last_call(counts, slot_total, where, rows, first, second, shared):
    experts, units, tokens = first[1].shape
    features = rows.shape[1]
    node_tokens, shared_units = shared[0].shape
    width = features // counts[0]
    here = node_tokens // counts[1]
    step = 256 if units % 256 == 0 else units
    parts = units // step

    def kernel(where_ref, rows_ref, *refs):
        given, (info_a, info_b), shared, refs = refs[:4], refs[4:6], refs[6:10], refs[10:]
        down_ref, hidden_ref, shared_ref = refs[:3]
        x_scr, grad_scr, scaled_scr, all_scr, ordered_scr, down_scr, hidden_scr, shared_scr, sems, out_sems = refs[3:]
        loads, copies = [], []

        def load(ref, scr):
            loads.append(pltpu.make_async_copy(ref, scr, sems.at[len(loads)]))
            loads[-1].start()

        def write(scr, ref):
            copies.append(pltpu.make_async_copy(scr, ref, out_sems.at[len(copies)]))
            copies[-1].start()

        for ref, scr in zip(given, (grad_scr, grad_scr, scaled_scr, scaled_scr)):
            load(ref, scr.at[:, :, pl.ds(len(loads) % 2 * tokens, tokens)])
        load(rows_ref.at[pl.ds(0, 2 * tokens)], x_scr)
        node, local = where_ref[0], where_ref[1]
        for n, part in enumerate(shared):
            at = pl.multiple_of((node ^ n) * node_tokens, node_tokens)
            all_scr[pl.ds(at, node_tokens), :] = part[...]
        for b, number in enumerate(block_numbers(node, local, *counts)):
            of = pl.ds(pl.multiple_of(number * here, here), here)
            ordered_scr[b * here : (b + 1) * here, :] = all_scr[of, :]
        slot = lax.broadcasted_iota(jnp.int32, (slot_total, 1), 0).astype(F32)

        def by_slot(e):
            gated = []
            for info in (info_a, info_b):
                gate = info[experts + e : experts + e + 1, :]
                gated.append(jnp.where(slot == info[e : e + 1, :], gate, 0.0).astype(BF16))
            hidden_scr[e] = dot(jnp.concatenate(gated, axis=1), grad_scr[e], 1, 1).astype(BF16)
            write(hidden_scr.at[e], hidden_ref.at[e])

        for copy in loads[:2]:
            copy.wait()
        for e in range(experts - 1):
            by_slot(e)
        for copy in loads[2:]:
            copy.wait()
        for e in range(experts):
            for n in range(parts):
                at = slice(n * step, (n + 1) * step)
                place = down_scr.at[e * parts + n]
                place[...] = dot(scaled_scr[e, at, :], x_scr[...], 1, 0).astype(BF16)
                write(place, down_ref.at[e, pl.ds(n * step, step)])
        columns = pl.ds(pl.multiple_of(node * width, width), width)
        shared_scr[...] = dot(ordered_scr[...], x_scr[:, columns], 0, 0).astype(BF16)
        write(shared_scr, shared_ref)
        by_slot(experts - 1)
        for copy in copies:
            copy.wait()

    return pl.pallas_call(
        kernel,
        out_shape=(
            jax.ShapeDtypeStruct((experts, units, features), BF16),
            jax.ShapeDtypeStruct((experts, slot_total, units), BF16),
            jax.ShapeDtypeStruct((shared_units, width), BF16),
        ),
        in_specs=[SMEM] + [ANY] * 5 + [VMEM] * 6,
        out_specs=[ANY] * 3,
        scratch_shapes=[
            pltpu.VMEM((2 * tokens, features), BF16),
            pltpu.VMEM((experts, units, 2 * tokens), BF16),
            pltpu.VMEM((experts, units, 2 * tokens), BF16),
            pltpu.VMEM((4 * node_tokens, shared_units), BF16),
            pltpu.VMEM((4 * node_tokens, shared_units), BF16),
            pltpu.VMEM((experts * parts, step, features), BF16),
            pltpu.VMEM((experts, slot_total, units), BF16),
            pltpu.VMEM((shared_units, width), BF16),
            pltpu.SemaphoreType.DMA((5,)),
            pltpu.SemaphoreType.DMA((experts * parts + experts + 1,)),
        ],
        compiler_params=pltpu.CompilerParams(vmem_limit_bytes=LAST_MIB * MIB),
        cost_estimate=pl.CostEstimate(flops=8 * 10**9, bytes_accessed=10**7, transcendentals=0),
        name="last",
    )(where, rows, first[1], second[1], first[2], second[2], first[3], second[3], *shared)


def shared_back_call(counts, where, weights, blocks, down):
    units, features = down.shape
    here = blocks[0].shape[0]
    tokens = here * counts[1]

    def kernel(where_ref, *refs):
        blocks, (weights_ref, down_ref, out_ref, near_scr) = refs[:-4], refs[-4:]
        node, local = where_ref[0], where_ref[1]
        for block, number in zip(blocks, block_numbers(node, local, *counts)[::2]):

            @pl.when(number // counts[1] == node)
            def _(block=block, number=number):
                to = pl.ds(pl.multiple_of(number % counts[1] * here, here), here)
                near_scr[to, :] = block[:, :features]

        back = dot(down_ref[...], near_scr[...], 1, 1) * weights_ref[1:2, :tokens]
        out_ref[...] = back.T.astype(BF16)

    return pl.pallas_call(
        kernel,
        out_shape=jax.ShapeDtypeStruct((tokens, units), BF16),
        in_specs=[SMEM] + [VMEM] * (len(blocks) + 2),
        out_specs=VMEM,
        scratch_shapes=[pltpu.VMEM((tokens, features), BF16)],
        compiler_params=pltpu.CompilerParams(vmem_limit_bytes=12 * MIB),
        cost_estimate=pl.CostEstimate(flops=SHARED_FLOPS, bytes_accessed=10**6, transcendentals=0),
        name="shared_back",
    )(where, *blocks, weights, down)


def gates_call(counts, parts, ids):
    experts = parts.shape[1]

    def kernel(ids_ref, parts_ref, out_ref):
        d_gate = jnp.zeros(out_ref.shape, F32)
        for node in range(counts[0]):
            total = parts_ref[node * counts[1]]
            for local in range(1, counts[1]):
                total = total + parts_ref[node * counts[1] + local]
            for e in range(experts):
                d_gate = d_gate + jnp.where(ids_ref[...] == node * experts + e, total[e : e + 1], 0.0)
        out_ref[...] = d_gate

    return pl.pallas_call(
        kernel,
        out_shape=jax.ShapeDtypeStruct(ids.shape, F32),
        in_specs=[VMEM] * 2,
        out_specs=VMEM,
        compiler_params=pltpu.CompilerParams(vmem_limit_bytes=4 * MIB),
        cost_estimate=LITTLE,
        name="gates",
    )(ids, parts)


def exchanged(a):
    return lax.all_to_all(a, AXES, split_axis=0, concat_axis=0, tiled=True)


def wide_body(
    out_grad,
    lengths,
    gate_weights,
    expert_ids,
    hidden_routed,
    down_routed,
    hidden_shared,
    down_shared,
):
    node_count = lax.axis_size("node")
    local_count = lax.axis_size("local")
    device_count = node_count * local_count
    here, features = out_grad.shape
    choices = expert_ids.shape[1]
    experts, slot_total, units = hidden_routed.shape
    capacity = slot_total // device_count
    node = lax.axis_index("node")
    pad = jnp.zeros((here, 128 - 2 * choices), BF16)
    packed = jnp.concatenate([out_grad, gate_weights, expert_ids.astype(BF16), pad], axis=1)
    rows = lax.all_gather(packed, AXES, axis=0, tiled=True)
    token_total = device_count * here
    ends = jnp.cumsum(lengths)
    places = jnp.arange(token_total, dtype=jnp.int32)
    inside = (places[:, None] >= (ends - lengths)[None, :]) & (places[:, None] < ends[None, :])
    weight = MEAN_LENGTH / jnp.sum(jnp.where(inside, lengths[None, :], 0), axis=1).astype(F32)
    x = rows[:, :features]
    gates = rows[:, features : features + choices].astype(F32)
    ids = rows[:, features + choices : features + 2 * choices].astype(jnp.int32)
    d_hidden, d_down, sums = [], [], []
    for e in range(experts):
        named = ids == node * experts + e
        hit = jnp.any(named, axis=1)
        gate = jnp.sum(jnp.where(named, gates, 0.0), axis=1)
        hits = hit.astype(jnp.int32).reshape(device_count, here)
        rank = (jnp.cumsum(hits, axis=1) - hits).reshape(-1)
        cell = places // here * capacity + rank
        cell = jnp.where(hit & (rank < capacity), cell, -1)
        placing = jnp.arange(slot_total, dtype=jnp.int32)[:, None] == cell[None, :]
        placing = placing.astype(BF16)
        hidden = dot(hidden_routed[e], placing, 0, 0)
        back = dot(down_routed[e], x, 1, 1) * weight[None, :]
        sums.append(jnp.sum(hidden * back, axis=0))
        gated = placing * gate.astype(BF16)[None, :]
        d_hidden.append(dot(gated, back.astype(BF16), 1, 1).astype(BF16))
        scaled = (hidden * (gate * weight)[None, :]).astype(BF16)
        d_down.append(dot(scaled, x, 1, 0).astype(BF16))
    slot_grad = jnp.stack(sums).reshape(experts, device_count, here)
    where = jnp.stack([node, lax.axis_index("local")]).astype(jnp.int32)
    d_gate = gates_call((node_count, local_count), exchanged(jnp.swapaxes(slot_grad, 0, 1)), expert_ids.T).T
    near_total = local_count * here
    near = lax.dynamic_slice_in_dim(x, node * near_total, near_total, 0)
    near_weight = lax.dynamic_slice_in_dim(weight, node * near_total, near_total, 0)
    shared_back = dot(near, down_shared, 1, 1)
    d_hidden_shared = (shared_back * near_weight[:, None]).astype(BF16)
    columns = features // node_count
    mine = lax.dynamic_slice_in_dim(x, node * columns, columns, 1)
    shared = lax.all_gather(hidden_shared, "node", axis=0, tiled=True)
    shared = (shared.astype(F32) * weight[:, None]).astype(BF16)
    d_down_shared = dot(shared, mine, 0, 0).astype(BF16)
    return (jnp.stack(d_hidden), jnp.stack(d_down), d_gate, d_hidden_shared, d_down_shared)


def body(
    out_grad,
    lengths,
    gate_weights,
    expert_ids,
    hidden_routed,
    down_routed,
    hidden_shared,
    down_shared,
):
    counts = lax.axis_size("node"), lax.axis_size("local")
    device_count = counts[0] * counts[1]
    here, features = out_grad.shape
    choices = expert_ids.shape[1]
    slot_total = hidden_routed.shape[1]
    capacity = slot_total // device_count
    where = jnp.stack([lax.axis_index("node"), lax.axis_index("local")]).astype(jnp.int32)
    up, down = ring_shift(*counts, 1), ring_shift(*counts, -1)

    def send(a, pairs):
        return lax.ppermute(a, AXES, pairs)

    def swapped(a):
        return lax.ppermute(a, "node", [(n, n ^ 1) for n in range(counts[0])])

    together = lax.optimization_barrier
    packed, where = together((pack_call(out_grad, gate_weights.T, expert_ids.T), where))
    forth, back, other = [packed], [packed], [swapped(packed)]
    weights, shared = weights_call(counts, lengths, where, hidden_shared)
    for step in range(3):
        forth.append(send(forth[-1], up))
        back.append(send(back[-1], down))
        other += [swapped(forth[-1]), swapped(back[-1])]
        if step == 0:
            back[-1], weights, shared = together((back[-1], weights, shared))
    own = [packed, forth[1], back[1], forth[2], back[2], forth[3], back[3]]
    early = [block for pair in zip(own[:4], other[:4]) for block in pair]
    first = half_call(
        counts, capacity, choices, 0, where, weights, early, down_routed, hidden_routed, None, None
    )
    rows, *first = first
    forth[3], back[3], first[3] = together((forth[3], back[3], first[3]))
    own[-2:] = forth[3], back[3]
    split = features // 2 // 128 * 128
    left, right = send(forth[3][:, :split], up), send(back[3][:, split:], down)
    across = lax.ppermute(shared, "node", [(n, n ^ 2) for n in range(counts[0])])
    shared = [shared, swapped(shared), across]
    d_hidden_shared = shared_back_call(counts, where, weights, own, down_shared)
    left, right, shared, d_hidden_shared = together((left, right, shared, d_hidden_shared))
    own.append(jnp.concatenate([left, right], axis=1))
    other.append(swapped(own[-1]))
    shared.append(swapped(shared[2]))
    late = [block for pair in zip(own[4:], other[4:]) for block in pair]
    second = half_call(
        counts, capacity, choices, len(early), where, weights, late, down_routed, hidden_routed, rows, first[3]
    )
    rows, *second = second
    d_gate = gates_call(counts, exchanged(second[3]), expert_ids.T).T
    d_down, d_hidden_routed, d_down_shared = last_call(
        counts, slot_total, where, rows, (None, *first[:3]), (None, *second[:3]), shared
    )
    return (d_hidden_routed, d_down, d_gate, d_hidden_shared, d_down_shared)


def solution(mesh):
    placed = (
        P(("groups", "node", "local"), None),
        P("groups"),
        P(("groups", "node", "local"), None),
        P(("groups", "node", "local"), None),
        P("node", "groups", "local"),
        P("node", "local", None),
        P(("groups", "node"), "local"),
        P("local", None),
    )
    small = mesh.shape["node"] == 4 and mesh.shape["local"] == 4
    return jax.shard_map(
        body if small else wide_body,
        mesh=mesh,
        in_specs=placed,
        out_specs=(
            P("node", "groups", "local"),
            P(("groups", "node"), "local", None),
            P(("groups", "node", "local"), None),
            P(("groups", "node"), "local"),
            P(("groups", "local"), "node"),
        ),
        check_vma=False,
    )
```

time: 96.6 us -> 60 us (0.62)
  matrix products: 28.5 us -> 0 us
  Pallas kernels: 0 us -> 21.6 us
  local copies, waits for them, and re-layouts: 24.9 us -> 3.94 us
  other arithmetic: 14 us -> 0.08 us
  waiting for transfers between devices: 8.57 us -> 13.6 us
    dot_general x10 -> x0, matrix products: 28.5 us -> none  [dot(): lax.dot_general(a, b, (((ca,), (cb,)), ((), ())), preferred_element_type=...]
    pallas_call x0 -> x7, Pallas kernels: none -> 21.6 us  [the longest x1 9.27 us: last_call(): pl.pallas_call(kernel, out_shape=(jax.ShapeDtypeStruct((experts, units, f...]
    unnamed x31 -> x21, local copies, waits for them, and re-layouts: 12 us -> 3.9 us
    another operation x8 -> x1, other arithmetic: 6.25 us -> 0.08 us  [body(): jnp.stack([lax.axis_index('node'), lax.axis_index('local')])]
    all_to_all x0 -> x1, starting transfers between devices: none -> 6.12 us  [exchanged(): return lax.all_to_all(a, AXES, split_axis=0, concat_axis=0, tiled=True)]
    ppermute x25 -> x19, starting transfers between devices: 19.1 us -> 13.5 us  [the longest x8 9.89 us: send(): return lax.ppermute(a, AXES, pairs)]
    ppermute x25 -> x19, waiting for transfers between devices: 8.57 us -> 13.6 us  [the longest x8 12.6 us: send(): return lax.ppermute(a, AXES, pairs)]
    gather x6 -> x0, local copies, waits for them, and re-layouts: 4.96 us -> none  [the longest x1 2.64 us: body(): shared_back = dot(blocked[near].reshape(-1, features), down_shared, 1, 1)]
  transfers between devices with their start and end apart: 25 -> 20, of which waited for: 8 -> 6; matrix products, arithmetic and copies ran while one was open for 48% -> 0% of each run, Pallas kernels for 0% -> 35%
where the time goes in v3:
time: 60 us; the launch traced here: 59.7 us
  Pallas kernels  21.6 us (36%)
  starting transfers between devices  19.6 us (33%)
  waiting for transfers between devices  13.6 us (23%)
  local copies, waits for them, and re-layouts  3.94 us (7%)
  between operations  0.83 us (1%)
    ppermute x8, waiting for transfers between devices, send(): return lax.ppermute(a, AXES, pairs)  12.6 us
    ppermute x8, starting transfers between devices, send(): return lax.ppermute(a, AXES, pairs)  9.89 us
    pallas_call x1, Pallas kernels, last_call(): pl.pallas_call(kernel, out_shape=(jax.ShapeDtypeStruct((experts, units, f...  9.27 us
    pallas_call x2, Pallas kernels, half_call(): pl.pallas_call(kernel, out_shape=(jax.ShapeDtypeStruct((-(-ROWS_BYTES //...  8.19 us
    all_to_all x1, starting transfers between devices, exchanged(): return lax.all_to_all(a, AXES, split_axis=0, concat_axis=0, tiled=True)  6.12 us
    unnamed x21, local copies, waits for them, and re-layouts  3.9 us
    pallas_call x1, Pallas kernels, shared_back_call(): pl.pallas_call(kernel, out_shape=jax.ShapeDtypeStruct((tokens, units), BF...  2.63 us
    ppermute x10, starting transfers between devices, swapped(): return lax.ppermute(a, 'node', [(n, n ^ 1) for n in range(counts[0])])  2.14 us
  transfers between devices with their start and end apart: 20, of which 6 were waited for; matrix products, arithmetic and copies ran while one was open for 0% of the time, Pallas kernels for 35%

profile of v3, /device:TPU:0, one launch (start us, length us, event | category | flops | bytes accessed | tf_op | source)
XLA Modules:
  0.0 59.7 jit_solution(10811252169398470335)
XLA Ops:
  0.6 0.1 pad_add_fusion.where_ref
  0.7 0.0 copy-start.1
  0.7 0.9 %copy-done.1 = bf16[32,3584]{1,0:T(8,128)(2,1)S(1)} copy-done((bf16[32,3584]{1,0:T(8,128)(2,1)S(1)}, bf16[32,3584]{1,0:T(8,128)(2,1)}, u32[]{:S(2)}) %copy-start.1) | copy-done | bytes 229400
  1.6 0.0 copy-start.2
  1.7 0.7 %copy-done.2 = s32[32,8]{0,1:T(8,128)S(1)} copy-done((s32[32,8]{0,1:T(8,128)S(1)}, s32[32,8]{0,1:T(8,128)}, u32[]{:S(2)}) %copy-start.2) | copy-done | bytes 1048
  2.3 0.7 %copy-done.4 = bf16[32,8]{0,1:T(8,128)(2,1)S(1)} copy-done((bf16[32,8]{0,1:T(8,128)(2,1)S(1)}, bf16[32,8]{0,1:T(8,128)(2,1)}, u32[]{:S(2)}) %copy-start.4) | copy-done | bytes 536
  3.0 0.2 pack.1.refs_0_
  3.2 0.0 slice-start.1
  3.2 0.0 copy-start
  3.2 3.1 %collective-permute-start.3 = (bf16[32,3712]{1,0:T(8,128)(2,1)S(1)}, bf16[32,3712]{1,0:T(8,128)(2,1)S(1)}, u32[]{:S(2)}, u32[]{:S(2)}) collective-permute-start(bf16[32,3712]{1,0:T(8,128)(2,1)S(1)} %pack.1.refs_0_), channel_id=1, source_target_pairs={{0,1},{4,5},{1,2},{5,6},{2,3},{6,7},{3,11},{7,15},{11,10},{15,14},... | collective-permute-start | bytes 712712 | tf_op jit(solution)/shard_map/ppermute | solution.py:486
  6.3 0.0 collective-permute-start
  6.3 0.0 collective-permute-start.7
  6.3 5.7 %collective-permute-done.3.refs_2_.refs_1_ = bf16[32,3712]{1,0:T(8,128)(2,1)S(1)} collective-permute-done((bf16[32,3712]{1,0:T(8,128)(2,1)S(1)}, bf16[32,3712]{1,0:T(8,128)(2,1)S(1)}, u32[]{:S(2)}, u32[]{:S(2)}) %collective-permute-start.3) | collective-permute-done | bytes 237600 | tf_op jit(solution)/shard_map/ppermute | solution.py:486
  12.0 1.8 %collective-permute-start.4 = (bf16[32,3712]{1,0:T(8,128)(2,1)S(1)}, bf16[32,3712]{1,0:T(8,128)(2,1)S(1)}, u32[]{:S(2)}, u32[]{:S(2)}) collective-permute-start(bf16[32,3712]{1,0:T(8,128)(2,1)S(1)} %collective-permute-done.3.refs_2_.refs_1_), channel_id=1, source_target_pairs={{0,1},{4,5},{1,2},{5,6},{2,3},{6,7},{3,11},{7,15},{11,10},{15,14},... | collective-permute-start | bytes 712712 | tf_op jit(solution)/shard_map/ppermute | solution.py:486
  13.8 0.9 %copy-done.6 = bf16[128,512]{1,0:T(8,128)(2,1)S(1)} copy-done((bf16[128,512]{1,0:T(8,128)(2,1)S(1)}, bf16[128,512]{1,0:T(8,128)(2,1)}, u32[]{:S(2)}) %copy-start.6) | copy-done | bytes 131096
  14.7 0.7 %copy-done.7 = s32[16]{0:T(128)S(1)} copy-done((s32[16]{0:T(128)S(1)}, s32[16]{0:T(128)}, u32[]{:S(2)}) %copy-start.7) | copy-done | bytes 88
  15.4 0.8 %weights.1 = (f32[8,512]{1,0:T(8,128)S(1)}, bf16[128,512]{1,0:T(8,128)(2,1)S(1)}) custom-call(s32[16]{0:T(128)S(1)} %copy-done.7, s32[2]{0:T(128)S(1)} %pad_add_fusion.where_ref, bf16[128,512]{1,0:T(8,128)(2,1)S(1)} %copy-done.6), custom_call_target="tpu_custom_call" | custom-call | flops 20000000000 | bytes 1000000 | tf_op jit(solution)/shard_map/weights/pallas_call | solution.py:135
  16.2 0.1 collective-permute-start.8
  16.2 0.0 collective-permute-done.refs_4_.refs_2_
  16.3 0.0 copy-start.5
  16.3 0.5 collective-permute-start.9
  16.7 0.2 collective-permute-start.1
  17.0 2.0 %collective-permute-done.4.refs_6_.refs_3_ = bf16[32,3712]{1,0:T(8,128)(2,1)S(1)} collective-permute-done((bf16[32,3712]{1,0:T(8,128)(2,1)S(1)}, bf16[32,3712]{1,0:T(8,128)(2,1)S(1)}, u32[]{:S(2)}, u32[]{:S(2)}) %collective-permute-start.4) | collective-permute-done | bytes 237600 | tf_op jit(solution)/shard_map/ppermute | solution.py:486
  19.0 0.0 collective-permute-start.10
  19.0 0.0 collective-permute-done.7.refs_1_
  19.0 0.5 collective-permute-start.15
  19.5 0.0 collective-permute-done.8.refs_3_
  19.5 1.4 %collective-permute-start.16 = (bf16[128,512]{1,0:T(8,128)(2,1)S(1)}, bf16[128,512]{1,0:T(8,128)(2,1)S(1)}, u32[]{:S(2)}, u32[]{:S(2)}) collective-permute-start(bf16[128,512]{1,0:T(8,128)(2,1)S(1)} %get-tuple-element.55.refs_6_), channel_id=1, source_target_pairs={{0,8},{4,12},{8,0},{12,4},{1,9},{5,13},{9,1},{13,5},{2,10},{6,14},... | collective-permute-start | bytes 393224 | tf_op jit(solution)/shard_map/ppermute | solution.py:511
  20.9 0.0 collective-permute-done.9.refs_5_
  20.9 1.6 %collective-permute-start.5 = (bf16[32,3712]{1,0:T(8,128)(2,1)S(1)}, bf16[32,3712]{1,0:T(8,128)(2,1)S(1)}, u32[]{:S(2)}, u32[]{:S(2)}) collective-permute-start(bf16[32,3712]{1,0:T(8,128)(2,1)S(1)} %collective-permute-done.4.refs_6_.refs_3_), channel_id=1, source_target_pairs={{0,1},{4,5},{1,2},{5,6},{2,3},{6,7},{3,11},{7,15},{11,10},{15,14},... | collective-permute-start | bytes 712712 | tf_op jit(solution)/shard_map/ppermute | solution.py:486
  22.5 2.0 %collective-permute-done.1.refs_4_.refs_0_ = bf16[32,3712]{1,0:T(8,128)(2,1)S(1)} collective-permute-done((bf16[32,3712]{1,0:T(8,128)(2,1)S(1)}, bf16[32,3712]{1,0:T(8,128)(2,1)S(1)}, u32[]{:S(2)}, u32[]{:S(2)}) %collective-permute-start.1) | collective-permute-done | bytes 237600 | tf_op jit(solution)/shard_map/ppermute | solution.py:486
  24.5 1.1 %collective-permute-start.6 = (bf16[32,3712]{1,0:T(8,128)(2,1)S(1)}, bf16[32,3712]{1,0:T(8,128)(2,1)S(1)}, u32[]{:S(2)}, u32[]{:S(2)}) collective-permute-start(bf16[32,3712]{1,0:T(8,128)(2,1)S(1)} %collective-permute-done.1.refs_4_.refs_0_), channel_id=1, source_target_pairs={{0,8},{4,12},{1,0},{5,4},{2,1},{6,5},{3,2},{7,6},{11,3},{15,7},{10... | collective-permute-start | bytes 712712 | tf_op jit(solution)/shard_map/ppermute | solution.py:486
  25.6 0.0 collective-permute-done.10.refs_7_
  25.6 0.0 collective-permute-start.2
  25.6 0.0 slice-done
  25.6 0.0 slice-done.1
  25.6 0.0 copy-done
  25.6 3.8 %half_first.1 = (bf16[9655,3584]{1,0:T(8,128)(2,1)}, bf16[2,512,256]{2,1,0:T(8,128)(2,1)S(1)}, bf16[2,512,256]{2,1,0:T(8,128)(2,1)S(1)}, f32[8,256]{1,0:T(8,128)S(1)}, f32[16,2,32]{2,1,0:T(2,128)S(1)}) custom-call(s32[2]{0:T(128)S(1)} %pad_add_fusion.where_ref, bf16[32,3712]{1,0:T(8,128)(2,1)S(1)} %pack.1.refs_0_, ...), custom_call_target="tpu_custom_call" | custom-call | flops 6000000000 | bytes 1000000 | tf_op jit(solution)/shard_map/half_first/pallas_call | solution.py:231
  29.4 2.0 %collective-permute-done.6.refs_6_.refs_4_ = bf16[32,3712]{1,0:T(8,128)(2,1)S(1)} collective-permute-done((bf16[32,3712]{1,0:T(8,128)(2,1)S(1)}, bf16[32,3712]{1,0:T(8,128)(2,1)S(1)}, u32[]{:S(2)}, u32[]{:S(2)}) %collective-permute-start.6) | collective-permute-done | bytes 237600 | tf_op jit(solution)/shard_map/ppermute | solution.py:486
  31.5 0.0 collective-permute-done.5.refs_5_.refs_2_
  31.5 1.3 %collective-permute-start.14 = (bf16[32,1920]{1,0:T(8,128)(2,1)S(1)}, bf16[32,1920]{1,0:T(8,128)(2,1)S(1)}, u32[]{:S(2)}, u32[]{:S(2)}) collective-permute-start(bf16[32,1920]{1,0:T(8,128)(2,1)S(1)} %slice.7), channel_id=1, source_target_pairs={{0,8},{4,12},{1,0},{5,4},{2,1},{6,5},{3,2},{7,6},{11,3},{15,7},{10... | collective-permute-start | bytes 368648 | tf_op jit(solution)/shard_map/ppermute | solution.py:486
  32.8 0.8 %collective-permute-start.13 = (bf16[32,1792]{1,0:T(8,128)(2,1)S(1)}, bf16[32,1792]{1,0:T(8,128)(2,1)S(1)}, u32[]{:S(2)}, u32[]{:S(2)}) collective-permute-start(bf16[32,1792]{1,0:T(8,128)(2,1)S(1)} %slice.6), channel_id=1, source_target_pairs={{0,1},{4,5},{1,2},{5,6},{2,3},{6,7},{3,11},{7,15},{11,10},{15,14},... | collective-permute-start | bytes 344072 | tf_op jit(solution)/shard_map/ppermute | solution.py:486
  33.6 0.0 copy-done.5
  33.6 2.6 %shared_back.1 = bf16[128,512]{1,0:T(8,128)(2,1)} custom-call(s32[2]{0:T(128)S(1)} %pad_add_fusion.where_ref, bf16[32,3712]{1,0:T(8,128)(2,1)S(1)} %pack.1.refs_0_, bf16[32,3712]{1,0:T(8,128)(2,1)S(1)} %collective-permute-done.3.refs_2_.refs_1_, bf16[32,3712]{1,0:T(8,128)(2,1)S(1)} %collective-permute-done.refs_4_.refs_2_, ...), custom_call_target="tpu_custom_call" | custom-call | flops 3000000000 | bytes 1000000 | tf_op jit(solution)/shard_map/shared_back/pallas_call | solution.py:363
  36.3 0.0 collective-permute-done.15.refs_7_
  36.3 0.0 collective-permute-start.12
  36.3 0.0 collective-permute-done.16.refs_8_
  36.3 0.5 collective-permute-start.11
  36.8 0.9 %collective-permute-done.13 = bf16[32,1792]{1,0:T(8,128)(2,1)S(1)} collective-permute-done((bf16[32,1792]{1,0:T(8,128)(2,1)S(1)}, bf16[32,1792]{1,0:T(8,128)(2,1)S(1)}, u32[]{:S(2)}, u32[]{:S(2)}) %collective-permute-start.13) | collective-permute-done | bytes 114720 | tf_op jit(solution)/shard_map/ppermute | solution.py:486
  37.6 0.0 collective-permute-done.14
  37.7 0.1 collective-permute-start.17
  37.7 0.5 collective-permute-start.18
  38.2 0.0 collective-permute-done.2.refs_1_
  38.2 0.0 collective-permute-done.12.refs_5_
  38.3 0.0 collective-permute-done.11.refs_3_
  38.3 1.0 %collective-permute-done.17.refs_7_ = bf16[32,3712]{1,0:T(8,128)(2,1)S(1)} collective-permute-done((bf16[32,3712]{1,0:T(8,128)(2,1)S(1)}, bf16[32,3712]{1,0:T(8,128)(2,1)S(1)}, u32[]{:S(2)}, u32[]{:S(2)}) %collective-permute-start.17) | collective-permute-done | bytes 237600 | tf_op jit(solution)/shard_map/ppermute | solution.py:489
  39.2 4.4 %half_second.1 = (bf16[9655,3584]{1,0:T(8,128)(2,1)}, bf16[2,512,256]{2,1,0:T(8,128)(2,1)S(1)}, bf16[2,512,256]{2,1,0:T(8,128)(2,1)S(1)}, f32[8,256]{1,0:T(8,128)S(1)}, f32[16,2,32]{2,1,0:T(2,128)}) custom-call(s32[2]{0:T(128)S(1)} %pad_add_fusion.where_ref, ...), custom_call_target="tpu_custom_call", output_to_operand_aliasing={{0}: (12, {})} | custom-call | flops 6000000000 | bytes 1000000 | tf_op jit(solution)/shard_map/half_second/pallas_call | solution.py:231
  43.6 6.1 %all-to-all-start = ((f32[16,2,32]{2,1,0:T(2,128)}), f32[16,2,32]{2,1,0:T(2,128)S(1)}, u32[]{:S(2)}, u32[]{:S(2)}) async-start(f32[16,2,32]{2,1,0:T(2,128)} %get-tuple-element.60), calls=%async_computation | async-start | bytes 32768 | tf_op jit(solution)/shard_map/all_to_all | solution.py:400
  49.8 0.0 collective-permute-done.18.refs_9_
  49.8 0.0 copy-start.3
  49.8 9.3 %last.1 = (bf16[2,512,3584]{2,1,0:T(8,128)(2,1)}, bf16[2,496,512]{2,1,0:T(8,128)(2,1)}, bf16[512,896]{1,0:T(8,128)(2,1)}) custom-call(s32[2]{0:T(128)S(1)} %pad_add_fusion.where_ref, bf16[9655,3584]{1,0:T(8,128)(2,1)} %get-tuple-element.48.rows_ref, bf16[2,512,256]{2,1,0:T(8,128)(2,1)S(1)} %get-tuple-element.49.refs_0_, ...), custom_call_target="tpu_custom_call" | custom-call | flops 8000000000 | bytes 10000000 | tf_op jit(solution)/shard_map/last/pallas_call | solution.py:318
  59.1 0.0 all-to-all-done.parts_ref
  59.1 0.0 copy-done.3
  59.1 0.6 %gates.1 = f32[8,32]{1,0:T(8,128)} custom-call(s32[8,32]{1,0:T(8,128)S(1)} %bitcast.8, f32[16,2,32]{2,1,0:T(2,128)S(1)} %all-to-all-done.parts_ref), custom_call_target="tpu_custom_call" | custom-call | flops 1000000 | bytes 10000 | tf_op jit(solution)/shard_map/gates/pallas_call | solution.py:388
  (9 shorter events, 0.1 us)
Async XLA Ops:
  0.7 0.9 %copy-start.1 = (bf16[32,3584]{1,0:T(8,128)(2,1)S(1)}, bf16[32,3584]{1,0:T(8,128)(2,1)}, u32[]{:S(2)}) copy-start(bf16[32,3584]{1,0:T(8,128)(2,1)} %rows_ref.1) | copy-start | bytes 688132
  1.6 0.7 %copy-start.2 = (s32[32,8]{0,1:T(8,128)S(1)}, s32[32,8]{0,1:T(8,128)}, u32[]{:S(2)}) copy-start(s32[32,8]{0,1:T(8,128)} %param.11) | copy-start | bytes 3076
  2.3 0.7 %copy-start.4 = (bf16[32,8]{0,1:T(8,128)(2,1)S(1)}, bf16[32,8]{0,1:T(8,128)(2,1)}, u32[]{:S(2)}) copy-start(bf16[32,8]{0,1:T(8,128)(2,1)} %param.10) | copy-start | bytes 1540
  3.0 22.6 %slice-start = ((s8[7340032]{0:T(1024)(128)(4,1)}), s8[3145728]{0:T(1024)(128)(4,1)S(1)}, s32[]{:S(2)}) async-start(s8[7340032]{0:T(1024)(128)(4,1)} %bitcast.5), calls=%async_computation.1 | async-start | bytes 6291456
  3.2 22.4 %slice-start.1 = ((s8[7340032]{0:T(1024)(128)(4,1)}), s8[4194304]{0:T(1024)(128)(4,1)S(1)}, s32[]{:S(2)}) async-start(s8[7340032]{0:T(1024)(128)(4,1)} %bitcast.5), calls=%async_computation.2 | async-start | bytes 8388608
  3.2 22.4 %copy-start = (bf16[2,496,512]{2,1,0:T(8,128)(2,1)S(1)}, bf16[2,496,512]{2,1,0:T(8,128)(2,1)}, u32[]{:S(2)}) copy-start(bf16[2,496,512]{2,1,0:T(8,128)(2,1)} %refs_10_.3) | copy-start | bytes 3047428
  3.2 8.8 %collective-permute-start.3 = (bf16[32,3712]{1,0:T(8,128)(2,1)S(1)}, bf16[32,3712]{1,0:T(8,128)(2,1)S(1)}, u32[]{:S(2)}, u32[]{:S(2)}) collective-permute-start(bf16[32,3712]{1,0:T(8,128)(2,1)S(1)} %pack.1.refs_0_), channel_id=1, source_target_pairs={{0,1},{4,5},{1,2},{5,6},{2,3},{6,7},{3,11},{7,15},{11,10},{15,14},... | collective-permute-start | bytes 712712 | tf_op jit(solution)/shard_map/ppermute | solution.py:486
  6.3 9.9 %collective-permute-start = (bf16[32,3712]{1,0:T(8,128)(2,1)S(1)}, bf16[32,3712]{1,0:T(8,128)(2,1)S(1)}, u32[]{:S(2)}, u32[]{:S(2)}) collective-permute-start(bf16[32,3712]{1,0:T(8,128)(2,1)S(1)} %pack.1.refs_0_), channel_id=1, source_target_pairs={{0,8},{4,12},{1,0},{5,4},{2,1},{6,5},{3,2},{7,6},{11,3},{15,7},{10... | collective-permute-start | bytes 712712 | tf_op jit(solution)/shard_map/ppermute | solution.py:486
  6.3 12.7 %collective-permute-start.7 = (bf16[32,3712]{1,0:T(8,128)(2,1)S(1)}, bf16[32,3712]{1,0:T(8,128)(2,1)S(1)}, u32[]{:S(2)}, u32[]{:S(2)}) collective-permute-start(bf16[32,3712]{1,0:T(8,128)(2,1)S(1)} %pack.1.refs_0_), channel_id=1, source_target_pairs={{0,4},{4,0},{8,12},{12,8},{1,5},{5,1},{9,13},{13,9},{2,6},{6,2},{1... | collective-permute-start | bytes 712712 | tf_op jit(solution)/shard_map/ppermute | solution.py:489
  12.0 7.0 %collective-permute-start.4 = (bf16[32,3712]{1,0:T(8,128)(2,1)S(1)}, bf16[32,3712]{1,0:T(8,128)(2,1)S(1)}, u32[]{:S(2)}, u32[]{:S(2)}) collective-permute-start(bf16[32,3712]{1,0:T(8,128)(2,1)S(1)} %collective-permute-done.3.refs_2_.refs_1_), channel_id=1, source_target_pairs={{0,1},{4,5},{1,2},{5,6},{2,3},{6,7},{3,11},{7,15},{11,10},{15,14},... | collective-permute-start | bytes 712712 | tf_op jit(solution)/shard_map/ppermute | solution.py:486
  13.8 0.9 %copy-start.6 = (bf16[128,512]{1,0:T(8,128)(2,1)S(1)}, bf16[128,512]{1,0:T(8,128)(2,1)}, u32[]{:S(2)}) copy-start(bf16[128,512]{1,0:T(8,128)(2,1)} %shared_ref.1) | copy-start | bytes 393220
  14.7 0.7 %copy-start.7 = (s32[16]{0:T(128)S(1)}, s32[16]{0:T(128)}, u32[]{:S(2)}) copy-start(s32[16]{0:T(128)} %lens_ref.1) | copy-start | bytes 196
  16.2 3.4 %collective-permute-start.8 = (bf16[32,3712]{1,0:T(8,128)(2,1)S(1)}, bf16[32,3712]{1,0:T(8,128)(2,1)S(1)}, u32[]{:S(2)}, u32[]{:S(2)}) collective-permute-start(bf16[32,3712]{1,0:T(8,128)(2,1)S(1)} %collective-permute-done.3.refs_2_.refs_1_), channel_id=1, source_target_pairs={{0,4},{4,0},{8,12},{12,8},{1,5},{5,1},{9,13},{13,9},{2,6},{6,2},{1... | collective-permute-start | bytes 712712 | tf_op jit(solution)/shard_map/ppermute | solution.py:489
  16.3 17.4 %copy-start.5 = (bf16[512,3584]{1,0:T(8,128)(2,1)S(1)}, bf16[512,3584]{1,0:T(8,128)(2,1)}, u32[]{:S(2)}) copy-start(bf16[512,3584]{1,0:T(8,128)(2,1)} %refs_8_.1) | copy-start | bytes 11010052
  16.3 4.7 %collective-permute-start.9 = (bf16[32,3712]{1,0:T(8,128)(2,1)S(1)}, bf16[32,3712]{1,0:T(8,128)(2,1)S(1)}, u32[]{:S(2)}, u32[]{:S(2)}) collective-permute-start(bf16[32,3712]{1,0:T(8,128)(2,1)S(1)} %collective-permute-done.refs_4_.refs_2_), channel_id=1, source_target_pairs={{0,4},{4,0},{8,12},{12,8},{1,5},{5,1},{9,13},{13,9},{2,6},{6,2},{1... | collective-permute-start | bytes 712712 | tf_op jit(solution)/shard_map/ppermute | solution.py:489
  16.7 7.8 %collective-permute-start.1 = (bf16[32,3712]{1,0:T(8,128)(2,1)S(1)}, bf16[32,3712]{1,0:T(8,128)(2,1)S(1)}, u32[]{:S(2)}, u32[]{:S(2)}) collective-permute-start(bf16[32,3712]{1,0:T(8,128)(2,1)S(1)} %collective-permute-done.refs_4_.refs_2_), channel_id=1, source_target_pairs={{0,8},{4,12},{1,0},{5,4},{2,1},{6,5},{3,2},{7,6},{11,3},{15,7},{10... | collective-permute-start | bytes 712712 | tf_op jit(solution)/shard_map/ppermute | solution.py:486
  19.0 6.6 %collective-permute-start.10 = (bf16[32,3712]{1,0:T(8,128)(2,1)S(1)}, bf16[32,3712]{1,0:T(8,128)(2,1)S(1)}, u32[]{:S(2)}, u32[]{:S(2)}) collective-permute-start(bf16[32,3712]{1,0:T(8,128)(2,1)S(1)} %collective-permute-done.4.refs_6_.refs_3_), channel_id=1, source_target_pairs={{0,4},{4,0},{8,12},{12,8},{1,5},{5,1},{9,13},{13,9},{2,6},{6,2},{1... | collective-permute-start | bytes 712712 | tf_op jit(solution)/shard_map/ppermute | solution.py:489
  19.0 17.3 %collective-permute-start.15 = (bf16[128,512]{1,0:T(8,128)(2,1)S(1)}, bf16[128,512]{1,0:T(8,128)(2,1)S(1)}, u32[]{:S(2)}, u32[]{:S(2)}) collective-permute-start(bf16[128,512]{1,0:T(8,128)(2,1)S(1)} %get-tuple-element.55.refs_6_), channel_id=1, source_target_pairs={{0,4},{4,0},{8,12},{12,8},{1,5},{5,1},{9,13},{13,9},{2,6},{6,2},{1... | collective-permute-start | bytes 393224 | tf_op jit(solution)/shard_map/ppermute | solution.py:489
  19.5 16.8 %collective-permute-start.16 = (bf16[128,512]{1,0:T(8,128)(2,1)S(1)}, bf16[128,512]{1,0:T(8,128)(2,1)S(1)}, u32[]{:S(2)}, u32[]{:S(2)}) collective-permute-start(bf16[128,512]{1,0:T(8,128)(2,1)S(1)} %get-tuple-element.55.refs_6_), channel_id=1, source_target_pairs={{0,8},{4,12},{8,0},{12,4},{1,9},{5,13},{9,1},{13,5},{2,10},{6,14},... | collective-permute-start | bytes 393224 | tf_op jit(solution)/shard_map/ppermute | solution.py:511
  20.9 10.5 %collective-permute-start.5 = (bf16[32,3712]{1,0:T(8,128)(2,1)S(1)}, bf16[32,3712]{1,0:T(8,128)(2,1)S(1)}, u32[]{:S(2)}, u32[]{:S(2)}) collective-permute-start(bf16[32,3712]{1,0:T(8,128)(2,1)S(1)} %collective-permute-done.4.refs_6_.refs_3_), channel_id=1, source_target_pairs={{0,1},{4,5},{1,2},{5,6},{2,3},{6,7},{3,11},{7,15},{11,10},{15,14},... | collective-permute-start | bytes 712712 | tf_op jit(solution)/shard_map/ppermute | solution.py:486
  24.5 6.9 %collective-permute-start.6 = (bf16[32,3712]{1,0:T(8,128)(2,1)S(1)}, bf16[32,3712]{1,0:T(8,128)(2,1)S(1)}, u32[]{:S(2)}, u32[]{:S(2)}) collective-permute-start(bf16[32,3712]{1,0:T(8,128)(2,1)S(1)} %collective-permute-done.1.refs_4_.refs_0_), channel_id=1, source_target_pairs={{0,8},{4,12},{1,0},{5,4},{2,1},{6,5},{3,2},{7,6},{11,3},{15,7},{10... | collective-permute-start | bytes 712712 | tf_op jit(solution)/shard_map/ppermute | solution.py:486
  25.6 12.6 %collective-permute-start.2 = (bf16[32,3712]{1,0:T(8,128)(2,1)S(1)}, bf16[32,3712]{1,0:T(8,128)(2,1)S(1)}, u32[]{:S(2)}, u32[]{:S(2)}) collective-permute-start(bf16[32,3712]{1,0:T(8,128)(2,1)S(1)} %collective-permute-done.1.refs_4_.refs_0_), channel_id=1, source_target_pairs={{0,4},{4,0},{8,12},{12,8},{1,5},{5,1},{9,13},{13,9},{2,6},{6,2},{1... | collective-permute-start | bytes 712712 | tf_op jit(solution)/shard_map/ppermute | solution.py:489
  31.5 6.2 %collective-permute-start.14 = (bf16[32,1920]{1,0:T(8,128)(2,1)S(1)}, bf16[32,1920]{1,0:T(8,128)(2,1)S(1)}, u32[]{:S(2)}, u32[]{:S(2)}) collective-permute-start(bf16[32,1920]{1,0:T(8,128)(2,1)S(1)} %slice.7), channel_id=1, source_target_pairs={{0,8},{4,12},{1,0},{5,4},{2,1},{6,5},{3,2},{7,6},{11,3},{15,7},{10... | collective-permute-start | bytes 368648 | tf_op jit(solution)/shard_map/ppermute | solution.py:486
  32.8 4.8 %collective-permute-start.13 = (bf16[32,1792]{1,0:T(8,128)(2,1)S(1)}, bf16[32,1792]{1,0:T(8,128)(2,1)S(1)}, u32[]{:S(2)}, u32[]{:S(2)}) collective-permute-start(bf16[32,1792]{1,0:T(8,128)(2,1)S(1)} %slice.6), channel_id=1, source_target_pairs={{0,1},{4,5},{1,2},{5,6},{2,3},{6,7},{3,11},{7,15},{11,10},{15,14},... | collective-permute-start | bytes 344072 | tf_op jit(solution)/shard_map/ppermute | solution.py:486
  36.3 2.0 %collective-permute-start.12 = (bf16[32,3712]{1,0:T(8,128)(2,1)S(1)}, bf16[32,3712]{1,0:T(8,128)(2,1)S(1)}, u32[]{:S(2)}, u32[]{:S(2)}) collective-permute-start(bf16[32,3712]{1,0:T(8,128)(2,1)S(1)} %collective-permute-done.6.refs_6_.refs_4_), channel_id=1, source_target_pairs={{0,4},{4,0},{8,12},{12,8},{1,5},{5,1},{9,13},{13,9},{2,6},{6,2},{1... | collective-permute-start | bytes 712712 | tf_op jit(solution)/shard_map/ppermute | solution.py:489
  36.3 2.0 %collective-permute-start.11 = (bf16[32,3712]{1,0:T(8,128)(2,1)S(1)}, bf16[32,3712]{1,0:T(8,128)(2,1)S(1)}, u32[]{:S(2)}, u32[]{:S(2)}) collective-permute-start(bf16[32,3712]{1,0:T(8,128)(2,1)S(1)} %collective-permute-done.5.refs_5_.refs_2_), channel_id=1, source_target_pairs={{0,4},{4,0},{8,12},{12,8},{1,5},{5,1},{9,13},{13,9},{2,6},{6,2},{1... | collective-permute-start | bytes 712712 | tf_op jit(solution)/shard_map/ppermute | solution.py:489
  37.7 1.6 %collective-permute-start.17 = (bf16[32,3712]{1,0:T(8,128)(2,1)S(1)}, bf16[32,3712]{1,0:T(8,128)(2,1)S(1)}, u32[]{:S(2)}, u32[]{:S(2)}) collective-permute-start(bf16[32,3712]{1,0:T(8,128)(2,1)S(1)} %constant_dynamic-update-slice_fusion.refs_6_), channel_id=1, source_target_pairs={{0,4},{4,0},{8,12},{12,8},{1,5},{5,1},{9,13},{13,9},{2,6},{6,2},{1... | collective-permute-start | bytes 712712 | tf_op jit(solution)/shard_map/ppermute | solution.py:489
  37.7 12.0 %collective-permute-start.18 = (bf16[128,512]{1,0:T(8,128)(2,1)S(1)}, bf16[128,512]{1,0:T(8,128)(2,1)S(1)}, u32[]{:S(2)}, u32[]{:S(2)}) collective-permute-start(bf16[128,512]{1,0:T(8,128)(2,1)S(1)} %collective-permute-done.16.refs_8_), channel_id=1, source_target_pairs={{0,4},{4,0},{8,12},{12,8},{1,5},{5,1},{9,13},{13,9},{2,6},{6,2},{1... | collective-permute-start | bytes 393224 | tf_op jit(solution)/shard_map/ppermute | solution.py:489
  43.6 15.4 %all-to-all-start = ((f32[16,2,32]{2,1,0:T(2,128)}), f32[16,2,32]{2,1,0:T(2,128)S(1)}, u32[]{:S(2)}, u32[]{:S(2)}) async-start(f32[16,2,32]{2,1,0:T(2,128)} %get-tuple-element.60), calls=%async_computation | async-start | bytes 32768 | tf_op jit(solution)/shard_map/all_to_all | solution.py:400
  49.8 9.3 %copy-start.3 = (s32[32,8]{0,1:T(8,128)S(1)}, s32[32,8]{0,1:T(8,128)}, u32[]{:S(2)}) copy-start(s32[32,8]{0,1:T(8,128)} %param.11) | copy-start | bytes 3076

commit v4 on v3

--- a/solution.py
+++ b/solution.py
@@ -69,7 +69,7 @@
 WEIGHTS_FLOPS = 20 * 10**9
 HALF_FLOPS = 6 * 10**9
 SHARED_FLOPS = 3 * 10**9
-PACK_MIB = 50
+PACK_MIB = 57
 LAST_MIB = 40
 ROWS_BYTES = 66 * MIB
 LITTLE = pl.CostEstimate(flops=10**6, bytes_accessed=10**4, transcendentals=0)
@@ -115,12 +115,15 @@
     )(out_grad, gates, ids)
 
 
-def weights_call(counts, lengths, where, shared):
+def weights_call(counts, lengths, where, shared, hidden):
+    experts, slot_total, units = hidden.shape
     node_tokens, _ = shared.shape
     here = node_tokens // counts[1]
     tokens = counts[0] * node_tokens
 
-    def kernel(lens_ref, where_ref, shared_ref, weight_ref, out_ref):
+    def kernel(lens_ref, where_ref, shared_ref, hidden_ref, weight_ref, out_ref, turned_ref):
+        for e in range(experts):
+            turned_ref[e] = hidden_ref[e].astype(F32).T.astype(BF16)
         node, local = where_ref[0], where_ref[1]
         number = numbers_at(block_numbers(node, local, *counts), tokens, here)
         token = lax.broadcasted_iota(jnp.int32, (1, tokens), 1)
@@ -134,19 +137,23 @@
 
     return pl.pallas_call(
         kernel,
-        out_shape=(jax.ShapeDtypeStruct((8, tokens), F32), jax.ShapeDtypeStruct(shared.shape, BF16)),
-        in_specs=[SMEM, SMEM, VMEM],
-        out_specs=[VMEM] * 2,
-        compiler_params=pltpu.CompilerParams(vmem_limit_bytes=4 * MIB),
+        out_shape=(
+            jax.ShapeDtypeStruct((8, tokens), F32),
+            jax.ShapeDtypeStruct(shared.shape, BF16),
+            jax.ShapeDtypeStruct((experts, units, slot_total), BF16),
+        ),
+        in_specs=[SMEM, SMEM, VMEM, VMEM],
+        out_specs=[VMEM] * 3,
+        compiler_params=pltpu.CompilerParams(vmem_limit_bytes=8 * MIB),
         cost_estimate=pl.CostEstimate(flops=WEIGHTS_FLOPS, bytes_accessed=10**6, transcendentals=0),
         name="weights",
-    )(lengths, where, shared)
+    )(lengths, where, shared, hidden)
 
 
 def place(node, numbers, capacity, blocks, weight, hidden_ref, features, choices):
     here = blocks[0].shape[0]
     tokens = here * len(blocks)
-    experts, slot_total, _ = hidden_ref.shape
+    experts, _, slot_total = hidden_ref.shape
     tags = jnp.concatenate([block[:, features:] for block in blocks], axis=0).astype(F32).T
     gates, ids = tags[:choices], tags[choices : 2 * choices]
     number = numbers_at(numbers, tokens, here).astype(F32)
@@ -172,7 +179,7 @@
         info = jnp.where(row == e, cell, info)
         info = jnp.where(row == experts + e, gate[e], info)
         placing = (slot == cell).astype(F32).astype(BF16)
-        hidden = dot(hidden_ref[e], placing, 0, 0)
+        hidden = dot(hidden_ref[e], placing, 1, 0)
         placed.append(hidden.astype(BF16))
         scaled.append((hidden * (gate[e] * weight)).astype(BF16))
     return info, placed, scaled
@@ -278,7 +285,9 @@
 
         for ref, scr in zip(given, (grad_scr, grad_scr, scaled_scr, scaled_scr)):
             load(ref, scr.at[:, :, pl.ds(len(loads) % 2 * tokens, tokens)])
-        load(rows_ref.at[pl.ds(0, 2 * tokens)], x_scr)
+        for n in range(2):
+            at = pl.ds(n * (features // 2), features // 2)
+            load(rows_ref.at[pl.ds(0, 2 * tokens), at], x_scr.at[:, at])
         node, local = where_ref[0], where_ref[1]
         for n, part in enumerate(shared):
             at = pl.multiple_of((node ^ n) * node_tokens, node_tokens)
@@ -298,20 +307,23 @@
 
         for copy in loads[:2]:
             copy.wait()
-        for e in range(experts - 1):
+        for e in range(experts):
             by_slot(e)
-        for copy in loads[2:]:
+        for copy in loads[2:4]:
             copy.wait()
         for e in range(experts):
             for n in range(parts):
                 at = slice(n * step, (n + 1) * step)
                 place = down_scr.at[e * parts + n]
-                place[...] = dot(scaled_scr[e, at, :], x_scr[...], 1, 0).astype(BF16)
+                for half in range(2):
+                    if e == n == 0:
+                        loads[4 + half].wait()
+                    columns = slice(half * (features // 2), (half + 1) * (features // 2))
+                    place[:, columns] = dot(scaled_scr[e, at, :], x_scr[:, columns], 1, 0).astype(BF16)
                 write(place, down_ref.at[e, pl.ds(n * step, step)])
         columns = pl.ds(pl.multiple_of(node * width, width), width)
         shared_scr[...] = dot(ordered_scr[...], x_scr[:, columns], 0, 0).astype(BF16)
         write(shared_scr, shared_ref)
-        by_slot(experts - 1)
         for copy in copies:
             copy.wait()
 
@@ -333,7 +345,7 @@
             pltpu.VMEM((experts * parts, step, features), BF16),
             pltpu.VMEM((experts, slot_total, units), BF16),
             pltpu.VMEM((shared_units, width), BF16),
-            pltpu.SemaphoreType.DMA((5,)),
+            pltpu.SemaphoreType.DMA((6,)),
             pltpu.SemaphoreType.DMA((experts * parts + experts + 1,)),
         ],
         compiler_params=pltpu.CompilerParams(vmem_limit_bytes=LAST_MIB * MIB),
@@ -491,39 +503,44 @@
     together = lax.optimization_barrier
     packed, where = together((pack_call(out_grad, gate_weights.T, expert_ids.T), where))
     forth, back, other = [packed], [packed], [swapped(packed)]
-    weights, shared = weights_call(counts, lengths, where, hidden_shared)
+    weights, shared, turned = weights_call(counts, lengths, where, hidden_shared, hidden_routed)
     for step in range(3):
         forth.append(send(forth[-1], up))
         back.append(send(back[-1], down))
         other += [swapped(forth[-1]), swapped(back[-1])]
         if step == 0:
-            back[-1], weights, shared = together((back[-1], weights, shared))
+            forth[-1], weights, shared, turned = together((forth[-1], weights, shared, turned))
+            shared = [shared, swapped(shared)]
+        if step == 1:
+            forth[-1], shared = together((forth[-1], shared))
     own = [packed, forth[1], back[1], forth[2], back[2], forth[3], back[3]]
     early = [block for pair in zip(own[:4], other[:4]) for block in pair]
     first = half_call(
-        counts, capacity, choices, 0, where, weights, early, down_routed, hidden_routed, None, None
+        counts, capacity, choices, 0, where, weights, early, down_routed, turned, None, None
     )
     rows, *first = first
     forth[3], back[3], first[3] = together((forth[3], back[3], first[3]))
     own[-2:] = forth[3], back[3]
     split = features // 2 // 128 * 128
     left, right = send(forth[3][:, :split], up), send(back[3][:, split:], down)
-    across = lax.ppermute(shared, "node", [(n, n ^ 2) for n in range(counts[0])])
-    shared = [shared, swapped(shared), across]
     d_hidden_shared = shared_back_call(counts, where, weights, own, down_shared)
     left, right, shared, d_hidden_shared = together((left, right, shared, d_hidden_shared))
     own.append(jnp.concatenate([left, right], axis=1))
     other.append(swapped(own[-1]))
-    shared.append(swapped(shared[2]))
+    shared.append(lax.ppermute(shared[0], "node", [(n, n ^ 2) for n in range(counts[0])]))
     late = [block for pair in zip(own[4:], other[4:]) for block in pair]
     second = half_call(
-        counts, capacity, choices, len(early), where, weights, late, down_routed, hidden_routed, rows, first[3]
+        counts, capacity, choices, len(early), where, weights, late, down_routed, turned, rows, first[3]
     )
     rows, *second = second
-    d_gate = gates_call(counts, exchanged(second[3]), expert_ids.T).T
+    second[3], shared[2] = together((second[3], shared[2]))
+    shared.append(swapped(shared[2]))
+    parts = exchanged(second[3])
     d_down, d_hidden_routed, d_down_shared = last_call(
         counts, slot_total, where, rows, (None, *first[:3]), (None, *second[:3]), shared
     )
+    parts, d_down_shared = together((parts, d_down_shared))
+    d_gate = gates_call(counts, parts, expert_ids.T).T
     return (d_hidden_routed, d_down, d_gate, d_hidden_shared, d_down_shared)
 
 

time: 60 us -> 55.3 us (0.922)
  waiting for transfers between devices: 13.6 us -> 10.8 us
  starting transfers between devices: 19.6 us -> 17.9 us
  local copies, waits for them, and re-layouts: 3.94 us -> 2.84 us
  Pallas kernels: 21.6 us -> 22.6 us
    ppermute x8, waiting for transfers between devices: 12.6 us -> 10.2 us  [send(): return lax.ppermute(a, AXES, pairs)]
    pallas_call x1, Pallas kernels: 0.18 us -> 1.84 us  [pack_call(): pl.pallas_call(kernel, out_shape=jax.ShapeDtypeStruct((here, features + 1...]
    unnamed x21 -> x17, local copies, waits for them, and re-layouts: 3.9 us -> 2.81 us
    pallas_call x1, Pallas kernels: 9.27 us -> 8.3 us  [last_call(): pl.pallas_call(kernel, out_shape=(jax.ShapeDtypeStruct((experts, units, f...]
    ppermute x8, starting transfers between devices: 9.89 us -> 9.01 us  [send(): return lax.ppermute(a, AXES, pairs)]
    ppermute x10, starting transfers between devices: 2.14 us -> 1.47 us  [swapped(): return lax.ppermute(a, 'node', [(n, n ^ 1) for n in range(counts[0])])]
  transfers between devices with their start and end apart: 20 -> 20, of which waited for: 6 -> 6; matrix products, arithmetic and copies ran while one was open for 0% -> 0% of each run, Pallas kernels for 35% -> 37%
where the time goes in v4:
time: 55.3 us; the launch traced here: 55 us
  Pallas kernels  22.6 us (41%)
  starting transfers between devices  17.9 us (32%)
  waiting for transfers between devices  10.8 us (20%)
  local copies, waits for them, and re-layouts  2.84 us (5%)
  between operations  0.83 us (2%)
    ppermute x8, waiting for transfers between devices, send(): return lax.ppermute(a, AXES, pairs)  10.2 us
    ppermute x8, starting transfers between devices, send(): return lax.ppermute(a, AXES, pairs)  9.01 us
    pallas_call x1, Pallas kernels, last_call(): pl.pallas_call(kernel, out_shape=(jax.ShapeDtypeStruct((experts, units, f...  8.3 us
    pallas_call x2, Pallas kernels, half_call(): pl.pallas_call(kernel, out_shape=(jax.ShapeDtypeStruct((-(-ROWS_BYTES //...  8.16 us
    all_to_all x1, starting transfers between devices, exchanged(): return lax.all_to_all(a, AXES, split_axis=0, concat_axis=0, tiled=True)  5.8 us
    unnamed x17, local copies, waits for them, and re-layouts  2.81 us
    pallas_call x1, Pallas kernels, shared_back_call(): pl.pallas_call(kernel, out_shape=jax.ShapeDtypeStruct((tokens, units), BF...  2.63 us
    pallas_call x1, Pallas kernels, pack_call(): pl.pallas_call(kernel, out_shape=jax.ShapeDtypeStruct((here, features + 1...  1.84 us
  transfers between devices with their start and end apart: 20, of which 6 were waited for; matrix products, arithmetic and copies ran while one was open for 0% of the time, Pallas kernels for 37%

profile of v4, /device:TPU:0, one launch (start us, length us, event | category | flops | bytes accessed | tf_op | source)
XLA Modules:
  0.0 55.0 jit_solution(17873486604091293713)
XLA Ops:
  0.6 0.1 pad_add_fusion.where_ref
  0.7 0.0 slice-start
  0.7 1.8 %pack.1.refs_0_ = bf16[32,3712]{1,0:T(8,128)(2,1)} custom-call(bf16[32,3584]{1,0:T(8,128)(2,1)} %rows_ref.1, bf16[8,32]{1,0:T(8,128)(2,1)} %bitcast.10, s32[8,32]{1,0:T(8,128)} %bitcast.7), custom_call_target="tpu_custom_call" | custom-call | flops 1000000 | bytes 10000 | tf_op jit(solution)/shard_map/pack/pallas_call | solution.py:102
  2.6 0.0 copy-start
  2.6 0.0 slice-start.1
  2.6 3.1 %collective-permute-start.3 = (bf16[32,3712]{1,0:T(8,128)(2,1)}, bf16[32,3712]{1,0:T(8,128)(2,1)S(1)}, u32[]{:S(2)}, u32[]{:S(2)}) collective-permute-start(bf16[32,3712]{1,0:T(8,128)(2,1)} %pack.1.refs_0_), channel_id=1, source_target_pairs={{0,1},{4,5},{1,2},{5,6},{2,3},{6,7},{3,11},{7,15},{11,10},{15,14},... | collective-permute-start | bytes 712712 | tf_op jit(solution)/shard_map/ppermute | solution.py:498
  5.7 0.0 collective-permute-start
  5.7 0.0 copy-start.3
  5.7 1.2 %copy-done.3 = bf16[2,496,512]{2,1,0:T(8,128)(2,1)S(1)} copy-done((bf16[2,496,512]{2,1,0:T(8,128)(2,1)S(1)}, bf16[2,496,512]{2,1,0:T(8,128)(2,1)}, u32[]{:S(2)}) %copy-start.3) | copy-done | bytes 1015832
  6.9 0.0 copy-start.4
  6.9 0.9 %copy-done.4 = bf16[128,512]{1,0:T(8,128)(2,1)S(1)} copy-done((bf16[128,512]{1,0:T(8,128)(2,1)S(1)}, bf16[128,512]{1,0:T(8,128)(2,1)}, u32[]{:S(2)}) %copy-start.4) | copy-done | bytes 131096
  7.8 0.0 copy-start.5
  7.8 0.7 %copy-done.5 = s32[16]{0:T(128)S(1)} copy-done((s32[16]{0:T(128)S(1)}, s32[16]{0:T(128)}, u32[]{:S(2)}) %copy-start.5) | copy-done | bytes 88
  8.4 1.0 %weights.1 = (f32[8,512]{1,0:T(8,128)S(1)}, bf16[128,512]{1,0:T(8,128)(2,1)S(1)}, bf16[2,512,496]{2,1,0:T(8,128)(2,1)S(1)}) custom-call(s32[16]{0:T(128)S(1)} %copy-done.5, s32[2]{0:T(128)S(1)} %pad_add_fusion.where_ref, bf16[128,512]{1,0:T(8,128)(2,1)S(1)} %copy-done.4, bf16[2,496,512]{2,1,0:T(8,128)(2,1)S(1)} %copy-done.3), custom_call_target="tpu_custom_call" | custom-call | flops 20000000000 | bytes 1000000 | tf_op jit(solution)/shard_map/weights/pallas_call | solution.py:138
  9.5 2.1 %collective-permute-done.3.refs_2_.refs_1_ = bf16[32,3712]{1,0:T(8,128)(2,1)S(1)} collective-permute-done((bf16[32,3712]{1,0:T(8,128)(2,1)}, bf16[32,3712]{1,0:T(8,128)(2,1)S(1)}, u32[]{:S(2)}, u32[]{:S(2)}) %collective-permute-start.3) | collective-permute-done | bytes 237600 | tf_op jit(solution)/shard_map/ppermute | solution.py:498
  11.6 0.0 copy-start.2
  11.6 1.8 %collective-permute-start.4 = (bf16[32,3712]{1,0:T(8,128)(2,1)S(1)}, bf16[32,3712]{1,0:T(8,128)(2,1)S(1)}, u32[]{:S(2)}, u32[]{:S(2)}) collective-permute-start(bf16[32,3712]{1,0:T(8,128)(2,1)S(1)} %collective-permute-done.3.refs_2_.refs_1_), channel_id=1, source_target_pairs={{0,1},{4,5},{1,2},{5,6},{2,3},{6,7},{3,11},{7,15},{11,10},{15,14},... | collective-permute-start | bytes 712712 | tf_op jit(solution)/shard_map/ppermute | solution.py:498
  13.4 0.0 collective-permute-start.5
  13.4 0.0 copy-done
  13.4 0.5 collective-permute-start.8
  13.9 0.0 collective-permute-done.refs_4_.refs_2_
  13.9 0.2 collective-permute-start.1
  14.1 0.0 collective-permute-start.10
  14.1 0.6 %collective-permute-done.5.refs_7_ = bf16[128,512]{1,0:T(8,128)(2,1)S(1)} collective-permute-done((bf16[128,512]{1,0:T(8,128)(2,1)S(1)}, bf16[128,512]{1,0:T(8,128)(2,1)S(1)}, u32[]{:S(2)}, u32[]{:S(2)}) %collective-permute-start.5) | collective-permute-done | bytes 131104 | tf_op jit(solution)/shard_map/ppermute | solution.py:501
  14.7 0.1 collective-permute-start.9
  14.9 3.7 %collective-permute-done.4.refs_6_.refs_3_ = bf16[32,3712]{1,0:T(8,128)(2,1)S(1)} collective-permute-done((bf16[32,3712]{1,0:T(8,128)(2,1)S(1)}, bf16[32,3712]{1,0:T(8,128)(2,1)S(1)}, u32[]{:S(2)}, u32[]{:S(2)}) %collective-permute-start.4) | collective-permute-done | bytes 237600 | tf_op jit(solution)/shard_map/ppermute | solution.py:498
  18.6 0.0 collective-permute-start.11
  18.6 0.0 collective-permute-done.8.refs_1_
  18.6 1.5 %collective-permute-start.6 = (bf16[32,3712]{1,0:T(8,128)(2,1)S(1)}, bf16[32,3712]{1,0:T(8,128)(2,1)S(1)}, u32[]{:S(2)}, u32[]{:S(2)}) collective-permute-start(bf16[32,3712]{1,0:T(8,128)(2,1)S(1)} %collective-permute-done.4.refs_6_.refs_3_), channel_id=1, source_target_pairs={{0,1},{4,5},{1,2},{5,6},{2,3},{6,7},{3,11},{7,15},{11,10},{15,14},... | collective-permute-start | bytes 712712 | tf_op jit(solution)/shard_map/ppermute | solution.py:498
  20.0 1.6 %collective-permute-done.1.refs_4_.refs_0_ = bf16[32,3712]{1,0:T(8,128)(2,1)S(1)} collective-permute-done((bf16[32,3712]{1,0:T(8,128)(2,1)S(1)}, bf16[32,3712]{1,0:T(8,128)(2,1)S(1)}, u32[]{:S(2)}, u32[]{:S(2)}) %collective-permute-start.1) | collective-permute-done | bytes 237600 | tf_op jit(solution)/shard_map/ppermute | solution.py:498
  21.6 0.3 collective-permute-start.7
  21.9 0.0 collective-permute-done.10.refs_5_
  21.9 0.0 collective-permute-start.2
  21.9 0.0 collective-permute-done.9.refs_3_
  21.9 0.0 collective-permute-done.11.refs_7_
  22.0 0.0 slice-done
  22.0 0.0 slice-done.1
  22.0 3.8 %half_first.1 = (bf16[9655,3584]{1,0:T(8,128)(2,1)}, bf16[2,512,256]{2,1,0:T(8,128)(2,1)S(1)}, bf16[2,512,256]{2,1,0:T(8,128)(2,1)S(1)}, f32[8,256]{1,0:T(8,128)S(1)}, f32[16,2,32]{2,1,0:T(2,128)S(1)}) custom-call(s32[2]{0:T(128)S(1)} %pad_add_fusion.where_ref, bf16[32,3712]{1,0:T(8,128)(2,1)S(1)} %copy-done, ...), custom_call_target="tpu_custom_call" | custom-call | flops 6000000000 | bytes 1000000 | tf_op jit(solution)/shard_map/half_first/pallas_call | solution.py:238
  25.8 1.0 %collective-permute-done.6.refs_5_.refs_2_ = bf16[32,3712]{1,0:T(8,128)(2,1)S(1)} collective-permute-done((bf16[32,3712]{1,0:T(8,128)(2,1)S(1)}, bf16[32,3712]{1,0:T(8,128)(2,1)S(1)}, u32[]{:S(2)}, u32[]{:S(2)}) %collective-permute-start.6) | collective-permute-done | bytes 237600 | tf_op jit(solution)/shard_map/ppermute | solution.py:498
  26.8 1.8 %collective-permute-done.7.refs_6_.refs_4_ = bf16[32,3712]{1,0:T(8,128)(2,1)S(1)} collective-permute-done((bf16[32,3712]{1,0:T(8,128)(2,1)S(1)}, bf16[32,3712]{1,0:T(8,128)(2,1)S(1)}, u32[]{:S(2)}, u32[]{:S(2)}) %collective-permute-start.7) | collective-permute-done | bytes 237600 | tf_op jit(solution)/shard_map/ppermute | solution.py:498
  28.6 0.4 collective-permute-start.15
  29.0 1.7 %collective-permute-start.14 = (bf16[32,1792]{1,0:T(8,128)(2,1)S(1)}, bf16[32,1792]{1,0:T(8,128)(2,1)S(1)}, u32[]{:S(2)}, u32[]{:S(2)}) collective-permute-start(bf16[32,1792]{1,0:T(8,128)(2,1)S(1)} %slice.6), channel_id=1, source_target_pairs={{0,1},{4,5},{1,2},{5,6},{2,3},{6,7},{3,11},{7,15},{11,10},{15,14},... | collective-permute-start | bytes 344072 | tf_op jit(solution)/shard_map/ppermute | solution.py:498
  30.7 0.0 collective-permute-start.12
  30.7 0.5 collective-permute-start.13
  31.2 0.0 copy-done.2
  31.2 2.6 %shared_back.1 = bf16[128,512]{1,0:T(8,128)(2,1)} custom-call(s32[2]{0:T(128)S(1)} %pad_add_fusion.where_ref, bf16[32,3712]{1,0:T(8,128)(2,1)S(1)} %copy-done, bf16[32,3712]{1,0:T(8,128)(2,1)S(1)} %collective-permute-done.3.refs_2_.refs_1_, bf16[32,3712]{1,0:T(8,128)(2,1)S(1)} %collective-permute-done.refs_4_.refs_2_, ...), custom_call_target="tpu_custom_call" | custom-call | flops 3000000000 | bytes 1000000 | tf_op jit(solution)/shard_map/shared_back/pallas_call | solution.py:375
  33.8 0.0 collective-permute-done.14
  33.9 0.0 collective-permute-done.15
  33.9 0.1 collective-permute-start.16
  34.0 1.7 %collective-permute-start.17 = (bf16[128,512]{1,0:T(8,128)(2,1)S(1)}, bf16[128,512]{1,0:T(8,128)(2,1)S(1)}, u32[]{:S(2)}, u32[]{:S(2)}) collective-permute-start(bf16[128,512]{1,0:T(8,128)(2,1)S(1)} %get-tuple-element.68.refs_6_), channel_id=1, source_target_pairs={{0,8},{4,12},{8,0},{12,4},{1,9},{5,13},{9,1},{13,5},{2,10},{6,14},... | collective-permute-start | bytes 393224 | tf_op jit(solution)/shard_map/ppermute | solution.py:530
  35.6 0.0 collective-permute-done.2.refs_1_
  35.6 0.0 collective-permute-done.12.refs_3_
  35.6 0.0 collective-permute-done.13.refs_5_
  35.6 0.0 collective-permute-done.16.refs_7_
  35.6 4.4 %half_second.1 = (bf16[9655,3584]{1,0:T(8,128)(2,1)}, bf16[2,512,256]{2,1,0:T(8,128)(2,1)S(1)}, bf16[2,512,256]{2,1,0:T(8,128)(2,1)S(1)}, f32[8,256]{1,0:T(8,128)S(1)}, f32[16,2,32]{2,1,0:T(2,128)}) custom-call(s32[2]{0:T(128)S(1)} %pad_add_fusion.where_ref, ...), custom_call_target="tpu_custom_call", output_to_operand_aliasing={{0}: (12, {})} | custom-call | flops 6000000000 | bytes 1000000 | tf_op jit(solution)/shard_map/half_second/pallas_call | solution.py:238
  40.0 0.0 collective-permute-done.17.refs_8_
  40.0 0.2 collective-permute-start.18
  40.3 5.8 %all-to-all-start = ((f32[16,2,32]{2,1,0:T(2,128)}), f32[16,2,32]{2,1,0:T(2,128)S(1)}, u32[]{:S(2)}, u32[]{:S(2)}) async-start(f32[16,2,32]{2,1,0:T(2,128)} %get-tuple-element.74), calls=%async_computation | async-start | bytes 32768 | tf_op jit(solution)/shard_map/all_to_all | solution.py:412
  46.1 0.0 collective-permute-done.18.refs_9_
  46.1 0.0 copy-start.1
  46.1 8.3 %last.1 = (bf16[2,512,3584]{2,1,0:T(8,128)(2,1)}, bf16[2,496,512]{2,1,0:T(8,128)(2,1)}, bf16[512,896]{1,0:T(8,128)(2,1)}) custom-call(s32[2]{0:T(128)S(1)} %pad_add_fusion.where_ref, bf16[9655,3584]{1,0:T(8,128)(2,1)} %get-tuple-element.61.rows_ref, bf16[2,512,256]{2,1,0:T(8,128)(2,1)S(1)} %get-tuple-element.62.refs_0_, ...), custom_call_target="tpu_custom_call" | custom-call | flops 8000000000 | bytes 10000000 | tf_op jit(solution)/shard_map/last/pallas_call | solution.py:330
  54.4 0.0 all-to-all-done.parts_ref
  54.4 0.0 copy-done.1
  54.4 0.6 %gates.1 = f32[8,32]{1,0:T(8,128)} custom-call(s32[8,32]{1,0:T(8,128)S(1)} %bitcast.8, f32[16,2,32]{2,1,0:T(2,128)S(1)} %all-to-all-done.parts_ref), custom_call_target="tpu_custom_call" | custom-call | flops 1000000 | bytes 10000 | tf_op jit(solution)/shard_map/gates/pallas_call | solution.py:400
  (5 shorter events, 0.0 us)
Async XLA Ops:
  0.7 21.2 %slice-start = ((s8[7340032]{0:T(1024)(128)(4,1)}), s8[3145728]{0:T(1024)(128)(4,1)S(1)}, s32[]{:S(2)}) async-start(s8[7340032]{0:T(1024)(128)(4,1)} %bitcast.5), calls=%async_computation.1 | async-start | bytes 6291456
  2.6 10.8 %copy-start = (bf16[32,3712]{1,0:T(8,128)(2,1)S(1)}, bf16[32,3712]{1,0:T(8,128)(2,1)}, u32[]{:S(2)}) copy-start(bf16[32,3712]{1,0:T(8,128)(2,1)} %pack.1.refs_0_) | copy-start | bytes 712708
  2.6 19.4 %slice-start.1 = ((s8[7340032]{0:T(1024)(128)(4,1)}), s8[4194304]{0:T(1024)(128)(4,1)S(1)}, s32[]{:S(2)}) async-start(s8[7340032]{0:T(1024)(128)(4,1)} %bitcast.5), calls=%async_computation.2 | async-start | bytes 8388608
  2.6 9.0 %collective-permute-start.3 = (bf16[32,3712]{1,0:T(8,128)(2,1)}, bf16[32,3712]{1,0:T(8,128)(2,1)S(1)}, u32[]{:S(2)}, u32[]{:S(2)}) collective-permute-start(bf16[32,3712]{1,0:T(8,128)(2,1)} %pack.1.refs_0_), channel_id=1, source_target_pairs={{0,1},{4,5},{1,2},{5,6},{2,3},{6,7},{3,11},{7,15},{11,10},{15,14},... | collective-permute-start | bytes 712712 | tf_op jit(solution)/shard_map/ppermute | solution.py:498
  5.7 8.2 %collective-permute-start = (bf16[32,3712]{1,0:T(8,128)(2,1)}, bf16[32,3712]{1,0:T(8,128)(2,1)S(1)}, u32[]{:S(2)}, u32[]{:S(2)}) collective-permute-start(bf16[32,3712]{1,0:T(8,128)(2,1)} %pack.1.refs_0_), channel_id=1, source_target_pairs={{0,8},{4,12},{1,0},{5,4},{2,1},{6,5},{3,2},{7,6},{11,3},{15,7},{10... | collective-permute-start | bytes 712712 | tf_op jit(solution)/shard_map/ppermute | solution.py:498
  5.7 1.2 %copy-start.3 = (bf16[2,496,512]{2,1,0:T(8,128)(2,1)S(1)}, bf16[2,496,512]{2,1,0:T(8,128)(2,1)}, u32[]{:S(2)}) copy-start(bf16[2,496,512]{2,1,0:T(8,128)(2,1)} %hidden_ref.1) | copy-start | bytes 3047428
  6.9 0.9 %copy-start.4 = (bf16[128,512]{1,0:T(8,128)(2,1)S(1)}, bf16[128,512]{1,0:T(8,128)(2,1)}, u32[]{:S(2)}) copy-start(bf16[128,512]{1,0:T(8,128)(2,1)} %shared_ref.1) | copy-start | bytes 393220
  7.8 0.7 %copy-start.5 = (s32[16]{0:T(128)S(1)}, s32[16]{0:T(128)}, u32[]{:S(2)}) copy-start(s32[16]{0:T(128)} %lens_ref.1) | copy-start | bytes 196
  11.6 19.6 %copy-start.2 = (bf16[512,3584]{1,0:T(8,128)(2,1)S(1)}, bf16[512,3584]{1,0:T(8,128)(2,1)}, u32[]{:S(2)}) copy-start(bf16[512,3584]{1,0:T(8,128)(2,1)} %refs_8_.1) | copy-start | bytes 11010052
  11.6 7.0 %collective-permute-start.4 = (bf16[32,3712]{1,0:T(8,128)(2,1)S(1)}, bf16[32,3712]{1,0:T(8,128)(2,1)S(1)}, u32[]{:S(2)}, u32[]{:S(2)}) collective-permute-start(bf16[32,3712]{1,0:T(8,128)(2,1)S(1)} %collective-permute-done.3.refs_2_.refs_1_), channel_id=1, source_target_pairs={{0,1},{4,5},{1,2},{5,6},{2,3},{6,7},{3,11},{7,15},{11,10},{15,14},... | collective-permute-start | bytes 712712 | tf_op jit(solution)/shard_map/ppermute | solution.py:498
  13.4 1.3 %collective-permute-start.5 = (bf16[128,512]{1,0:T(8,128)(2,1)S(1)}, bf16[128,512]{1,0:T(8,128)(2,1)S(1)}, u32[]{:S(2)}, u32[]{:S(2)}) collective-permute-start(bf16[128,512]{1,0:T(8,128)(2,1)S(1)} %get-tuple-element.68.refs_6_), channel_id=1, source_target_pairs={{0,4},{4,0},{8,12},{12,8},{1,5},{5,1},{9,13},{13,9},{2,6},{6,2},{1... | collective-permute-start | bytes 393224 | tf_op jit(solution)/shard_map/ppermute | solution.py:501
  13.4 5.2 %collective-permute-start.8 = (bf16[32,3712]{1,0:T(8,128)(2,1)S(1)}, bf16[32,3712]{1,0:T(8,128)(2,1)S(1)}, u32[]{:S(2)}, u32[]{:S(2)}) collective-permute-start(bf16[32,3712]{1,0:T(8,128)(2,1)S(1)} %copy-done), channel_id=1, source_target_pairs={{0,4},{4,0},{8,12},{12,8},{1,5},{5,1},{9,13},{13,9},{2,6},{6,2},{1... | collective-permute-start | bytes 712712 | tf_op jit(solution)/shard_map/ppermute | solution.py:501
  13.9 7.7 %collective-permute-start.1 = (bf16[32,3712]{1,0:T(8,128)(2,1)S(1)}, bf16[32,3712]{1,0:T(8,128)(2,1)S(1)}, u32[]{:S(2)}, u32[]{:S(2)}) collective-permute-start(bf16[32,3712]{1,0:T(8,128)(2,1)S(1)} %collective-permute-done.refs_4_.refs_2_), channel_id=1, source_target_pairs={{0,8},{4,12},{1,0},{5,4},{2,1},{6,5},{3,2},{7,6},{11,3},{15,7},{10... | collective-permute-start | bytes 712712 | tf_op jit(solution)/shard_map/ppermute | solution.py:498
  14.1 7.8 %collective-permute-start.10 = (bf16[32,3712]{1,0:T(8,128)(2,1)S(1)}, bf16[32,3712]{1,0:T(8,128)(2,1)S(1)}, u32[]{:S(2)}, u32[]{:S(2)}) collective-permute-start(bf16[32,3712]{1,0:T(8,128)(2,1)S(1)} %collective-permute-done.refs_4_.refs_2_), channel_id=1, source_target_pairs={{0,4},{4,0},{8,12},{12,8},{1,5},{5,1},{9,13},{13,9},{2,6},{6,2},{1... | collective-permute-start | bytes 712712 | tf_op jit(solution)/shard_map/ppermute | solution.py:501
  14.7 7.2 %collective-permute-start.9 = (bf16[32,3712]{1,0:T(8,128)(2,1)S(1)}, bf16[32,3712]{1,0:T(8,128)(2,1)S(1)}, u32[]{:S(2)}, u32[]{:S(2)}) collective-permute-start(bf16[32,3712]{1,0:T(8,128)(2,1)S(1)} %collective-permute-done.3.refs_2_.refs_1_), channel_id=1, source_target_pairs={{0,4},{4,0},{8,12},{12,8},{1,5},{5,1},{9,13},{13,9},{2,6},{6,2},{1... | collective-permute-start | bytes 712712 | tf_op jit(solution)/shard_map/ppermute | solution.py:501
  18.6 3.4 %collective-permute-start.11 = (bf16[32,3712]{1,0:T(8,128)(2,1)S(1)}, bf16[32,3712]{1,0:T(8,128)(2,1)S(1)}, u32[]{:S(2)}, u32[]{:S(2)}) collective-permute-start(bf16[32,3712]{1,0:T(8,128)(2,1)S(1)} %collective-permute-done.4.refs_6_.refs_3_), channel_id=1, source_target_pairs={{0,4},{4,0},{8,12},{12,8},{1,5},{5,1},{9,13},{13,9},{2,6},{6,2},{1... | collective-permute-start | bytes 712712 | tf_op jit(solution)/shard_map/ppermute | solution.py:501
  18.6 8.2 %collective-permute-start.6 = (bf16[32,3712]{1,0:T(8,128)(2,1)S(1)}, bf16[32,3712]{1,0:T(8,128)(2,1)S(1)}, u32[]{:S(2)}, u32[]{:S(2)}) collective-permute-start(bf16[32,3712]{1,0:T(8,128)(2,1)S(1)} %collective-permute-done.4.refs_6_.refs_3_), channel_id=1, source_target_pairs={{0,1},{4,5},{1,2},{5,6},{2,3},{6,7},{3,11},{7,15},{11,10},{15,14},... | collective-permute-start | bytes 712712 | tf_op jit(solution)/shard_map/ppermute | solution.py:498
  21.6 6.9 %collective-permute-start.7 = (bf16[32,3712]{1,0:T(8,128)(2,1)S(1)}, bf16[32,3712]{1,0:T(8,128)(2,1)S(1)}, u32[]{:S(2)}, u32[]{:S(2)}) collective-permute-start(bf16[32,3712]{1,0:T(8,128)(2,1)S(1)} %collective-permute-done.1.refs_4_.refs_0_), channel_id=1, source_target_pairs={{0,8},{4,12},{1,0},{5,4},{2,1},{6,5},{3,2},{7,6},{11,3},{15,7},{10... | collective-permute-start | bytes 712712 | tf_op jit(solution)/shard_map/ppermute | solution.py:498
  21.9 13.7 %collective-permute-start.2 = (bf16[32,3712]{1,0:T(8,128)(2,1)S(1)}, bf16[32,3712]{1,0:T(8,128)(2,1)S(1)}, u32[]{:S(2)}, u32[]{:S(2)}) collective-permute-start(bf16[32,3712]{1,0:T(8,128)(2,1)S(1)} %collective-permute-done.1.refs_4_.refs_0_), channel_id=1, source_target_pairs={{0,4},{4,0},{8,12},{12,8},{1,5},{5,1},{9,13},{13,9},{2,6},{6,2},{1... | collective-permute-start | bytes 712712 | tf_op jit(solution)/shard_map/ppermute | solution.py:501
  28.6 5.3 %collective-permute-start.15 = (bf16[32,1920]{1,0:T(8,128)(2,1)S(1)}, bf16[32,1920]{1,0:T(8,128)(2,1)S(1)}, u32[]{:S(2)}, u32[]{:S(2)}) collective-permute-start(bf16[32,1920]{1,0:T(8,128)(2,1)S(1)} %slice.7), channel_id=1, source_target_pairs={{0,8},{4,12},{1,0},{5,4},{2,1},{6,5},{3,2},{7,6},{11,3},{15,7},{10... | collective-permute-start | bytes 368648 | tf_op jit(solution)/shard_map/ppermute | solution.py:498
  29.0 4.9 %collective-permute-start.14 = (bf16[32,1792]{1,0:T(8,128)(2,1)S(1)}, bf16[32,1792]{1,0:T(8,128)(2,1)S(1)}, u32[]{:S(2)}, u32[]{:S(2)}) collective-permute-start(bf16[32,1792]{1,0:T(8,128)(2,1)S(1)} %slice.6), channel_id=1, source_target_pairs={{0,1},{4,5},{1,2},{5,6},{2,3},{6,7},{3,11},{7,15},{11,10},{15,14},... | collective-permute-start | bytes 344072 | tf_op jit(solution)/shard_map/ppermute | solution.py:498
  30.7 4.9 %collective-permute-start.12 = (bf16[32,3712]{1,0:T(8,128)(2,1)S(1)}, bf16[32,3712]{1,0:T(8,128)(2,1)S(1)}, u32[]{:S(2)}, u32[]{:S(2)}) collective-permute-start(bf16[32,3712]{1,0:T(8,128)(2,1)S(1)} %collective-permute-done.6.refs_5_.refs_2_), channel_id=1, source_target_pairs={{0,4},{4,0},{8,12},{12,8},{1,5},{5,1},{9,13},{13,9},{2,6},{6,2},{1... | collective-permute-start | bytes 712712 | tf_op jit(solution)/shard_map/ppermute | solution.py:501
  30.7 4.9 %collective-permute-start.13 = (bf16[32,3712]{1,0:T(8,128)(2,1)S(1)}, bf16[32,3712]{1,0:T(8,128)(2,1)S(1)}, u32[]{:S(2)}, u32[]{:S(2)}) collective-permute-start(bf16[32,3712]{1,0:T(8,128)(2,1)S(1)} %collective-permute-done.7.refs_6_.refs_4_), channel_id=1, source_target_pairs={{0,4},{4,0},{8,12},{12,8},{1,5},{5,1},{9,13},{13,9},{2,6},{6,2},{1... | collective-permute-start | bytes 712712 | tf_op jit(solution)/shard_map/ppermute | solution.py:501
  33.9 1.7 %collective-permute-start.16 = (bf16[32,3712]{1,0:T(8,128)(2,1)S(1)}, bf16[32,3712]{1,0:T(8,128)(2,1)S(1)}, u32[]{:S(2)}, u32[]{:S(2)}) collective-permute-start(bf16[32,3712]{1,0:T(8,128)(2,1)S(1)} %constant_dynamic-update-slice_fusion.refs_6_), channel_id=1, source_target_pairs={{0,4},{4,0},{8,12},{12,8},{1,5},{5,1},{9,13},{13,9},{2,6},{6,2},{1... | collective-permute-start | bytes 712712 | tf_op jit(solution)/shard_map/ppermute | solution.py:501
  34.0 6.1 %collective-permute-start.17 = (bf16[128,512]{1,0:T(8,128)(2,1)S(1)}, bf16[128,512]{1,0:T(8,128)(2,1)S(1)}, u32[]{:S(2)}, u32[]{:S(2)}) collective-permute-start(bf16[128,512]{1,0:T(8,128)(2,1)S(1)} %get-tuple-element.68.refs_6_), channel_id=1, source_target_pairs={{0,8},{4,12},{8,0},{12,4},{1,9},{5,13},{9,1},{13,5},{2,10},{6,14},... | collective-permute-start | bytes 393224 | tf_op jit(solution)/shard_map/ppermute | solution.py:530
  40.0 6.0 %collective-permute-start.18 = (bf16[128,512]{1,0:T(8,128)(2,1)S(1)}, bf16[128,512]{1,0:T(8,128)(2,1)S(1)}, u32[]{:S(2)}, u32[]{:S(2)}) collective-permute-start(bf16[128,512]{1,0:T(8,128)(2,1)S(1)} %collective-permute-done.17.refs_8_), channel_id=1, source_target_pairs={{0,4},{4,0},{8,12},{12,8},{1,5},{5,1},{9,13},{13,9},{2,6},{6,2},{1... | collective-permute-start | bytes 393224 | tf_op jit(solution)/shard_map/ppermute | solution.py:501
  40.3 14.1 %all-to-all-start = ((f32[16,2,32]{2,1,0:T(2,128)}), f32[16,2,32]{2,1,0:T(2,128)S(1)}, u32[]{:S(2)}, u32[]{:S(2)}) async-start(f32[16,2,32]{2,1,0:T(2,128)} %get-tuple-element.74), calls=%async_computation | async-start | bytes 32768 | tf_op jit(solution)/shard_map/all_to_all | solution.py:412
  46.1 8.3 %copy-start.1 = (s32[32,8]{0,1:T(8,128)S(1)}, s32[32,8]{0,1:T(8,128)}, u32[]{:S(2)}) copy-start(s32[32,8]{0,1:T(8,128)} %param.11) | copy-start | bytes 3076

commit v5 on v4

--- a/solution.py
+++ b/solution.py
@@ -519,9 +519,9 @@
         counts, capacity, choices, 0, where, weights, early, down_routed, turned, None, None
     )
     rows, *first = first
-    forth[3], back[3], first[3] = together((forth[3], back[3], first[3]))
+    forth[3], first[3] = together((forth[3], first[3]))
     own[-2:] = forth[3], back[3]
-    split = features // 2 // 128 * 128
+    split = features * 5 // 8 // 128 * 128
     left, right = send(forth[3][:, :split], up), send(back[3][:, split:], down)
     d_hidden_shared = shared_back_call(counts, where, weights, own, down_shared)
     left, right, shared, d_hidden_shared = together((left, right, shared, d_hidden_shared))

time: 55.3 us -> 53.7 us (0.971)
  starting transfers between devices: 17.9 us -> 15.8 us
    ppermute x1, starting transfers between devices: 1.65 us -> 0.56 us  [body(): lax.ppermute(shared[0], 'node', [(n, n ^ 2) for n in range(counts[0])])]
    ppermute x10, waiting for transfers between devices: 0.62 us -> 1.54 us  [swapped(): return lax.ppermute(a, 'node', [(n, n ^ 1) for n in range(counts[0])])]
    all_to_all x1, starting transfers between devices: 5.8 us -> 5.03 us  [exchanged(): return lax.all_to_all(a, AXES, split_axis=0, concat_axis=0, tiled=True)]
  transfers between devices with their start and end apart: 20 -> 20, of which waited for: 6 -> 8; matrix products, arithmetic and copies ran while one was open for 0% -> 0% of each run, Pallas kernels for 37% -> 38%
where the time goes in v5:
time: 53.7 us; the launch traced here: 53.4 us
  Pallas kernels  22.6 us (42%)
  starting transfers between devices  15.8 us (29%)
  waiting for transfers between devices  11.3 us (21%)
  local copies, waits for them, and re-layouts  2.84 us (5%)
  between operations  0.82 us (2%)
    ppermute x8, waiting for transfers between devices, send(): return lax.ppermute(a, AXES, pairs)  9.73 us
    ppermute x8, starting transfers between devices, send(): return lax.ppermute(a, AXES, pairs)  8.81 us
    pallas_call x1, Pallas kernels, last_call(): pl.pallas_call(kernel, out_shape=(jax.ShapeDtypeStruct((experts, units, f...  8.3 us
    pallas_call x2, Pallas kernels, half_call(): pl.pallas_call(kernel, out_shape=(jax.ShapeDtypeStruct((-(-ROWS_BYTES //...  8.15 us
    all_to_all x1, starting transfers between devices, exchanged(): return lax.all_to_all(a, AXES, split_axis=0, concat_axis=0, tiled=True)  5.03 us
    unnamed x17, local copies, waits for them, and re-layouts  2.81 us
    pallas_call x1, Pallas kernels, shared_back_call(): pl.pallas_call(kernel, out_shape=jax.ShapeDtypeStruct((tokens, units), BF...  2.63 us
    pallas_call x1, Pallas kernels, pack_call(): pl.pallas_call(kernel, out_shape=jax.ShapeDtypeStruct((here, features + 1...  1.84 us
  transfers between devices with their start and end apart: 20, of which 8 were waited for; matrix products, arithmetic and copies ran while one was open for 0% of the time, Pallas kernels for 38%

profile of v5, /device:TPU:0, one launch (start us, length us, event | category | flops | bytes accessed | tf_op | source)
XLA Modules:
  0.0 53.4 jit_solution(9450606171672739603)
XLA Ops:
  0.6 0.1 pad_add_fusion.where_ref
  0.7 0.0 slice-start
  0.7 1.8 %pack.1.refs_0_ = bf16[32,3712]{1,0:T(8,128)(2,1)} custom-call(bf16[32,3584]{1,0:T(8,128)(2,1)} %rows_ref.1, bf16[8,32]{1,0:T(8,128)(2,1)} %bitcast.10, s32[8,32]{1,0:T(8,128)} %bitcast.7), custom_call_target="tpu_custom_call" | custom-call | flops 1000000 | bytes 10000 | tf_op jit(solution)/shard_map/pack/pallas_call | solution.py:102
  2.6 0.0 copy-start
  2.6 0.0 slice-start.1
  2.6 3.1 %collective-permute-start.3 = (bf16[32,3712]{1,0:T(8,128)(2,1)}, bf16[32,3712]{1,0:T(8,128)(2,1)S(1)}, u32[]{:S(2)}, u32[]{:S(2)}) collective-permute-start(bf16[32,3712]{1,0:T(8,128)(2,1)} %pack.1.refs_0_), channel_id=1, source_target_pairs={{0,1},{4,5},{1,2},{5,6},{2,3},{6,7},{3,11},{7,15},{11,10},{15,14},... | collective-permute-start | bytes 712712 | tf_op jit(solution)/shard_map/ppermute | solution.py:498
  5.7 0.0 collective-permute-start
  5.7 0.0 copy-start.3
  5.7 1.2 %copy-done.3 = bf16[2,496,512]{2,1,0:T(8,128)(2,1)S(1)} copy-done((bf16[2,496,512]{2,1,0:T(8,128)(2,1)S(1)}, bf16[2,496,512]{2,1,0:T(8,128)(2,1)}, u32[]{:S(2)}) %copy-start.3) | copy-done | bytes 1015832
  6.9 0.0 copy-start.4
  6.9 0.9 %copy-done.4 = bf16[128,512]{1,0:T(8,128)(2,1)S(1)} copy-done((bf16[128,512]{1,0:T(8,128)(2,1)S(1)}, bf16[128,512]{1,0:T(8,128)(2,1)}, u32[]{:S(2)}) %copy-start.4) | copy-done | bytes 131096
  7.8 0.0 copy-start.5
  7.8 0.7 %copy-done.5 = s32[16]{0:T(128)S(1)} copy-done((s32[16]{0:T(128)S(1)}, s32[16]{0:T(128)}, u32[]{:S(2)}) %copy-start.5) | copy-done | bytes 88
  8.4 1.0 %weights.1 = (f32[8,512]{1,0:T(8,128)S(1)}, bf16[128,512]{1,0:T(8,128)(2,1)S(1)}, bf16[2,512,496]{2,1,0:T(8,128)(2,1)S(1)}) custom-call(s32[16]{0:T(128)S(1)} %copy-done.5, s32[2]{0:T(128)S(1)} %pad_add_fusion.where_ref, bf16[128,512]{1,0:T(8,128)(2,1)S(1)} %copy-done.4, bf16[2,496,512]{2,1,0:T(8,128)(2,1)S(1)} %copy-done.3), custom_call_target="tpu_custom_call" | custom-call | flops 20000000000 | bytes 1000000 | tf_op jit(solution)/shard_map/weights/pallas_call | solution.py:138
  9.5 2.1 %collective-permute-done.3.refs_2_.refs_1_ = bf16[32,3712]{1,0:T(8,128)(2,1)S(1)} collective-permute-done((bf16[32,3712]{1,0:T(8,128)(2,1)}, bf16[32,3712]{1,0:T(8,128)(2,1)S(1)}, u32[]{:S(2)}, u32[]{:S(2)}) %collective-permute-start.3) | collective-permute-done | bytes 237600 | tf_op jit(solution)/shard_map/ppermute | solution.py:498
  11.6 0.0 copy-start.2
  11.6 1.8 %collective-permute-start.4 = (bf16[32,3712]{1,0:T(8,128)(2,1)S(1)}, bf16[32,3712]{1,0:T(8,128)(2,1)S(1)}, u32[]{:S(2)}, u32[]{:S(2)}) collective-permute-start(bf16[32,3712]{1,0:T(8,128)(2,1)S(1)} %collective-permute-done.3.refs_2_.refs_1_), channel_id=1, source_target_pairs={{0,1},{4,5},{1,2},{5,6},{2,3},{6,7},{3,11},{7,15},{11,10},{15,14},... | collective-permute-start | bytes 712712 | tf_op jit(solution)/shard_map/ppermute | solution.py:498
  13.4 0.0 collective-permute-start.5
  13.4 0.0 copy-done
  13.4 0.5 collective-permute-start.7
  13.9 0.0 collective-permute-done.refs_4_.refs_2_
  13.9 0.2 collective-permute-start.1
  14.1 0.0 collective-permute-start.9
  14.1 0.6 %collective-permute-done.5.refs_7_ = bf16[128,512]{1,0:T(8,128)(2,1)S(1)} collective-permute-done((bf16[128,512]{1,0:T(8,128)(2,1)S(1)}, bf16[128,512]{1,0:T(8,128)(2,1)S(1)}, u32[]{:S(2)}, u32[]{:S(2)}) %collective-permute-start.5) | collective-permute-done | bytes 131104 | tf_op jit(solution)/shard_map/ppermute | solution.py:501
  14.7 0.1 collective-permute-start.8
  14.9 3.7 %collective-permute-done.4.refs_6_.refs_3_ = bf16[32,3712]{1,0:T(8,128)(2,1)S(1)} collective-permute-done((bf16[32,3712]{1,0:T(8,128)(2,1)S(1)}, bf16[32,3712]{1,0:T(8,128)(2,1)S(1)}, u32[]{:S(2)}, u32[]{:S(2)}) %collective-permute-start.4) | collective-permute-done | bytes 237600 | tf_op jit(solution)/shard_map/ppermute | solution.py:498
  18.6 0.0 collective-permute-start.10
  18.6 0.0 collective-permute-done.7.refs_1_
  18.6 1.5 %collective-permute-start.6 = (bf16[32,3712]{1,0:T(8,128)(2,1)S(1)}, bf16[32,3712]{1,0:T(8,128)(2,1)S(1)}, u32[]{:S(2)}, u32[]{:S(2)}) collective-permute-start(bf16[32,3712]{1,0:T(8,128)(2,1)S(1)} %collective-permute-done.4.refs_6_.refs_3_), channel_id=1, source_target_pairs={{0,1},{4,5},{1,2},{5,6},{2,3},{6,7},{3,11},{7,15},{11,10},{15,14},... | collective-permute-start | bytes 712712 | tf_op jit(solution)/shard_map/ppermute | solution.py:498
  20.0 1.6 %collective-permute-done.1.refs_4_.refs_0_ = bf16[32,3712]{1,0:T(8,128)(2,1)S(1)} collective-permute-done((bf16[32,3712]{1,0:T(8,128)(2,1)S(1)}, bf16[32,3712]{1,0:T(8,128)(2,1)S(1)}, u32[]{:S(2)}, u32[]{:S(2)}) %collective-permute-start.1) | collective-permute-done | bytes 237600 | tf_op jit(solution)/shard_map/ppermute | solution.py:498
  21.6 0.3 collective-permute-start.12
  21.9 0.0 collective-permute-done.9.refs_5_
  21.9 0.0 collective-permute-start.2
  21.9 0.0 collective-permute-done.8.refs_3_
  21.9 0.0 collective-permute-done.10.refs_7_
  22.0 0.0 slice-done
  22.0 0.0 slice-done.1
  22.0 3.8 %half_first.1 = (bf16[9655,3584]{1,0:T(8,128)(2,1)}, bf16[2,512,256]{2,1,0:T(8,128)(2,1)S(1)}, bf16[2,512,256]{2,1,0:T(8,128)(2,1)S(1)}, f32[8,256]{1,0:T(8,128)S(1)}, f32[16,2,32]{2,1,0:T(2,128)S(1)}) custom-call(s32[2]{0:T(128)S(1)} %pad_add_fusion.where_ref, bf16[32,3712]{1,0:T(8,128)(2,1)S(1)} %copy-done, ...), custom_call_target="tpu_custom_call" | custom-call | flops 6000000000 | bytes 1000000 | tf_op jit(solution)/shard_map/half_first/pallas_call | solution.py:238
  25.8 1.0 %collective-permute-done.6.refs_5_.refs_2_ = bf16[32,3712]{1,0:T(8,128)(2,1)S(1)} collective-permute-done((bf16[32,3712]{1,0:T(8,128)(2,1)S(1)}, bf16[32,3712]{1,0:T(8,128)(2,1)S(1)}, u32[]{:S(2)}, u32[]{:S(2)}) %collective-permute-start.6) | collective-permute-done | bytes 237600 | tf_op jit(solution)/shard_map/ppermute | solution.py:498
  26.8 1.5 %collective-permute-start.14 = (bf16[32,2176]{1,0:T(8,128)(2,1)S(1)}, bf16[32,2176]{1,0:T(8,128)(2,1)S(1)}, u32[]{:S(2)}, u32[]{:S(2)}) collective-permute-start(bf16[32,2176]{1,0:T(8,128)(2,1)S(1)} %slice.6), channel_id=1, source_target_pairs={{0,1},{4,5},{1,2},{5,6},{2,3},{6,7},{3,11},{7,15},{11,10},{15,14},... | collective-permute-start | bytes 417800 | tf_op jit(solution)/shard_map/ppermute | solution.py:498
  28.3 0.2 collective-permute-done.12.refs_6_.refs_4_
  28.6 0.4 collective-permute-start.15
  29.0 0.0 collective-permute-start.11
  29.0 0.5 collective-permute-start.13
  29.5 0.0 copy-done.2
  29.5 2.6 %shared_back.1 = bf16[128,512]{1,0:T(8,128)(2,1)} custom-call(s32[2]{0:T(128)S(1)} %pad_add_fusion.where_ref, bf16[32,3712]{1,0:T(8,128)(2,1)S(1)} %copy-done, bf16[32,3712]{1,0:T(8,128)(2,1)S(1)} %collective-permute-done.3.refs_2_.refs_1_, bf16[32,3712]{1,0:T(8,128)(2,1)S(1)} %collective-permute-done.refs_4_.refs_2_, ...), custom_call_target="tpu_custom_call" | custom-call | flops 3000000000 | bytes 1000000 | tf_op jit(solution)/shard_map/shared_back/pallas_call | solution.py:375
  32.1 1.1 %collective-permute-done.15 = bf16[32,1536]{1,0:T(8,128)(2,1)S(1)} collective-permute-done((bf16[32,1536]{1,0:T(8,128)(2,1)S(1)}, bf16[32,1536]{1,0:T(8,128)(2,1)S(1)}, u32[]{:S(2)}, u32[]{:S(2)}) %collective-permute-start.15) | collective-permute-done | bytes 98336 | tf_op jit(solution)/shard_map/ppermute | solution.py:498
  33.2 0.0 collective-permute-done.14
  33.3 0.1 collective-permute-start.16
  33.3 0.6 %collective-permute-start.17 = (bf16[128,512]{1,0:T(8,128)(2,1)S(1)}, bf16[128,512]{1,0:T(8,128)(2,1)S(1)}, u32[]{:S(2)}, u32[]{:S(2)}) collective-permute-start(bf16[128,512]{1,0:T(8,128)(2,1)S(1)} %get-tuple-element.66.refs_6_), channel_id=1, source_target_pairs={{0,8},{4,12},{8,0},{12,4},{1,9},{5,13},{9,1},{13,5},{2,10},{6,14},... | collective-permute-start | bytes 393224 | tf_op jit(solution)/shard_map/ppermute | solution.py:530
  33.9 0.0 collective-permute-done.2.refs_1_
  33.9 0.0 collective-permute-done.11.refs_3_
  33.9 0.0 collective-permute-done.13.refs_5_
  33.9 0.9 %collective-permute-done.16.refs_7_ = bf16[32,3712]{1,0:T(8,128)(2,1)S(1)} collective-permute-done((bf16[32,3712]{1,0:T(8,128)(2,1)S(1)}, bf16[32,3712]{1,0:T(8,128)(2,1)S(1)}, u32[]{:S(2)}, u32[]{:S(2)}) %collective-permute-start.16) | collective-permute-done | bytes 237600 | tf_op jit(solution)/shard_map/ppermute | solution.py:501
  34.8 4.4 %half_second.1 = (bf16[9655,3584]{1,0:T(8,128)(2,1)}, bf16[2,512,256]{2,1,0:T(8,128)(2,1)S(1)}, bf16[2,512,256]{2,1,0:T(8,128)(2,1)S(1)}, f32[8,256]{1,0:T(8,128)S(1)}, f32[16,2,32]{2,1,0:T(2,128)}) custom-call(s32[2]{0:T(128)S(1)} %pad_add_fusion.where_ref, ...), custom_call_target="tpu_custom_call", output_to_operand_aliasing={{0}: (12, {})} | custom-call | flops 6000000000 | bytes 1000000 | tf_op jit(solution)/shard_map/half_second/pallas_call | solution.py:238
  39.2 0.1 collective-permute-done.17.refs_8_
  39.3 0.2 collective-permute-start.18
  39.4 5.0 %all-to-all-start = ((f32[16,2,32]{2,1,0:T(2,128)}), f32[16,2,32]{2,1,0:T(2,128)S(1)}, u32[]{:S(2)}, u32[]{:S(2)}) async-start(f32[16,2,32]{2,1,0:T(2,128)} %get-tuple-element.72), calls=%async_computation | async-start | bytes 32768 | tf_op jit(solution)/shard_map/all_to_all | solution.py:412
  44.5 0.0 collective-permute-done.18.refs_9_
  44.5 0.0 copy-start.1
  44.5 8.3 %last.1 = (bf16[2,512,3584]{2,1,0:T(8,128)(2,1)}, bf16[2,496,512]{2,1,0:T(8,128)(2,1)}, bf16[512,896]{1,0:T(8,128)(2,1)}) custom-call(s32[2]{0:T(128)S(1)} %pad_add_fusion.where_ref, bf16[9655,3584]{1,0:T(8,128)(2,1)} %get-tuple-element.59.rows_ref, bf16[2,512,256]{2,1,0:T(8,128)(2,1)S(1)} %get-tuple-element.60.refs_0_, ...), custom_call_target="tpu_custom_call" | custom-call | flops 8000000000 | bytes 10000000 | tf_op jit(solution)/shard_map/last/pallas_call | solution.py:330
  52.8 0.0 all-to-all-done.parts_ref
  52.8 0.0 copy-done.1
  52.8 0.6 %gates.1 = f32[8,32]{1,0:T(8,128)} custom-call(s32[8,32]{1,0:T(8,128)S(1)} %bitcast.8, f32[16,2,32]{2,1,0:T(2,128)S(1)} %all-to-all-done.parts_ref), custom_call_target="tpu_custom_call" | custom-call | flops 1000000 | bytes 10000 | tf_op jit(solution)/shard_map/gates/pallas_call | solution.py:400
  (5 shorter events, 0.0 us)
Async XLA Ops:
  0.7 21.2 %slice-start = ((s8[7340032]{0:T(1024)(128)(4,1)}), s8[3145728]{0:T(1024)(128)(4,1)S(1)}, s32[]{:S(2)}) async-start(s8[7340032]{0:T(1024)(128)(4,1)} %bitcast.5), calls=%async_computation.1 | async-start | bytes 6291456
  2.6 10.8 %copy-start = (bf16[32,3712]{1,0:T(8,128)(2,1)S(1)}, bf16[32,3712]{1,0:T(8,128)(2,1)}, u32[]{:S(2)}) copy-start(bf16[32,3712]{1,0:T(8,128)(2,1)} %pack.1.refs_0_) | copy-start | bytes 712708
  2.6 19.4 %slice-start.1 = ((s8[7340032]{0:T(1024)(128)(4,1)}), s8[4194304]{0:T(1024)(128)(4,1)S(1)}, s32[]{:S(2)}) async-start(s8[7340032]{0:T(1024)(128)(4,1)} %bitcast.5), calls=%async_computation.2 | async-start | bytes 8388608
  2.6 9.0 %collective-permute-start.3 = (bf16[32,3712]{1,0:T(8,128)(2,1)}, bf16[32,3712]{1,0:T(8,128)(2,1)S(1)}, u32[]{:S(2)}, u32[]{:S(2)}) collective-permute-start(bf16[32,3712]{1,0:T(8,128)(2,1)} %pack.1.refs_0_), channel_id=1, source_target_pairs={{0,1},{4,5},{1,2},{5,6},{2,3},{6,7},{3,11},{7,15},{11,10},{15,14},... | collective-permute-start | bytes 712712 | tf_op jit(solution)/shard_map/ppermute | solution.py:498
  5.7 8.2 %collective-permute-start = (bf16[32,3712]{1,0:T(8,128)(2,1)}, bf16[32,3712]{1,0:T(8,128)(2,1)S(1)}, u32[]{:S(2)}, u32[]{:S(2)}) collective-permute-start(bf16[32,3712]{1,0:T(8,128)(2,1)} %pack.1.refs_0_), channel_id=1, source_target_pairs={{0,8},{4,12},{1,0},{5,4},{2,1},{6,5},{3,2},{7,6},{11,3},{15,7},{10... | collective-permute-start | bytes 712712 | tf_op jit(solution)/shard_map/ppermute | solution.py:498
  5.7 1.2 %copy-start.3 = (bf16[2,496,512]{2,1,0:T(8,128)(2,1)S(1)}, bf16[2,496,512]{2,1,0:T(8,128)(2,1)}, u32[]{:S(2)}) copy-start(bf16[2,496,512]{2,1,0:T(8,128)(2,1)} %hidden_ref.1) | copy-start | bytes 3047428
  6.9 0.9 %copy-start.4 = (bf16[128,512]{1,0:T(8,128)(2,1)S(1)}, bf16[128,512]{1,0:T(8,128)(2,1)}, u32[]{:S(2)}) copy-start(bf16[128,512]{1,0:T(8,128)(2,1)} %shared_ref.1) | copy-start | bytes 393220
  7.8 0.7 %copy-start.5 = (s32[16]{0:T(128)S(1)}, s32[16]{0:T(128)}, u32[]{:S(2)}) copy-start(s32[16]{0:T(128)} %lens_ref.1) | copy-start | bytes 196
  11.6 17.9 %copy-start.2 = (bf16[512,3584]{1,0:T(8,128)(2,1)S(1)}, bf16[512,3584]{1,0:T(8,128)(2,1)}, u32[]{:S(2)}) copy-start(bf16[512,3584]{1,0:T(8,128)(2,1)} %refs_8_.1) | copy-start | bytes 11010052
  11.6 7.0 %collective-permute-start.4 = (bf16[32,3712]{1,0:T(8,128)(2,1)S(1)}, bf16[32,3712]{1,0:T(8,128)(2,1)S(1)}, u32[]{:S(2)}, u32[]{:S(2)}) collective-permute-start(bf16[32,3712]{1,0:T(8,128)(2,1)S(1)} %collective-permute-done.3.refs_2_.refs_1_), channel_id=1, source_target_pairs={{0,1},{4,5},{1,2},{5,6},{2,3},{6,7},{3,11},{7,15},{11,10},{15,14},... | collective-permute-start | bytes 712712 | tf_op jit(solution)/shard_map/ppermute | solution.py:498
  13.4 1.3 %collective-permute-start.5 = (bf16[128,512]{1,0:T(8,128)(2,1)S(1)}, bf16[128,512]{1,0:T(8,128)(2,1)S(1)}, u32[]{:S(2)}, u32[]{:S(2)}) collective-permute-start(bf16[128,512]{1,0:T(8,128)(2,1)S(1)} %get-tuple-element.66.refs_6_), channel_id=1, source_target_pairs={{0,4},{4,0},{8,12},{12,8},{1,5},{5,1},{9,13},{13,9},{2,6},{6,2},{1... | collective-permute-start | bytes 393224 | tf_op jit(solution)/shard_map/ppermute | solution.py:501
  13.4 5.2 %collective-permute-start.7 = (bf16[32,3712]{1,0:T(8,128)(2,1)S(1)}, bf16[32,3712]{1,0:T(8,128)(2,1)S(1)}, u32[]{:S(2)}, u32[]{:S(2)}) collective-permute-start(bf16[32,3712]{1,0:T(8,128)(2,1)S(1)} %copy-done), channel_id=1, source_target_pairs={{0,4},{4,0},{8,12},{12,8},{1,5},{5,1},{9,13},{13,9},{2,6},{6,2},{1... | collective-permute-start | bytes 712712 | tf_op jit(solution)/shard_map/ppermute | solution.py:501
  13.9 7.7 %collective-permute-start.1 = (bf16[32,3712]{1,0:T(8,128)(2,1)S(1)}, bf16[32,3712]{1,0:T(8,128)(2,1)S(1)}, u32[]{:S(2)}, u32[]{:S(2)}) collective-permute-start(bf16[32,3712]{1,0:T(8,128)(2,1)S(1)} %collective-permute-done.refs_4_.refs_2_), channel_id=1, source_target_pairs={{0,8},{4,12},{1,0},{5,4},{2,1},{6,5},{3,2},{7,6},{11,3},{15,7},{10... | collective-permute-start | bytes 712712 | tf_op jit(solution)/shard_map/ppermute | solution.py:498
  14.1 7.8 %collective-permute-start.9 = (bf16[32,3712]{1,0:T(8,128)(2,1)S(1)}, bf16[32,3712]{1,0:T(8,128)(2,1)S(1)}, u32[]{:S(2)}, u32[]{:S(2)}) collective-permute-start(bf16[32,3712]{1,0:T(8,128)(2,1)S(1)} %collective-permute-done.refs_4_.refs_2_), channel_id=1, source_target_pairs={{0,4},{4,0},{8,12},{12,8},{1,5},{5,1},{9,13},{13,9},{2,6},{6,2},{1... | collective-permute-start | bytes 712712 | tf_op jit(solution)/shard_map/ppermute | solution.py:501
  14.7 7.2 %collective-permute-start.8 = (bf16[32,3712]{1,0:T(8,128)(2,1)S(1)}, bf16[32,3712]{1,0:T(8,128)(2,1)S(1)}, u32[]{:S(2)}, u32[]{:S(2)}) collective-permute-start(bf16[32,3712]{1,0:T(8,128)(2,1)S(1)} %collective-permute-done.3.refs_2_.refs_1_), channel_id=1, source_target_pairs={{0,4},{4,0},{8,12},{12,8},{1,5},{5,1},{9,13},{13,9},{2,6},{6,2},{1... | collective-permute-start | bytes 712712 | tf_op jit(solution)/shard_map/ppermute | solution.py:501
  18.6 3.4 %collective-permute-start.10 = (bf16[32,3712]{1,0:T(8,128)(2,1)S(1)}, bf16[32,3712]{1,0:T(8,128)(2,1)S(1)}, u32[]{:S(2)}, u32[]{:S(2)}) collective-permute-start(bf16[32,3712]{1,0:T(8,128)(2,1)S(1)} %collective-permute-done.4.refs_6_.refs_3_), channel_id=1, source_target_pairs={{0,4},{4,0},{8,12},{12,8},{1,5},{5,1},{9,13},{13,9},{2,6},{6,2},{1... | collective-permute-start | bytes 712712 | tf_op jit(solution)/shard_map/ppermute | solution.py:501
  18.6 8.2 %collective-permute-start.6 = (bf16[32,3712]{1,0:T(8,128)(2,1)S(1)}, bf16[32,3712]{1,0:T(8,128)(2,1)S(1)}, u32[]{:S(2)}, u32[]{:S(2)}) collective-permute-start(bf16[32,3712]{1,0:T(8,128)(2,1)S(1)} %collective-permute-done.4.refs_6_.refs_3_), channel_id=1, source_target_pairs={{0,1},{4,5},{1,2},{5,6},{2,3},{6,7},{3,11},{7,15},{11,10},{15,14},... | collective-permute-start | bytes 712712 | tf_op jit(solution)/shard_map/ppermute | solution.py:498
  21.6 6.9 %collective-permute-start.12 = (bf16[32,3712]{1,0:T(8,128)(2,1)S(1)}, bf16[32,3712]{1,0:T(8,128)(2,1)S(1)}, u32[]{:S(2)}, u32[]{:S(2)}) collective-permute-start(bf16[32,3712]{1,0:T(8,128)(2,1)S(1)} %collective-permute-done.1.refs_4_.refs_0_), channel_id=1, source_target_pairs={{0,8},{4,12},{1,0},{5,4},{2,1},{6,5},{3,2},{7,6},{11,3},{15,7},{10... | collective-permute-start | bytes 712712 | tf_op jit(solution)/shard_map/ppermute | solution.py:498
  21.9 12.0 %collective-permute-start.2 = (bf16[32,3712]{1,0:T(8,128)(2,1)S(1)}, bf16[32,3712]{1,0:T(8,128)(2,1)S(1)}, u32[]{:S(2)}, u32[]{:S(2)}) collective-permute-start(bf16[32,3712]{1,0:T(8,128)(2,1)S(1)} %collective-permute-done.1.refs_4_.refs_0_), channel_id=1, source_target_pairs={{0,4},{4,0},{8,12},{12,8},{1,5},{5,1},{9,13},{13,9},{2,6},{6,2},{1... | collective-permute-start | bytes 712712 | tf_op jit(solution)/shard_map/ppermute | solution.py:501
  26.8 6.5 %collective-permute-start.14 = (bf16[32,2176]{1,0:T(8,128)(2,1)S(1)}, bf16[32,2176]{1,0:T(8,128)(2,1)S(1)}, u32[]{:S(2)}, u32[]{:S(2)}) collective-permute-start(bf16[32,2176]{1,0:T(8,128)(2,1)S(1)} %slice.6), channel_id=1, source_target_pairs={{0,1},{4,5},{1,2},{5,6},{2,3},{6,7},{3,11},{7,15},{11,10},{15,14},... | collective-permute-start | bytes 417800 | tf_op jit(solution)/shard_map/ppermute | solution.py:498
  28.6 4.7 %collective-permute-start.15 = (bf16[32,1536]{1,0:T(8,128)(2,1)S(1)}, bf16[32,1536]{1,0:T(8,128)(2,1)S(1)}, u32[]{:S(2)}, u32[]{:S(2)}) collective-permute-start(bf16[32,1536]{1,0:T(8,128)(2,1)S(1)} %slice.8), channel_id=1, source_target_pairs={{0,8},{4,12},{1,0},{5,4},{2,1},{6,5},{3,2},{7,6},{11,3},{15,7},{10... | collective-permute-start | bytes 294920 | tf_op jit(solution)/shard_map/ppermute | solution.py:498
  29.0 4.9 %collective-permute-start.11 = (bf16[32,3712]{1,0:T(8,128)(2,1)S(1)}, bf16[32,3712]{1,0:T(8,128)(2,1)S(1)}, u32[]{:S(2)}, u32[]{:S(2)}) collective-permute-start(bf16[32,3712]{1,0:T(8,128)(2,1)S(1)} %collective-permute-done.6.refs_5_.refs_2_), channel_id=1, source_target_pairs={{0,4},{4,0},{8,12},{12,8},{1,5},{5,1},{9,13},{13,9},{2,6},{6,2},{1... | collective-permute-start | bytes 712712 | tf_op jit(solution)/shard_map/ppermute | solution.py:501
  29.0 4.9 %collective-permute-start.13 = (bf16[32,3712]{1,0:T(8,128)(2,1)S(1)}, bf16[32,3712]{1,0:T(8,128)(2,1)S(1)}, u32[]{:S(2)}, u32[]{:S(2)}) collective-permute-start(bf16[32,3712]{1,0:T(8,128)(2,1)S(1)} %collective-permute-done.12.refs_6_.refs_4_), channel_id=1, source_target_pairs={{0,4},{4,0},{8,12},{12,8},{1,5},{5,1},{9,13},{13,9},{2,6},{6,2},{1... | collective-permute-start | bytes 712712 | tf_op jit(solution)/shard_map/ppermute | solution.py:501
  33.3 1.6 %collective-permute-start.16 = (bf16[32,3712]{1,0:T(8,128)(2,1)S(1)}, bf16[32,3712]{1,0:T(8,128)(2,1)S(1)}, u32[]{:S(2)}, u32[]{:S(2)}) collective-permute-start(bf16[32,3712]{1,0:T(8,128)(2,1)S(1)} %constant_dynamic-update-slice_fusion.refs_6_), channel_id=1, source_target_pairs={{0,4},{4,0},{8,12},{12,8},{1,5},{5,1},{9,13},{13,9},{2,6},{6,2},{1... | collective-permute-start | bytes 712712 | tf_op jit(solution)/shard_map/ppermute | solution.py:501
  33.3 5.9 %collective-permute-start.17 = (bf16[128,512]{1,0:T(8,128)(2,1)S(1)}, bf16[128,512]{1,0:T(8,128)(2,1)S(1)}, u32[]{:S(2)}, u32[]{:S(2)}) collective-permute-start(bf16[128,512]{1,0:T(8,128)(2,1)S(1)} %get-tuple-element.66.refs_6_), channel_id=1, source_target_pairs={{0,8},{4,12},{8,0},{12,4},{1,9},{5,13},{9,1},{13,5},{2,10},{6,14},... | collective-permute-start | bytes 393224 | tf_op jit(solution)/shard_map/ppermute | solution.py:530
  39.3 5.2 %collective-permute-start.18 = (bf16[128,512]{1,0:T(8,128)(2,1)S(1)}, bf16[128,512]{1,0:T(8,128)(2,1)S(1)}, u32[]{:S(2)}, u32[]{:S(2)}) collective-permute-start(bf16[128,512]{1,0:T(8,128)(2,1)S(1)} %collective-permute-done.17.refs_8_), channel_id=1, source_target_pairs={{0,4},{4,0},{8,12},{12,8},{1,5},{5,1},{9,13},{13,9},{2,6},{6,2},{1... | collective-permute-start | bytes 393224 | tf_op jit(solution)/shard_map/ppermute | solution.py:501
  39.4 13.4 %all-to-all-start = ((f32[16,2,32]{2,1,0:T(2,128)}), f32[16,2,32]{2,1,0:T(2,128)S(1)}, u32[]{:S(2)}, u32[]{:S(2)}) async-start(f32[16,2,32]{2,1,0:T(2,128)} %get-tuple-element.72), calls=%async_computation | async-start | bytes 32768 | tf_op jit(solution)/shard_map/all_to_all | solution.py:412
  44.5 8.3 %copy-start.1 = (s32[32,8]{0,1:T(8,128)S(1)}, s32[32,8]{0,1:T(8,128)}, u32[]{:S(2)}) copy-start(s32[32,8]{0,1:T(8,128)} %param.11) | copy-start | bytes 3076
